TPU v7x, 256 devices: a whole 4x4x8 slice. The times are simulated.
256 devices in a mesh: dp: 8 (over y, core), ctx: 32 (over z, x).
Axes of the slice: x: 4, y: 4, z: 8, core: 2. Of those that a mesh axis runs over, the one named last changes fastest.
Arguments:
- kv_latent: bfloat16 [8, 4096, 576], P('dp', 'ctx'), may hold values from -6.1 to 6.1
- q_nope: bfloat16 [8, 4096, 512], P('dp', 'ctx'), may hold values from -6 to 6
- q_rope: bfloat16 [8, 4096, 256], P('dp', 'ctx'), may hold values from -430 to 430
- w_key_up: bfloat16 [512, 512], replicated, may hold values from -0.25 to 0.25
- w_value_up: bfloat16 [512, 512], replicated, may hold values from -0.25 to 0.25
- out_grad: bfloat16 [8, 4096, 512], P('dp', 'ctx'), may hold values from -6 to 6
- segment_ids: int32 [8, 4096], P('dp', 'ctx'), may hold values from 0 to 9, never falling along the last dimension, each value on 1 to 1536 neighbouring positions
Outputs:
- grad_q_nope: bfloat16 [8, 4096, 512], P('dp', 'ctx')
- grad_q_rope: bfloat16 [8, 4096, 256], P('dp', 'ctx')
- grad_latent: bfloat16 [8, 4096, 576], P('dp', 'ctx')
- grad_w_key_up: float32 [512, 512], P('ctx')
- grad_w_value_up: float32 [512, 512], P('ctx')
Inputs may be any that keep to these rules, and one draw needn't show every extreme that they name: `segment_ids`: ids never fall along a sequence; each document holds at most 1536 positions and some document holds exactly 1536.
All inputs are finite; a program needn't handle non-finite values.
Results may differ from a plain program's by a relative error of at most 0.039.
Values may be sent and summed in bfloat16 or wider, within the bound.
No kernel may reach another device: no remote copies, remote signals or barrier semaphores. Data moves between devices by JAX's collectives and lax.ppermute only.
A program may use at most 128 MiB of HBM per device.

v0:
```python
import jax
import jax.numpy as jnp
from jax import lax
from jax.sharding import PartitionSpec as P


def product(pattern, left_operand, right_operand):
    return jnp.einsum(pattern, left_operand, right_operand, preferred_element_type=jnp.float32)


def block_grads(
    window,
    window_marks,
    key_pos,
    query_nope,
    query_rope,
    out_grads,
    query_marks,
    query_pos,
    key_up,
    value_up,
):
    latent_width = key_up.shape[0]
    latents = window[:, :latent_width]
    rope_keys = window[:, latent_width:]
    score_scale = (query_nope.shape[2] + query_rope.shape[2]) ** (-0.5)
    key_rows = product("kl,lhd->khd", latents, key_up).astype(jnp.bfloat16)
    query_latent = product("thd,lhd->thl", query_nope, key_up).astype(jnp.bfloat16)
    out_latent = product("thd,lhd->thl", out_grads, value_up).astype(jnp.bfloat16)
    scores = (
        product("thd,khd->htk", query_nope, key_rows)
        + product("thr,kr->htk", query_rope, rope_keys)
    ) * score_scale
    allowed = (key_pos[None, :] <= query_pos[:, None]) & (
        window_marks[None, :] == query_marks[:, None]
    )
    scores = jnp.where(allowed[None], scores, -jnp.inf)
    row_max = jnp.max(scores, axis=-1, keepdims=True)
    weights = jnp.exp(scores - row_max)
    attention = weights / jnp.sum(weights, axis=-1, keepdims=True)
    attention_low = attention.astype(jnp.bfloat16)
    dprob = product("thl,kl->htk", out_latent, latents)
    row_delta = jnp.sum(attention * dprob, axis=-1, keepdims=True)
    score_grad = (attention * (dprob - row_delta) * score_scale).astype(jnp.bfloat16)
    grad_nope = product("htk,khd->thd", score_grad, key_rows)
    grad_rope = product("htk,kr->thr", score_grad, rope_keys)
    latent_part = product("htk,thl->kl", score_grad, query_latent) + product(
        "htk,thl->kl", attention_low, out_latent
    )
    rope_part = product("htk,thr->kr", score_grad, query_rope)
    latent_mix = product("htk,kl->thl", score_grad, latents).astype(jnp.bfloat16)
    value_mix = product("htk,kl->thl", attention_low, latents).astype(jnp.bfloat16)
    grad_key_up = product("thd,thl->hdl", query_nope, latent_mix)
    grad_value_up = product("thd,thl->hdl", out_grads, value_mix)
    return (
        grad_nope,
        grad_rope,
        jnp.concatenate([latent_part, rope_part], axis=1),
        grad_key_up,
        grad_value_up,
    )


def body(kv_latent, q_nope, q_rope, w_key_up, w_value_up, out_grad, segment_ids):
    latent_rows = kv_latent[0]
    tok_rows, full_width = latent_rows.shape
    latent_width, head_cols = w_key_up.shape
    rope_width = full_width - latent_width
    head_count = q_rope.shape[2] // rope_width
    head_width = head_cols // head_count
    ctx_count = lax.axis_size("ctx")
    ctx_index = lax.axis_index("ctx")
    doc_limit = min(1536, tok_rows * ctx_count * 3 // 4)
    reach_back = min((doc_limit + tok_rows - 2) // tok_rows, ctx_count - 1)
    start_row = ctx_index * tok_rows
    span_rows = (reach_back + 1) * tok_rows
    doc_marks = segment_ids[0] + 1
    all_rows, all_marks = (
        lax.all_gather(latent_rows, "ctx", axis=0, tiled=True),
        lax.all_gather(doc_marks, "ctx", axis=0, tiled=True),
    )
    padded = jnp.concatenate(
        [jnp.zeros((reach_back * tok_rows, full_width), jnp.bfloat16), all_rows], axis=0
    )
    padded_marks = jnp.concatenate([jnp.zeros((reach_back * tok_rows,), jnp.int32), all_marks])
    window = lax.dynamic_slice_in_dim(padded, start_row, span_rows, 0)
    window_marks = lax.dynamic_slice_in_dim(padded_marks, start_row, span_rows, 0)
    key_pos = start_row - reach_back * tok_rows + jnp.arange(span_rows, dtype=jnp.int32)
    query_pos = start_row + jnp.arange(tok_rows, dtype=jnp.int32)
    key_up = w_key_up.reshape(latent_width, head_count, head_width)
    value_up = w_value_up.reshape(latent_width, head_count, head_width)
    grad_nope, grad_rope, window_grad, grad_key, grad_value = block_grads(
        window,
        window_marks,
        key_pos,
        q_nope[0].reshape(tok_rows, head_count, head_width),
        q_rope[0].reshape(tok_rows, head_count, rope_width),
        out_grad[0].reshape(tok_rows, head_count, head_width),
        doc_marks,
        query_pos,
        key_up,
        value_up,
    )
    total_grad = jnp.zeros((reach_back * tok_rows + ctx_count * tok_rows, full_width), jnp.float32)
    total_grad = lax.dynamic_update_slice_in_dim(total_grad, window_grad, start_row, 0)
    own_grads = lax.psum_scatter(
        total_grad[reach_back * tok_rows :].astype(jnp.bfloat16),
        "ctx",
        scatter_dimension=0,
        tiled=True,
    )
    grad_key = grad_key.reshape(head_cols, latent_width)
    grad_value = grad_value.reshape(head_cols, latent_width)
    key_share, value_share = (
        lax.psum_scatter(
            grad_key.astype(jnp.bfloat16), "ctx", scatter_dimension=0, tiled=True
        ).astype(jnp.float32),
        lax.psum_scatter(
            grad_value.astype(jnp.bfloat16), "ctx", scatter_dimension=0, tiled=True
        ).astype(jnp.float32),
    )
    key_share, value_share = (
        lax.psum(key_share.astype(jnp.bfloat16), "dp").astype(jnp.float32),
        lax.psum(value_share.astype(jnp.bfloat16), "dp").astype(jnp.float32),
    )
    return (
        grad_nope.astype(jnp.bfloat16).reshape(1, tok_rows, head_cols),
        grad_rope.astype(jnp.bfloat16).reshape(1, tok_rows, head_count * rope_width),
        own_grads[None],
        key_share,
        value_share,
    )


def solution(mesh):
    return jax.shard_map(
        body,
        mesh=mesh,
        in_specs=(
            P("dp", "ctx", None),
            P("dp", "ctx", None),
            P("dp", "ctx", None),
            P(),
            P(),
            P("dp", "ctx", None),
            P("dp", "ctx"),
        ),
        out_specs=(
            P("dp", "ctx", None),
            P("dp", "ctx", None),
            P("dp", "ctx", None),
            P("ctx", None),
            P("ctx", None),
        ),
        check_vma=False,
    )
```

profile of v0, /device:TPU:1, one launch (start us, length us, event | category | flops | bytes accessed | tf_op | source)
XLA Modules:
  0.0 770.5 jit_solution(4019659197633294311)
XLA Ops:
  7.2 0.0 copy-start
  7.2 0.0 all-gather.4.cloned.1.call-start
  7.2 1.7 copy.51
  9.0 0.0 all-gather.4.cloned.1.call-update
  9.0 0.0 reduce-scatter.8.cloned.1.call-start
  9.1 1.0 copy.54
  10.0 0.0 copy-start.4
  10.0 1.0 copy.95
  11.1 1.0 copy.96
  12.1 0.7 broadcast_add_fusion
  12.8 35.9 %all-gather.1 = s32[1,4096]{1,0:T(1,128)S(1)} all-gather(s32[1,128]{1,0:T(1,128)S(1)} %get-tuple-element.22), channel_id=3, replica_groups=mesh['dp'=8,'ctx'=32] {'ctx'}, dimensions={1}, use_global_device_ids=true | all-gather | bytes 16896 | tf_op jit(solution)/shard_map/all_gather | solution.py:80
  48.7 0.1 pad_dynamic-slice_fusion.2
  48.8 1.0 compare_and_fusion
  49.8 47.3 %all-gather.4.cloned.1.call-done = bf16[1,4096,576]{2,1,0:T(8,128)(2,1)} async-done(((bf16[1,128,576]{2,1,0:T(8,128)(2,1)}), bf16[1,4096,576]{2,1,0:T(8,128)(2,1)}) %all-gather.4.cloned.1.call-update) | async-done | bytes 4718608 | tf_op jit(solution)/shard_map/all_gather | solution.py:79
  97.1 2.1 convolution_convert_fusion
  99.2 0.6 fusion.61
  99.9 1.0 fusion.7
  100.8 2.8 fusion.60
  103.6 5.6 convolution_convert_fusion.1
  109.2 0.0 reduce-scatter.8.cloned.1.call-update
  109.2 0.0 reduce-scatter.6.cloned.1.call-start
  109.3 0.3 fusion.16
  109.6 3.7 fusion.31
  113.3 6.7 fusion.15
  120.0 1.1 convolution_convert_fusion.2
  121.1 0.0 reduce-scatter.6.cloned.1.call-update
  121.1 0.2 reduce-scatter.10.cloned.1.call-start
  121.4 0.0 copy-done.5
  121.4 6.1 convolution_bitcast_fusion
  127.5 8.5 %fusion.12 = f32[1664,512,1]{0,1,2:T(8,128)} fusion(f32[1664,128,4]{1,0,2:T(8,128)} %fusion.31, bf16[128,4,128]{0,2,1:T(8,128)(2,1)S(1)} %bitcast.147, f32[4,128,1664]{1,2,0:T(8,128)} %get-tuple-element.25, f32[4,128]{1,0:T(4,128)S(1)} %get-tuple-element.24, bf16[512,512]{1,0:T(8,128)(2,1)S(1)} %copy-done), kind=kOutput, calls=%fused_computation.23 | convolution fusion | flops 945752192 | bytes 10881024 | tf_op jit(solution)/shard_map/htk,thl->kl/dot_general | solution.py:8
  135.9 6.8 bitcast_add_fusion
  142.7 0.4 broadcast_in_dim.18
  143.1 1.0 copy-done.2
  144.1 0.3 maximum_dynamic-update-slice_fusion
  144.4 2.8 slice.15
  147.2 7.7 copy.93
  154.9 0.0 reduce-scatter.10.cloned.1.call-update
  154.9 6.7 fusion.18
  161.6 0.8 copy.74
  162.3 6.2 fusion.19
  168.6 0.7 copy.75
  169.3 148.4 %reduce-scatter.8.cloned.1.call-done = bf16[16,512]{1,0:T(8,128)(2,1)} async-done(((bf16[512,512]{1,0:T(8,128)(2,1)}), bf16[16,512]{1,0:T(8,128)(2,1)}) %reduce-scatter.8.cloned.1.call-update) | async-done | bytes 16400 | tf_op jit(solution)/shard_map/reduce_scatter | solution.py:118
  317.7 215.9 %reduce-scatter.6.cloned.1.call-done = bf16[16,512]{1,0:T(8,128)(2,1)} async-done(((bf16[512,512]{1,0:T(8,128)(2,1)}), bf16[16,512]{1,0:T(8,128)(2,1)}) %reduce-scatter.6.cloned.1.call-update) | async-done | bytes 16400 | tf_op jit(solution)/shard_map/reduce_scatter | solution.py:115
  533.6 26.7 %all-reduce.2 = (bf16[16,512]{1,0:T(8,128)(2,1)S(1)}, bf16[16,512]{1,0:T(8,128)(2,1)S(1)}) all-reduce(bf16[16,512]{1,0:T(8,128)(2,1)} %reduce-scatter.6.cloned.1.call-done, bf16[16,512]{1,0:T(8,128)(2,1)} %reduce-scatter.8.cloned.1.call-done), channel_id=1, replica_groups=mesh['dp'=8,'ctx'=32] {'dp'}, use_global_device_ids=true, to_apply=%region_5.6 | all-reduce | flops 16384 | bytes 65536 | tf_op jit(solution)/shard_map/psum | solution.py:123
  560.3 0.6 convert_element_type.85
  560.9 0.6 convert_element_type.90
  561.6 200.7 %reduce-scatter.10.cloned.1.call-done = bf16[128,576]{1,0:T(8,128)(2,1)} async-done(((bf16[4096,576]{1,0:T(8,128)(2,1)}), bf16[128,576]{1,0:T(8,128)(2,1)}) %reduce-scatter.10.cloned.1.call-update) | async-done | bytes 147472
  762.3 1.7 copy.94
  (15 shorter events, 0.0 us)
Async XLA Ops:
  7.2 90.0 %copy-start = (bf16[512,512]{1,0:T(8,128)(2,1)S(1)}, bf16[512,512]{1,0:T(8,128)(2,1)}, u32[]{:S(2)}) copy-start(bf16[512,512]{1,0:T(8,128)(2,1)} %param.10) | copy-start | bytes 1572868
  7.2 89.9 %all-gather.4.cloned.1.call-start = ((), (), s32[]{:S(2)}) async-start(), calls=%async_computation.5 | async-start | bytes 5406720 | tf_op jit(solution)/shard_map/all_gather | solution.py:79
  9.0 308.7 %reduce-scatter.8.cloned.1.call-start = ((), (), s32[]{:S(2)}) async-start(), calls=%async_computation.4 | async-start | bytes 540672 | tf_op jit(solution)/shard_map/reduce_scatter | solution.py:118
  10.0 89.8 %copy-start.4 = (bf16[1,128,256]{1,2,0:T(8,128)(2,1)}, bf16[1,128,256]{1,2,0:T(8,128)(2,1)S(1)}, u32[]{:S(2)}) copy-start(bf16[1,128,256]{1,2,0:T(8,128)(2,1)S(1)} %copy.54) | copy-start | bytes 196612
  97.1 2.7 slice-start
  97.1 2.7 slice-start.1
  100.8 2.8 copy-start.1
  103.6 5.7 copy-start.3
  109.2 424.4 %reduce-scatter.6.cloned.1.call-start = ((), (), s32[]{:S(2)}) async-start(), calls=%async_computation.3 | async-start | bytes 540672 | tf_op jit(solution)/shard_map/reduce_scatter | solution.py:115
  113.3 8.1 %copy-start.5 = (bf16[1,128,256]{1,2,0:T(8,128)(2,1)S(1)}, bf16[1,128,256]{1,2,0:T(8,128)(2,1)}, u32[]{:S(2)}) copy-start(bf16[1,128,256]{1,2,0:T(8,128)(2,1)} %copy-done.4) | copy-start | bytes 196612
  121.1 641.1 %reduce-scatter.10.cloned.1.call-start = ((), (), s32[]{:S(2)}) async-start(), calls=%async_computation.6 | async-start | bytes 5406720
  142.7 1.5 copy-start.2
Sparse Core Ops, SparseCore 0:
  10.6 86.4 all-gather.3
  109.3 208.3 reduce-scatter.7
  322.0 211.5 reduce-scatter.5
  537.4 224.8 reduce-scatter.9
where the time goes:
time: 775 us; the launch traced here: 771 us
  waiting for transfers between devices  612 us (79%)
  blocking collectives  62.6 us (8%)
  matrix products  55.3 us (7%)
  local copies, waits for them, and re-layouts  20 us (3%)
  between operations  13.9 us (2%)
    reduce_scatter x1, waiting for transfers between devices, body(): lax.psum_scatter(grad_key.astype(jnp.bfloat16), 'ctx', scatter_dimension=...  216 us
    unnamed x5, waiting for transfers between devices  201 us
    reduce_scatter x1, waiting for transfers between devices, body(): lax.psum_scatter(grad_value.astype(jnp.bfloat16), 'ctx', scatter_dimensio...  148 us
    dot_general x13, matrix products, product(): jnp.einsum(pattern, left_operand, right_operand, preferred_element_type=j...  55.3 us
    all_gather x1, waiting for transfers between devices, body(): lax.all_gather(latent_rows, 'ctx', axis=0, tiled=True)  47.3 us
    all_gather x1, blocking collectives, body(): lax.all_gather(doc_marks, 'ctx', axis=0, tiled=True)  35.9 us
    psum x1, blocking collectives, body(): lax.psum(key_share.astype(jnp.bfloat16), 'dp').astype(jnp.float32)  26.7 us
  transfers between devices with their start and end apart: 4, of which 4 were waited for; matrix products, arithmetic and copies ran while one was open for 8% of the time, Pallas kernels for 0%

commit v1 on v0

v1 whole, which is shorter than its diff:
```python
import functools

import jax
import jax.numpy as jnp
from jax import lax
from jax.experimental import pallas as pl
from jax.experimental.pallas import tpu as pltpu
from jax.sharding import PartitionSpec as P

Z, X, Y = 8, 4, 4
HEADS, HEAD, ROPE, LATENT = 4, 128, 64, 512
ROWS = 128
REACH = 4
QROWS = X * ROWS
KROWS = REACH * ROWS
SCALE = (HEAD + ROPE) ** -0.5
NEG = -1e30
BF, F32 = jnp.bfloat16, jnp.float32
NT = (((1,), (1,)), ((), ()))
TN = (((0,), (0,)), ((), ()))
VMEM = pl.BlockSpec(memory_space=pltpu.VMEM)
SMEM = pl.BlockSpec(memory_space=pltpu.SMEM)


def x_shift(v, s):
    return lax.ppermute(v, "ctx", [(i, i // X * X + (i % X + s) % X) for i in range(Z * X)])


def z_shift(v, s):
    return lax.ppermute(v, "ctx", [(i, (i + s * X) % (Z * X)) for i in range(Z * X)])


def y_shift(v, s):
    return lax.ppermute(v, "dp", [(i, (i + 2 * s) % (2 * Y)) for i in range(2 * Y)])


def core_swap(v):
    return lax.ppermute(v, "dp", [(i, i ^ 1) for i in range(2 * Y)])


def call(kernel, out_shape, n_smem, n_vmem, scratch=(), flops=0, nbytes=0):
    return pl.pallas_call(
        kernel,
        out_shape=out_shape,
        in_specs=[SMEM] * n_smem + [VMEM] * n_vmem,
        out_specs=jax.tree.map(lambda _: VMEM, out_shape),
        scratch_shapes=list(scratch),
        compiler_params=pltpu.CompilerParams(vmem_limit_bytes=48 * 1024 * 1024),
        cost_estimate=pl.CostEstimate(flops=flops, bytes_accessed=nbytes, transcendentals=0),
    )


def pack_kernel(nope, rope, grad, kv, ids, q_out, c_out):
    for h in range(HEADS):
        q_out[h * 128:(h + 1) * 128, :] = nope[:, h * 128:(h + 1) * 128]
        q_out[512 + h * 128:512 + (h + 1) * 128, :] = grad[:, h * 128:(h + 1) * 128]
    for p in range(2):
        q_out[1024 + p * 128:1024 + (p + 1) * 128, :] = rope[:, p * 128:(p + 1) * 128]
    marks = jnp.broadcast_to(ids[...].astype(F32), (128, 128))
    q_out[1280:1296, :] = marks[:16].astype(BF)
    c_out[:, :512] = kv[:, :512]
    c_out[:, 512:640] = jnp.concatenate([kv[:, 512:576], marks.T[:, :64].astype(BF)], axis=1)


def pack(nope, rope, grad, kv, ids):
    return call(
        pack_kernel,
        (jax.ShapeDtypeStruct((1296, 128), BF), jax.ShapeDtypeStruct((128, 640), BF)),
        0, 5, nbytes=1 << 20,
    )(nope, rope, grad, kv, ids)


def stats_kernel(where, q0, q1, q2, q3, c0, c1, c2, c3, wk, wv, qc, gs, kc, vs, bias, stats, qid):
    xi, zi = where[0], where[1]
    for s, ref in enumerate((q0, q1, q2, q3)):
        at = pl.ds(pl.multiple_of(((xi + s) & 3) * 128, 128), 128)
        for h in range(HEADS):
            qc[h, at, 0:128] = ref[h * 128:(h + 1) * 128, :]
            qc[h, at, 128:256] = ref[1024 + h // 2 * 128:1152 + h // 2 * 128, :]
            gs[h, at, :] = ref[512 + h * 128:640 + h * 128, :]
        qid[:, at] = ref[1280:1296, :]
    latents = jnp.concatenate([c[:, :512] for c in (c0, c1, c2, c3)], axis=0)
    keys = jnp.dot(latents, wk[...], preferred_element_type=F32).astype(BF)
    values = jnp.dot(latents, wv[...], preferred_element_type=F32).astype(BF)
    lane = lax.broadcasted_iota(jnp.int32, (128, 128), 1)
    for h in range(HEADS):
        kc[h, :, 0:128] = keys[:, h * 128:(h + 1) * 128]
        vs[h, :, :] = values[:, h * 128:(h + 1) * 128]
    q_marks = qid[0:1, :].astype(F32)
    q_pos = zi * QROWS + lax.broadcasted_iota(jnp.int32, (128, QROWS), 1)
    for j, c in enumerate((c0, c1, c2, c3)):
        tail = c[:, 512:640].astype(F32)
        even = jnp.where(lane < 64, tail, 0.0)
        odd = pltpu.roll(even, 64, 1)
        for h in range(HEADS):
            kc[h, j * 128:(j + 1) * 128, 128:256] = (odd if h % 2 else even).astype(BF)
        first = ((zi - j) & (Z - 1)) * QROWS + xi * 128
        k_pos = first + lax.broadcasted_iota(jnp.int32, (128, QROWS), 0)
        allowed = (k_pos <= q_pos) & (tail[:, 64:65] == q_marks)
        bias[j * 128:(j + 1) * 128, :] = jnp.where(allowed, 0.0, NEG)
    for h in range(HEADS):
        for b in range(0, QROWS, 256):
            sl = slice(b, b + 256)
            s = lax.dot_general(kc[h], qc[h, sl, :], NT, preferred_element_type=F32) * SCALE + bias[:, sl]
            dp = lax.dot_general(vs[h], gs[h, sl, :], NT, preferred_element_type=F32)
            m = jnp.max(s, axis=0, keepdims=True)
            e = jnp.exp(s - m)
            stats[h:h + 1, sl] = m
            stats[4 + h:5 + h, sl] = jnp.sum(e, axis=0, keepdims=True)
            stats[8 + h:9 + h, sl] = jnp.sum(e * dp, axis=0, keepdims=True)
    stats[12:16, :] = jnp.zeros((4, QROWS), F32)


def run_stats(where, qs, cs, wk, wv):
    sds = jax.ShapeDtypeStruct
    return call(
        stats_kernel,
        (sds((4, QROWS, 256), BF), sds((4, QROWS, 128), BF), sds((4, KROWS, 256), BF), sds((4, KROWS, 128), BF),
         sds((KROWS, QROWS), F32), sds((16, QROWS), F32)),
        1, 10, scratch=[pltpu.VMEM((16, QROWS), BF)], flops=1_400_000_000, nbytes=8 << 20,
    )(where, *qs, *cs, wk, wv)


def grads_kernel(where, t0, t1, t2, t3, qc, gs, kc, vs, bias, c0, c1, c2, c3, wk, wv,
                 w_keep, w_send, d0, d1, d2, d3, o0, o1, o2, o3, p_scr, s_scr, dkv, dq):
    xi, core = where[0], where[2]
    tops = [t[0:4, :] for t in (t0, t1, t2, t3)]
    top = functools.reduce(jnp.maximum, tops)
    total = jnp.zeros((4, QROWS), F32)
    cross = jnp.zeros((4, QROWS), F32)
    for t, m in zip((t0, t1, t2, t3), tops):
        f = jnp.exp(m - top)
        total = total + f * t[4:8, :]
        cross = cross + f * t[8:12, :]
    inv = 1.0 / total
    delta = cross * inv
    rope_grad = [jnp.zeros((KROWS, 128), F32), jnp.zeros((KROWS, 128), F32)]
    pair = None
    for h in range(HEADS):
        for b in range(0, QROWS, 256):
            sl = slice(b, b + 256)
            s = lax.dot_general(kc[h], qc[h, sl, :], NT, preferred_element_type=F32) * SCALE + bias[:, sl]
            dp = lax.dot_general(vs[h], gs[h, sl, :], NT, preferred_element_type=F32)
            p = jnp.exp(s - top[h:h + 1, sl]) * inv[h:h + 1, sl]
            p_scr[h % 2, :, sl] = p.astype(BF)
            s_scr[h % 2, :, sl] = (p * (dp - delta[h:h + 1, sl]) * SCALE).astype(BF)
        cols = slice(h * 128, (h + 1) * 128)
        dkv[1, :, cols] = jnp.dot(p_scr[h % 2], gs[h], preferred_element_type=F32).astype(BF)
        dk = jnp.dot(s_scr[h % 2], qc[h], preferred_element_type=F32)
        dkv[0, :, cols] = dk[:, :128].astype(BF)
        rope_grad[h % 2] = rope_grad[h % 2] + dk[:, 128:]
        dqh = lax.dot_general(s_scr[h % 2], kc[h], TN, preferred_element_type=F32)
        dq[:, cols] = dqh[:, :128].astype(BF)
        if h % 2 == 0:
            pair = dqh[:, 128:]
        else:
            dq[:, 512 + h // 2 * 128:640 + h // 2 * 128] = (pair + dqh[:, 128:]).astype(BF)
    latents = jnp.concatenate([c[:, :512] for c in (c0, c1, c2, c3)], axis=0)
    for out, which in ((w_send, 1 - core), (w_keep, core)):
        w = lax.dot_general(dkv[which], latents, TN, preferred_element_type=F32).astype(BF)
        for r in range(32):
            out[r % 4, r // 4 * 16:r // 4 * 16 + 16, :] = w[r * 16:r * 16 + 16, :]
    lat = (lax.dot_general(dkv[0], wk[...], NT, preferred_element_type=F32)
           + lax.dot_general(dkv[1], wv[...], NT, preferred_element_type=F32)).astype(BF)
    lane = lax.broadcasted_iota(jnp.int32, (KROWS, 128), 1)
    tail = jnp.where(lane < 64, rope_grad[0] + pltpu.roll(rope_grad[1], 64, 1), 0.0).astype(BF)
    for j, d in enumerate((d0, d1, d2, d3)):
        d[:, :512] = lat[j * 128:(j + 1) * 128, :]
        d[:, 512:640] = tail[j * 128:(j + 1) * 128, :]
    for s, o in enumerate((o0, o1, o2, o3)):
        o[...] = dq[pl.ds(pl.multiple_of(((xi + s) & 3) * 128, 128), 128), :]


def run_grads(where, ts, mats, cs, wk, wv):
    sds = jax.ShapeDtypeStruct
    return call(
        grads_kernel,
        tuple([sds((4, 128, 512), BF)] * 2 + [sds((128, 640), BF)] * 4 + [sds((128, 768), BF)] * 4),
        1, 4 + 5 + 4 + 2,
        scratch=[pltpu.VMEM((2, KROWS, QROWS), BF), pltpu.VMEM((2, KROWS, QROWS), BF),
                 pltpu.VMEM((2, KROWS, 512), BF), pltpu.VMEM((QROWS, 768), BF)],
        flops=3_000_000_000, nbytes=10 << 20,
    )(where, *ts, *mats, *cs, wk, wv)


def spread_kernel(where, keep, recv, o0, o1, o2, o3):
    xi = where[0]
    for s, o in enumerate((o0, o1, o2, o3)):
        at = (xi + s) & 3
        o[...] = (keep[at].astype(F32) + recv[at].astype(F32)).astype(BF)


def spread(where, keep, recv):
    return call(spread_kernel, tuple([jax.ShapeDtypeStruct((128, 512), BF)] * 4), 1, 2, nbytes=2 << 20)(where, keep, recv)


def wide_sum(*parts):
    return functools.reduce(jnp.add, [p.astype(F32) for p in parts])


def body(kv_latent, q_nope, q_rope, w_key_up, w_value_up, out_grad, segment_ids):
    ctx = lax.axis_index("ctx")
    dp = lax.axis_index("dp")
    core = dp % 2
    where = jnp.stack([ctx % X, ctx // X, core]).astype(jnp.int32)
    q, c = pack(q_nope[0], q_rope[0], out_grad[0], kv_latent[0], segment_ids)
    qs = (q, x_shift(q, -1), x_shift(q, 2), x_shift(q, 1))
    c1 = z_shift(c, 1)
    c2 = z_shift(c1, 1)
    c3 = z_shift(c2, 1)
    cs = (c, c1, c2, c3)
    *mats, stats = run_stats(where, qs, cs, w_key_up, w_value_up)
    ts = (stats, x_shift(stats, 1), x_shift(stats, 2), x_shift(stats, -1))
    w_keep, w_send, d0, d1, d2, d3, o0, o1, o2, o3 = run_grads(where, ts, mats, cs, w_key_up, w_value_up)
    pieces = spread(where, w_keep, core_swap(w_send))
    w = wide_sum(pieces[0], x_shift(pieces[1], 1), x_shift(pieces[2], 2), x_shift(pieces[3], -1)).astype(BF)
    w = lax.all_to_all(w, "ctx", 0, 0, tiled=True, axis_index_groups=[[z * X + x for z in range(Z)] for x in range(X)])
    w = jnp.sum(w.reshape(Z, 16, 512).astype(F32), axis=0).astype(BF)
    w = wide_sum(w, y_shift(w, 1), y_shift(w, 2), y_shift(w, -1))
    other = core_swap(w)
    grad_key = jnp.where(core == 0, w, other)
    grad_value = jnp.where(core == 0, other, w)
    d = z_shift(d3, -1)
    d = z_shift(wide_sum(d, d2).astype(BF), -1)
    d = z_shift(wide_sum(d, d1).astype(BF), -1)
    grad_latent = wide_sum(d, d0).astype(BF)[:, :576]
    grad_q = wide_sum(o0, x_shift(o1, 1), x_shift(o2, 2), x_shift(o3, -1)).astype(BF)
    return grad_q[None, :, :512], grad_q[None, :, 512:], grad_latent[None], grad_key, grad_value


def solution(mesh):
    return jax.shard_map(
        body,
        mesh=mesh,
        in_specs=(
            P("dp", "ctx", None),
            P("dp", "ctx", None),
            P("dp", "ctx", None),
            P(),
            P(),
            P("dp", "ctx", None),
            P("dp", "ctx"),
        ),
        out_specs=(
            P("dp", "ctx", None),
            P("dp", "ctx", None),
            P("dp", "ctx", None),
            P("ctx", None),
            P("ctx", None),
        ),
        check_vma=False,
    )
```

time: 775 us -> 97.7 us (0.13)
  waiting for transfers between devices: 612 us -> 38.3 us
  blocking collectives: 62.6 us -> 0 us
  matrix products: 55.3 us -> 0 us
  starting transfers between devices: 0.34 us -> 36.8 us
  between operations: 13.9 us -> 0.77 us
  local copies, waits for them, and re-layouts: 20 us -> 7.66 us
  Pallas kernels: 0 us -> 12 us
    reduce_scatter x2 -> x0, waiting for transfers between devices: 364 us -> none  [the longest x1 216 us: body(): lax.psum_scatter(grad_key.astype(jnp.bfloat16), 'ctx', scatter_dimension=...]
    unnamed x5 -> x0, waiting for transfers between devices: 201 us -> none
    dot_general x13 -> x0, matrix products: 55.3 us -> none  [product(): jnp.einsum(pattern, left_operand, right_operand, preferred_element_type=j...]
    all_gather x1 -> x0, waiting for transfers between devices: 47.3 us -> none  [body(): lax.all_gather(latent_rows, 'ctx', axis=0, tiled=True)]
    all_gather x1 -> x0, blocking collectives: 35.9 us -> none  [body(): lax.all_gather(doc_marks, 'ctx', axis=0, tiled=True)]
    ppermute x0 -> x23, waiting for transfers between devices: none -> 31.7 us  [the longest x12 16.5 us: x_shift(): lax.ppermute(v, 'ctx', [(i, i // X * X + (i % X + s) % X) for i in range(...]
    ppermute x0 -> x23, starting transfers between devices: none -> 31.6 us  [the longest x12 11.2 us: x_shift(): lax.ppermute(v, 'ctx', [(i, i // X * X + (i % X + s) % X) for i in range(...]
    psum x1 -> x0, blocking collectives: 26.7 us -> none  [body(): lax.psum(key_share.astype(jnp.bfloat16), 'dp').astype(jnp.float32)]
  transfers between devices with their start and end apart: 4 -> 24, of which waited for: 4 -> 15; matrix products, arithmetic and copies ran while one was open for 8% -> 3% of each run, Pallas kernels for 0% -> 1%
where the time goes in v1:
time: 97.7 us; the launch traced here: 97.2 us
  waiting for transfers between devices  38.3 us (39%)
  starting transfers between devices  36.8 us (38%)
  Pallas kernels  12 us (12%)
  local copies, waits for them, and re-layouts  7.66 us (8%)
  other arithmetic  1.7 us (2%)
    ppermute x12, waiting for transfers between devices, x_shift(): lax.ppermute(v, 'ctx', [(i, i // X * X + (i % X + s) % X) for i in range(...  16.5 us
    ppermute x6, waiting for transfers between devices, z_shift(): lax.ppermute(v, 'ctx', [(i, (i + s * X) % (Z * X)) for i in range(Z * X)])  12.1 us
    ppermute x12, starting transfers between devices, x_shift(): lax.ppermute(v, 'ctx', [(i, i // X * X + (i % X + s) % X) for i in range(...  11.2 us
    ppermute x2, starting transfers between devices, core_swap(): return lax.ppermute(v, 'dp', [(i, i ^ 1) for i in range(2 * Y)])  10.3 us
    pallas_call x1, Pallas kernels, run_grads(): call(grads_kernel, tuple([sds((4, 128, 512), BF)] * 2 + [sds((128, 640),...  7.16 us
    all_to_all x1, waiting for transfers between devices, body(): lax.all_to_all(w, 'ctx', 0, 0, tiled=True, axis_index_groups=[[z * X + x...  6.64 us
    unnamed x20, local copies, waits for them, and re-layouts  6.36 us
    ppermute x6, starting transfers between devices, z_shift(): lax.ppermute(v, 'ctx', [(i, (i + s * X) % (Z * X)) for i in range(Z * X)])  6.27 us
  transfers between devices with their start and end apart: 24, of which 15 were waited for; matrix products, arithmetic and copies ran while one was open for 3% of the time, Pallas kernels for 1%

profile of v1, /device:TPU:1, one launch (start us, length us, event | category | flops | bytes accessed | tf_op | source)
XLA Modules:
  0.0 97.2 jit_solution(3065830647329806993)
XLA Ops:
  0.7 1.1 %copy.12 = bf16[1,128,576]{2,1,0:T(8,128)(2,1)S(1)} copy(bf16[1,128,576]{1,2,0:T(8,128)(2,1)} %param.7) | data formatting | bytes 294912 | tf_op args[0]
  1.8 0.6 copy-done.3
  2.4 0.8 copy-done.2
  3.3 0.2 shard_map.110
  3.4 2.5 %collective-permute-start.3 = (bf16[128,640]{1,0:T(8,128)(2,1)S(1)}, bf16[128,640]{1,0:T(8,128)(2,1)S(1)}, u32[]{:S(2)}, u32[]{:S(2)}) collective-permute-start(bf16[128,640]{1,0:T(8,128)(2,1)S(1)} %get-tuple-element.28.c0), channel_id=1, source_target_pairs={{0,4},{1,5},{2,6},{3,7},{4,8},{5,9},{6,10},{7,11},{8,12},{9,13},{1... | collective-permute-start | bytes 491528 | tf_op jit(solution)/shard_map/ppermute | solution.py:30
  6.0 1.2 %collective-permute-start.2 = (bf16[1296,128]{1,0:T(8,128)(2,1)S(1)}, bf16[1296,128]{1,0:T(8,128)(2,1)S(1)}, u32[]{:S(2)}, u32[]{:S(2)}) collective-permute-start(bf16[1296,128]{1,0:T(8,128)(2,1)S(1)} %get-tuple-element.27.q0), channel_id=1, source_target_pairs={{0,1},{1,2},{2,3},{3,0},{4,5},{5,6},{6,7},{7,4},{8,9},{9,10},{10,1... | collective-permute-start | bytes 995336 | tf_op jit(solution)/shard_map/ppermute | solution.py:26
  7.2 2.5 %collective-permute-start.1 = (bf16[1296,128]{1,0:T(8,128)(2,1)S(1)}, bf16[1296,128]{1,0:T(8,128)(2,1)S(1)}, u32[]{:S(2)}, u32[]{:S(2)}) collective-permute-start(bf16[1296,128]{1,0:T(8,128)(2,1)S(1)} %get-tuple-element.27.q0), channel_id=1, source_target_pairs={{0,2},{1,3},{2,0},{3,1},{4,6},{5,7},{6,4},{7,5},{8,10},{9,11},{10,... | collective-permute-start | bytes 995336 | tf_op jit(solution)/shard_map/ppermute | solution.py:26
  9.6 1.2 %collective-permute-start = (bf16[1296,128]{1,0:T(8,128)(2,1)S(1)}, bf16[1296,128]{1,0:T(8,128)(2,1)S(1)}, u32[]{:S(2)}, u32[]{:S(2)}) collective-permute-start(bf16[1296,128]{1,0:T(8,128)(2,1)S(1)} %get-tuple-element.27.q0), channel_id=1, source_target_pairs={{0,3},{1,0},{2,1},{3,2},{4,7},{5,4},{6,5},{7,6},{8,11},{9,8},{10,9... | collective-permute-start | bytes 995336 | tf_op jit(solution)/shard_map/ppermute | solution.py:26
  10.8 3.0 %collective-permute-done.3.c1 = bf16[128,640]{1,0:T(8,128)(2,1)S(1)} collective-permute-done((bf16[128,640]{1,0:T(8,128)(2,1)S(1)}, bf16[128,640]{1,0:T(8,128)(2,1)S(1)}, u32[]{:S(2)}, u32[]{:S(2)}) %collective-permute-start.3) | collective-permute-done | bytes 163872 | tf_op jit(solution)/shard_map/ppermute | solution.py:30
  13.8 5.7 %collective-permute-done.4.c2 = bf16[128,640]{1,0:T(8,128)(2,1)S(1)} collective-permute-done((bf16[128,640]{1,0:T(8,128)(2,1)S(1)}, bf16[128,640]{1,0:T(8,128)(2,1)S(1)}, u32[]{:S(2)}, u32[]{:S(2)}) %collective-permute-start.4) | collective-permute-done | bytes 163872 | tf_op jit(solution)/shard_map/ppermute | solution.py:30
  19.6 4.0 %collective-permute-done.1.q2 = bf16[1296,128]{1,0:T(8,128)(2,1)S(1)} collective-permute-done((bf16[1296,128]{1,0:T(8,128)(2,1)S(1)}, bf16[1296,128]{1,0:T(8,128)(2,1)S(1)}, u32[]{:S(2)}, u32[]{:S(2)}) %collective-permute-start.1) | collective-permute-done | bytes 331808 | tf_op jit(solution)/shard_map/ppermute | solution.py:26
  23.6 1.5 %collective-permute-done.5.c3 = bf16[128,640]{1,0:T(8,128)(2,1)S(1)} collective-permute-done((bf16[128,640]{1,0:T(8,128)(2,1)S(1)}, bf16[128,640]{1,0:T(8,128)(2,1)S(1)}, u32[]{:S(2)}, u32[]{:S(2)}) %collective-permute-start.5) | collective-permute-done | bytes 163872 | tf_op jit(solution)/shard_map/ppermute | solution.py:30
  25.1 1.0 %copy-done.5 = bf16[512,512]{1,0:T(8,128)(2,1)S(1)} copy-done((bf16[512,512]{1,0:T(8,128)(2,1)S(1)}, bf16[512,512]{1,0:T(8,128)(2,1)}, u32[]{:S(2)}) %copy-start.5) | copy-done | bytes 524312
  26.1 4.0 %shard_map.111 = (bf16[4,512,256]{2,1,0:T(8,128)(2,1)S(1)}, bf16[4,512,128]{2,1,0:T(8,128)(2,1)S(1)}, bf16[4,512,256]{2,1,0:T(8,128)(2,1)S(1)}, bf16[4,512,128]{...) custom-call(s32[3]{0:T(128)S(1)} %pad_add_fusion.where, bf16[1296,128]{1,0:T(8,128)(2,1)S(1)} %get-tuple-element.27.q0, ...), custom_call_target="tpu_custom_call" | custom-call | flops 1400000000 | bytes 8388608 | tf_op jit(solution)/shard_map/pallas_call | solution.py:116
  30.1 1.0 copy-done.7
  31.1 1.0 %copy-done.8 = bf16[4,512,256]{2,1,0:T(8,128)(2,1)} copy-done((bf16[4,512,256]{2,1,0:T(8,128)(2,1)}, bf16[4,512,256]{2,1,0:T(8,128)(2,1)S(1)}, u32[]{:S(2)}) %copy-start.8) | copy-done | bytes 1048600
  32.1 2.3 %collective-permute-start.8 = (f32[16,512]{1,0:T(8,128)S(1)}, f32[16,512]{1,0:T(8,128)S(1)}, u32[]{:S(2)}, u32[]{:S(2)}) collective-permute-start(f32[16,512]{1,0:T(8,128)S(1)} %get-tuple-element.29.t0), channel_id=1, source_target_pairs={{0,3},{1,0},{2,1},{3,2},{4,7},{5,4},{6,5},{7,6},{8,11},{9,8},{10,9... | collective-permute-start | bytes 98312 | tf_op jit(solution)/shard_map/ppermute | solution.py:26
  34.3 0.4 collective-permute-start.7
  34.7 0.6 collective-permute-start.6
  35.4 3.3 %collective-permute-done.7.t2 = f32[16,512]{1,0:T(8,128)S(1)} collective-permute-done((f32[16,512]{1,0:T(8,128)S(1)}, f32[16,512]{1,0:T(8,128)S(1)}, u32[]{:S(2)}, u32[]{:S(2)}) %collective-permute-start.7) | collective-permute-done | bytes 32800 | tf_op jit(solution)/shard_map/ppermute | solution.py:26
  38.6 0.3 collective-permute-done.6.t1
  39.0 7.2 %shard_map.112 = (bf16[4,128,512]{2,1,0:T(8,128)(2,1)S(1)}, bf16[4,128,512]{2,1,0:T(8,128)(2,1)S(1)}, bf16[128,640]{1,0:T(8,128)(2,1)S(1)}, bf16[128,640]{1,0:T(...) custom-call(s32[3]{0:T(128)S(1)} %pad_add_fusion.where, ...), custom_call_target="tpu_custom_call" | custom-call | flops 3000000000 | bytes 10485760 | tf_op jit(solution)/shard_map/pallas_call | solution.py:176
  46.1 4.9 %collective-permute-start.15 = (bf16[4,128,512]{2,1,0:T(8,128)(2,1)S(1)}, bf16[4,128,512]{2,1,0:T(8,128)(2,1)S(1)}, u32[]{:S(2)}, u32[]{:S(2)}) collective-permute-start(bf16[4,128,512]{2,1,0:T(8,128)(2,1)S(1)} %get-tuple-element.44), channel_id=1, source_target_pairs={{0,32},{32,0},{64,96},{96,64},{128,160},{160,128},{192,224},{224,1... | collective-permute-start | bytes 1572872 | tf_op jit(solution)/shard_map/ppermute | solution.py:38
  51.0 1.2 %collective-permute-start.12 = (bf16[128,640]{1,0:T(8,128)(2,1)}, bf16[128,640]{1,0:T(8,128)(2,1)S(1)}, u32[]{:S(2)}, u32[]{:S(2)}) collective-permute-start(bf16[128,640]{1,0:T(8,128)(2,1)} %get-tuple-element.39), channel_id=1, source_target_pairs={{0,28},{1,29},{2,30},{3,31},{4,0},{5,1},{6,2},{7,3},{8,4},{9,5},{1... | collective-permute-start | bytes 491528 | tf_op jit(solution)/shard_map/ppermute | solution.py:30
  52.2 1.0 %collective-permute-start.10 = (bf16[128,768]{1,0:T(8,128)(2,1)S(1)}, bf16[128,768]{1,0:T(8,128)(2,1)S(1)}, u32[]{:S(2)}, u32[]{:S(2)}) collective-permute-start(bf16[128,768]{1,0:T(8,128)(2,1)S(1)} %get-tuple-element.37), channel_id=1, source_target_pairs={{0,2},{1,3},{2,0},{3,1},{4,6},{5,7},{6,4},{7,5},{8,10},{9,11},{10,... | collective-permute-start | bytes 589832 | tf_op jit(solution)/shard_map/ppermute | solution.py:26
  53.2 1.9 %collective-permute-start.11 = (bf16[128,768]{1,0:T(8,128)(2,1)S(1)}, bf16[128,768]{1,0:T(8,128)(2,1)S(1)}, u32[]{:S(2)}, u32[]{:S(2)}) collective-permute-start(bf16[128,768]{1,0:T(8,128)(2,1)S(1)} %get-tuple-element.38), channel_id=1, source_target_pairs={{0,3},{1,0},{2,1},{3,2},{4,7},{5,4},{6,5},{7,6},{8,11},{9,8},{10,9... | collective-permute-start | bytes 589832 | tf_op jit(solution)/shard_map/ppermute | solution.py:26
  55.2 1.9 %collective-permute-done.12 = bf16[128,640]{1,0:T(8,128)(2,1)S(1)} collective-permute-done((bf16[128,640]{1,0:T(8,128)(2,1)}, bf16[128,640]{1,0:T(8,128)(2,1)S(1)}, u32[]{:S(2)}, u32[]{:S(2)}) %collective-permute-start.12) | collective-permute-done | bytes 163872 | tf_op jit(solution)/shard_map/ppermute | solution.py:30
  57.1 2.5 %collective-permute-start.13 = (bf16[128,640]{1,0:T(8,128)(2,1)S(1)}, bf16[128,640]{1,0:T(8,128)(2,1)S(1)}, u32[]{:S(2)}, u32[]{:S(2)}) collective-permute-start(bf16[128,640]{1,0:T(8,128)(2,1)S(1)} %add_convert_fusion.3), channel_id=1, source_target_pairs={{0,28},{1,29},{2,30},{3,31},{4,0},{5,1},{6,2},{7,3},{8,4},{9,5},{1... | collective-permute-start | bytes 491528 | tf_op jit(solution)/shard_map/ppermute | solution.py:30
  59.6 0.7 shard_map.113
  60.3 3.5 %collective-permute-done.9 = bf16[128,768]{1,0:T(8,128)(2,1)S(1)} collective-permute-done((bf16[128,768]{1,0:T(8,128)(2,1)S(1)}, bf16[128,768]{1,0:T(8,128)(2,1)S(1)}, u32[]{:S(2)}, u32[]{:S(2)}) %collective-permute-start.9) | collective-permute-done | bytes 196640 | tf_op jit(solution)/shard_map/ppermute | solution.py:26
  63.8 0.3 collective-permute-done.11
  64.1 0.1 add_convert_fusion
  64.2 1.8 %collective-permute-done.16 = bf16[128,512]{1,0:T(8,128)(2,1)S(1)} collective-permute-done((bf16[128,512]{1,0:T(8,128)(2,1)S(1)}, bf16[128,512]{1,0:T(8,128)(2,1)S(1)}, u32[]{:S(2)}, u32[]{:S(2)}) %collective-permute-start.16) | collective-permute-done | bytes 131104 | tf_op jit(solution)/shard_map/ppermute | solution.py:26
  66.0 3.1 %collective-permute-done.17 = bf16[128,512]{1,0:T(8,128)(2,1)S(1)} collective-permute-done((bf16[128,512]{1,0:T(8,128)(2,1)S(1)}, bf16[128,512]{1,0:T(8,128)(2,1)S(1)}, u32[]{:S(2)}, u32[]{:S(2)}) %collective-permute-start.17) | collective-permute-done | bytes 131104 | tf_op jit(solution)/shard_map/ppermute | solution.py:26
  69.2 0.1 collective-permute-done.18
  69.3 0.7 add_convert_fusion.4
  70.0 5.2 %all-to-all-start = ((bf16[8,16,512]{2,1,0:T(8,128)(2,1)}), bf16[8,16,512]{2,1,0:T(8,128)(2,1)S(1)}, u32[]{:S(2)}, u32[]{:S(2)}) async-start(bf16[8,16,512]{2,1,0:T(8,128)(2,1)} %bitcast.10), calls=%async_computation | async-start | bytes 262144 | tf_op jit(solution)/shard_map/all_to_all | solution.py:217
  75.2 0.7 slice_bitcast_fusion
  75.9 0.6 slice_bitcast_fusion.1
  76.5 6.6 %all-to-all-done = bf16[8,16,512]{2,1,0:T(8,128)(2,1)S(1)} async-done(((bf16[8,16,512]{2,1,0:T(8,128)(2,1)}), bf16[8,16,512]{2,1,0:T(8,128)(2,1)S(1)}, u32[]{:S(2)}, u32[]{:S(2)}) %all-to-all-start) | async-done | bytes 131104 | tf_op jit(solution)/shard_map/all_to_all | solution.py:217
  83.2 2.8 %collective-permute-start.21 = (bf16[16,512]{1,0:T(8,128)(2,1)S(1)}, bf16[16,512]{1,0:T(8,128)(2,1)S(1)}, u32[]{:S(2)}, u32[]{:S(2)}) collective-permute-start(bf16[16,512]{1,0:T(8,128)(2,1)S(1)} %reduce_sum.12), channel_id=1, source_target_pairs={{0,192},{32,224},{64,0},{96,32},{128,64},{160,96},{192,128},{224,1... | collective-permute-start | bytes 49160 | tf_op jit(solution)/shard_map/ppermute | solution.py:34
  86.0 0.3 collective-permute-start.20
  86.3 0.7 collective-permute-start.19
  87.2 2.9 %collective-permute-done.20 = bf16[16,512]{1,0:T(8,128)(2,1)S(1)} collective-permute-done((bf16[16,512]{1,0:T(8,128)(2,1)S(1)}, bf16[16,512]{1,0:T(8,128)(2,1)S(1)}, u32[]{:S(2)}, u32[]{:S(2)}) %collective-permute-start.20) | collective-permute-done | bytes 16416 | tf_op jit(solution)/shard_map/ppermute | solution.py:34
  90.1 0.2 collective-permute-done.19
  90.3 5.5 %collective-permute-start.22 = (f32[16,512]{1,0:T(8,128)S(1)}, f32[16,512]{1,0:T(8,128)S(1)}, u32[]{:S(2)}, u32[]{:S(2)}) collective-permute-start(f32[16,512]{1,0:T(8,128)S(1)} %convert_add_fusion), channel_id=1, source_target_pairs={{0,32},{32,0},{64,96},{96,64},{128,160},{160,128},{192,224},{224,1... | collective-permute-start | bytes 98312 | tf_op jit(solution)/shard_map/ppermute | solution.py:38
  95.8 0.8 copy.13
  96.6 0.6 broadcast_select_fusion
  (35 shorter events, 0.5 us)
Async XLA Ops:
  0.6 1.1 %copy-start.1 = (bf16[1,128,512]{2,1,0:T(8,128)(2,1)S(1)}, bf16[1,128,512]{2,1,0:T(8,128)(2,1)}, u32[]{:S(2)}) copy-start(bf16[1,128,512]{2,1,0:T(8,128)(2,1)} %param.12) | copy-start | bytes 393220
  0.6 1.1 %copy-start = (bf16[1,128,512]{2,1,0:T(8,128)(2,1)S(1)}, bf16[1,128,512]{2,1,0:T(8,128)(2,1)}, u32[]{:S(2)}) copy-start(bf16[1,128,512]{2,1,0:T(8,128)(2,1)} %param.8) | copy-start | bytes 393220
  1.8 0.7 copy-start.3
  2.4 0.8 copy-start.2
  3.3 21.8 %copy-start.4 = (bf16[512,512]{1,0:T(8,128)(2,1)S(1)}, bf16[512,512]{1,0:T(8,128)(2,1)}, u32[]{:S(2)}) copy-start(bf16[512,512]{1,0:T(8,128)(2,1)} %wk.3) | copy-start | bytes 1572868
  3.4 10.4 %collective-permute-start.3 = (bf16[128,640]{1,0:T(8,128)(2,1)S(1)}, bf16[128,640]{1,0:T(8,128)(2,1)S(1)}, u32[]{:S(2)}, u32[]{:S(2)}) collective-permute-start(bf16[128,640]{1,0:T(8,128)(2,1)S(1)} %get-tuple-element.28.c0), channel_id=1, source_target_pairs={{0,4},{1,5},{2,6},{3,7},{4,8},{5,9},{6,10},{7,11},{8,12},{9,13},{1... | collective-permute-start | bytes 491528 | tf_op jit(solution)/shard_map/ppermute | solution.py:30
  6.0 13.6 %collective-permute-start.2 = (bf16[1296,128]{1,0:T(8,128)(2,1)S(1)}, bf16[1296,128]{1,0:T(8,128)(2,1)S(1)}, u32[]{:S(2)}, u32[]{:S(2)}) collective-permute-start(bf16[1296,128]{1,0:T(8,128)(2,1)S(1)} %get-tuple-element.27.q0), channel_id=1, source_target_pairs={{0,1},{1,2},{2,3},{3,0},{4,5},{5,6},{6,7},{7,4},{8,9},{9,10},{10,1... | collective-permute-start | bytes 995336 | tf_op jit(solution)/shard_map/ppermute | solution.py:26
  7.2 16.4 %collective-permute-start.1 = (bf16[1296,128]{1,0:T(8,128)(2,1)S(1)}, bf16[1296,128]{1,0:T(8,128)(2,1)S(1)}, u32[]{:S(2)}, u32[]{:S(2)}) collective-permute-start(bf16[1296,128]{1,0:T(8,128)(2,1)S(1)} %get-tuple-element.27.q0), channel_id=1, source_target_pairs={{0,2},{1,3},{2,0},{3,1},{4,6},{5,7},{6,4},{7,5},{8,10},{9,11},{10,... | collective-permute-start | bytes 995336 | tf_op jit(solution)/shard_map/ppermute | solution.py:26
  9.6 14.0 %collective-permute-start = (bf16[1296,128]{1,0:T(8,128)(2,1)S(1)}, bf16[1296,128]{1,0:T(8,128)(2,1)S(1)}, u32[]{:S(2)}, u32[]{:S(2)}) collective-permute-start(bf16[1296,128]{1,0:T(8,128)(2,1)S(1)} %get-tuple-element.27.q0), channel_id=1, source_target_pairs={{0,3},{1,0},{2,1},{3,2},{4,7},{5,4},{6,5},{7,6},{8,11},{9,8},{10,9... | collective-permute-start | bytes 995336 | tf_op jit(solution)/shard_map/ppermute | solution.py:26
  13.8 5.7 %collective-permute-start.4 = (bf16[128,640]{1,0:T(8,128)(2,1)S(1)}, bf16[128,640]{1,0:T(8,128)(2,1)S(1)}, u32[]{:S(2)}, u32[]{:S(2)}) collective-permute-start(bf16[128,640]{1,0:T(8,128)(2,1)S(1)} %collective-permute-done.3.c1), channel_id=1, source_target_pairs={{0,4},{1,5},{2,6},{3,7},{4,8},{5,9},{6,10},{7,11},{8,12},{9,13},{1... | collective-permute-start | bytes 491528 | tf_op jit(solution)/shard_map/ppermute | solution.py:30
  19.5 5.6 %collective-permute-start.5 = (bf16[128,640]{1,0:T(8,128)(2,1)S(1)}, bf16[128,640]{1,0:T(8,128)(2,1)S(1)}, u32[]{:S(2)}, u32[]{:S(2)}) collective-permute-start(bf16[128,640]{1,0:T(8,128)(2,1)S(1)} %collective-permute-done.4.c2), channel_id=1, source_target_pairs={{0,4},{1,5},{2,6},{3,7},{4,8},{5,9},{6,10},{7,11},{8,12},{9,13},{1... | collective-permute-start | bytes 491528 | tf_op jit(solution)/shard_map/ppermute | solution.py:30
  25.1 1.0 %copy-start.5 = (bf16[512,512]{1,0:T(8,128)(2,1)S(1)}, bf16[512,512]{1,0:T(8,128)(2,1)}, u32[]{:S(2)}) copy-start(bf16[512,512]{1,0:T(8,128)(2,1)} %wv.3) | copy-start | bytes 1572868
  26.1 12.8 %copy-start.6 = (bf16[512,512]{1,0:T(8,128)(2,1)S(1)}, bf16[512,512]{1,0:T(8,128)(2,1)}, u32[]{:S(2)}) copy-start(bf16[512,512]{1,0:T(8,128)(2,1)} %wv.3) | copy-start | bytes 1572868
  30.1 1.0 copy-start.7
  31.1 1.0 %copy-start.8 = (bf16[4,512,256]{2,1,0:T(8,128)(2,1)}, bf16[4,512,256]{2,1,0:T(8,128)(2,1)S(1)}, u32[]{:S(2)}) copy-start(bf16[4,512,256]{2,1,0:T(8,128)(2,1)S(1)} %get-tuple-element.32.kc) | copy-start | bytes 3145732
  32.1 3.3 %collective-permute-start.8 = (f32[16,512]{1,0:T(8,128)S(1)}, f32[16,512]{1,0:T(8,128)S(1)}, u32[]{:S(2)}, u32[]{:S(2)}) collective-permute-start(f32[16,512]{1,0:T(8,128)S(1)} %get-tuple-element.29.t0), channel_id=1, source_target_pairs={{0,3},{1,0},{2,1},{3,2},{4,7},{5,4},{6,5},{7,6},{8,11},{9,8},{10,9... | collective-permute-start | bytes 98312 | tf_op jit(solution)/shard_map/ppermute | solution.py:26
  34.3 4.3 %collective-permute-start.7 = (f32[16,512]{1,0:T(8,128)S(1)}, f32[16,512]{1,0:T(8,128)S(1)}, u32[]{:S(2)}, u32[]{:S(2)}) collective-permute-start(f32[16,512]{1,0:T(8,128)S(1)} %get-tuple-element.29.t0), channel_id=1, source_target_pairs={{0,2},{1,3},{2,0},{3,1},{4,6},{5,7},{6,4},{7,5},{8,10},{9,11},{10,... | collective-permute-start | bytes 98312 | tf_op jit(solution)/shard_map/ppermute | solution.py:26
  34.7 4.3 %collective-permute-start.6 = (f32[16,512]{1,0:T(8,128)S(1)}, f32[16,512]{1,0:T(8,128)S(1)}, u32[]{:S(2)}, u32[]{:S(2)}) collective-permute-start(f32[16,512]{1,0:T(8,128)S(1)} %get-tuple-element.29.t0), channel_id=1, source_target_pairs={{0,1},{1,2},{2,3},{3,0},{4,5},{5,6},{6,7},{7,4},{8,9},{9,10},{10,1... | collective-permute-start | bytes 98312 | tf_op jit(solution)/shard_map/ppermute | solution.py:26
  46.1 13.4 %collective-permute-start.15 = (bf16[4,128,512]{2,1,0:T(8,128)(2,1)S(1)}, bf16[4,128,512]{2,1,0:T(8,128)(2,1)S(1)}, u32[]{:S(2)}, u32[]{:S(2)}) collective-permute-start(bf16[4,128,512]{2,1,0:T(8,128)(2,1)S(1)} %get-tuple-element.44), channel_id=1, source_target_pairs={{0,32},{32,0},{64,96},{96,64},{128,160},{160,128},{192,224},{224,1... | collective-permute-start | bytes 1572872 | tf_op jit(solution)/shard_map/ppermute | solution.py:38
  51.0 6.0 %collective-permute-start.12 = (bf16[128,640]{1,0:T(8,128)(2,1)}, bf16[128,640]{1,0:T(8,128)(2,1)S(1)}, u32[]{:S(2)}, u32[]{:S(2)}) collective-permute-start(bf16[128,640]{1,0:T(8,128)(2,1)} %get-tuple-element.39), channel_id=1, source_target_pairs={{0,28},{1,29},{2,30},{3,31},{4,0},{5,1},{6,2},{7,3},{8,4},{9,5},{1... | collective-permute-start | bytes 491528 | tf_op jit(solution)/shard_map/ppermute | solution.py:30
  52.2 11.6 %collective-permute-start.9 = (bf16[128,768]{1,0:T(8,128)(2,1)S(1)}, bf16[128,768]{1,0:T(8,128)(2,1)S(1)}, u32[]{:S(2)}, u32[]{:S(2)}) collective-permute-start(bf16[128,768]{1,0:T(8,128)(2,1)S(1)} %get-tuple-element.36), channel_id=1, source_target_pairs={{0,1},{1,2},{2,3},{3,0},{4,5},{5,6},{6,7},{7,4},{8,9},{9,10},{10,1... | collective-permute-start | bytes 589832 | tf_op jit(solution)/shard_map/ppermute | solution.py:26
  52.2 11.6 %collective-permute-start.10 = (bf16[128,768]{1,0:T(8,128)(2,1)S(1)}, bf16[128,768]{1,0:T(8,128)(2,1)S(1)}, u32[]{:S(2)}, u32[]{:S(2)}) collective-permute-start(bf16[128,768]{1,0:T(8,128)(2,1)S(1)} %get-tuple-element.37), channel_id=1, source_target_pairs={{0,2},{1,3},{2,0},{3,1},{4,6},{5,7},{6,4},{7,5},{8,10},{9,11},{10,... | collective-permute-start | bytes 589832 | tf_op jit(solution)/shard_map/ppermute | solution.py:26
  53.2 10.9 %collective-permute-start.11 = (bf16[128,768]{1,0:T(8,128)(2,1)S(1)}, bf16[128,768]{1,0:T(8,128)(2,1)S(1)}, u32[]{:S(2)}, u32[]{:S(2)}) collective-permute-start(bf16[128,768]{1,0:T(8,128)(2,1)S(1)} %get-tuple-element.38), channel_id=1, source_target_pairs={{0,3},{1,0},{2,1},{3,2},{4,7},{5,4},{6,5},{7,6},{8,11},{9,8},{10,9... | collective-permute-start | bytes 589832 | tf_op jit(solution)/shard_map/ppermute | solution.py:26
  57.1 29.9 %collective-permute-start.13 = (bf16[128,640]{1,0:T(8,128)(2,1)S(1)}, bf16[128,640]{1,0:T(8,128)(2,1)S(1)}, u32[]{:S(2)}, u32[]{:S(2)}) collective-permute-start(bf16[128,640]{1,0:T(8,128)(2,1)S(1)} %add_convert_fusion.3), channel_id=1, source_target_pairs={{0,28},{1,29},{2,30},{3,31},{4,0},{5,1},{6,2},{7,3},{8,4},{9,5},{1... | collective-permute-start | bytes 491528 | tf_op jit(solution)/shard_map/ppermute | solution.py:30
  60.2 5.8 %collective-permute-start.16 = (bf16[128,512]{1,0:T(8,128)(2,1)S(1)}, bf16[128,512]{1,0:T(8,128)(2,1)S(1)}, u32[]{:S(2)}, u32[]{:S(2)}) collective-permute-start(bf16[128,512]{1,0:T(8,128)(2,1)S(1)} %get-tuple-element.46), channel_id=1, source_target_pairs={{0,1},{1,2},{2,3},{3,0},{4,5},{5,6},{6,7},{7,4},{8,9},{9,10},{10,1... | collective-permute-start | bytes 393224 | tf_op jit(solution)/shard_map/ppermute | solution.py:26
  63.8 5.3 %collective-permute-start.17 = (bf16[128,512]{1,0:T(8,128)(2,1)S(1)}, bf16[128,512]{1,0:T(8,128)(2,1)S(1)}, u32[]{:S(2)}, u32[]{:S(2)}) collective-permute-start(bf16[128,512]{1,0:T(8,128)(2,1)S(1)} %get-tuple-element.47), channel_id=1, source_target_pairs={{0,2},{1,3},{2,0},{3,1},{4,6},{5,7},{6,4},{7,5},{8,10},{9,11},{10,... | collective-permute-start | bytes 393224 | tf_op jit(solution)/shard_map/ppermute | solution.py:26
  63.8 5.4 %collective-permute-start.18 = (bf16[128,512]{1,0:T(8,128)(2,1)S(1)}, bf16[128,512]{1,0:T(8,128)(2,1)S(1)}, u32[]{:S(2)}, u32[]{:S(2)}) collective-permute-start(bf16[128,512]{1,0:T(8,128)(2,1)S(1)} %get-tuple-element.48), channel_id=1, source_target_pairs={{0,3},{1,0},{2,1},{3,2},{4,7},{5,4},{6,5},{7,6},{8,11},{9,8},{10,9... | collective-permute-start | bytes 393224 | tf_op jit(solution)/shard_map/ppermute | solution.py:26
  70.0 13.1 %all-to-all-start = ((bf16[8,16,512]{2,1,0:T(8,128)(2,1)}), bf16[8,16,512]{2,1,0:T(8,128)(2,1)S(1)}, u32[]{:S(2)}, u32[]{:S(2)}) async-start(bf16[8,16,512]{2,1,0:T(8,128)(2,1)} %bitcast.10), calls=%async_computation | async-start | bytes 262144 | tf_op jit(solution)/shard_map/all_to_all | solution.py:217
  83.2 4.0 %collective-permute-start.21 = (bf16[16,512]{1,0:T(8,128)(2,1)S(1)}, bf16[16,512]{1,0:T(8,128)(2,1)S(1)}, u32[]{:S(2)}, u32[]{:S(2)}) collective-permute-start(bf16[16,512]{1,0:T(8,128)(2,1)S(1)} %reduce_sum.12), channel_id=1, source_target_pairs={{0,192},{32,224},{64,0},{96,32},{128,64},{160,96},{192,128},{224,1... | collective-permute-start | bytes 49160 | tf_op jit(solution)/shard_map/ppermute | solution.py:34
  86.0 4.1 %collective-permute-start.20 = (bf16[16,512]{1,0:T(8,128)(2,1)S(1)}, bf16[16,512]{1,0:T(8,128)(2,1)S(1)}, u32[]{:S(2)}, u32[]{:S(2)}) collective-permute-start(bf16[16,512]{1,0:T(8,128)(2,1)S(1)} %reduce_sum.12), channel_id=1, source_target_pairs={{0,128},{32,160},{64,192},{96,224},{128,0},{160,32},{192,64},{224,... | collective-permute-start | bytes 49160 | tf_op jit(solution)/shard_map/ppermute | solution.py:34
  86.3 3.9 %collective-permute-start.19 = (bf16[16,512]{1,0:T(8,128)(2,1)S(1)}, bf16[16,512]{1,0:T(8,128)(2,1)S(1)}, u32[]{:S(2)}, u32[]{:S(2)}) collective-permute-start(bf16[16,512]{1,0:T(8,128)(2,1)S(1)} %reduce_sum.12), channel_id=1, source_target_pairs={{0,64},{32,96},{64,128},{96,160},{128,192},{160,224},{192,0},{224,... | collective-permute-start | bytes 49160 | tf_op jit(solution)/shard_map/ppermute | solution.py:34
  87.1 8.6 %collective-permute-start.14 = (bf16[128,640]{1,0:T(8,128)(2,1)S(1)}, bf16[128,640]{1,0:T(8,128)(2,1)S(1)}, u32[]{:S(2)}, u32[]{:S(2)}) collective-permute-start(bf16[128,640]{1,0:T(8,128)(2,1)S(1)} %add_convert_fusion.2), channel_id=1, source_target_pairs={{0,28},{1,29},{2,30},{3,31},{4,0},{5,1},{6,2},{7,3},{8,4},{9,5},{1... | collective-permute-start | bytes 491528 | tf_op jit(solution)/shard_map/ppermute | solution.py:30
  90.3 6.3 %collective-permute-start.22 = (f32[16,512]{1,0:T(8,128)S(1)}, f32[16,512]{1,0:T(8,128)S(1)}, u32[]{:S(2)}, u32[]{:S(2)}) collective-permute-start(f32[16,512]{1,0:T(8,128)S(1)} %convert_add_fusion), channel_id=1, source_target_pairs={{0,32},{32,0},{64,96},{96,64},{128,160},{160,128},{192,224},{224,1... | collective-permute-start | bytes 98312 | tf_op jit(solution)/shard_map/ppermute | solution.py:38

commit v2 on v1

v2 whole, which is shorter than its diff:
```python
import functools

import jax
import jax.numpy as jnp
from jax import lax
from jax.experimental import pallas as pl
from jax.experimental.pallas import tpu as pltpu
from jax.sharding import PartitionSpec as P

Z, X, Y = 8, 4, 4
HEADS, HEAD, ROPE, LATENT = 4, 128, 64, 512
ROWS = 128
REACH = 4
QROWS = X * ROWS
KROWS = REACH * ROWS
HALF = KROWS // 2
SCALE = (HEAD + ROPE) ** -0.5
NEG = -1e30
CUT = 640
PACK_VMEM = 60.5
BF, F32 = jnp.bfloat16, jnp.float32
NT = (((1,), (1,)), ((), ()))
TN = (((0,), (0,)), ((), ()))
VMEM = pl.BlockSpec(memory_space=pltpu.VMEM)
SMEM = pl.BlockSpec(memory_space=pltpu.SMEM)
HBM = pl.BlockSpec(memory_space=pltpu.HBM)


def x_shift(v, s):
    return lax.ppermute(v, "ctx", [(i, i // X * X + (i % X + s) % X) for i in range(Z * X)])


def z_shift(v, s):
    return lax.ppermute(v, "ctx", [(i, (i + s * X) % (Z * X)) for i in range(Z * X)])


def y_pair(v, far):
    pairs = [(i, 2 * ((Y - 1 - i // 2) if far else (i // 2 ^ 1)) + i % 2) for i in range(2 * Y)]
    return lax.ppermute(v, "dp", pairs)


def core_swap(v):
    return lax.ppermute(v, "dp", [(i, i ^ 1) for i in range(2 * Y)])


def call(kernel, out_shape, n_smem, n_vmem, n_hbm=0, scratch=(), flops=0, nbytes=0, vmem=16):
    return pl.pallas_call(
        kernel,
        out_shape=out_shape,
        in_specs=[SMEM] * n_smem + [VMEM] * n_vmem + [HBM] * n_hbm,
        out_specs=jax.tree.map(lambda _: VMEM, out_shape),
        scratch_shapes=list(scratch),
        compiler_params=pltpu.CompilerParams(vmem_limit_bytes=int(vmem * (1 << 20))),
        cost_estimate=pl.CostEstimate(flops=flops, bytes_accessed=nbytes, transcendentals=0),
    )


def pack_kernel(nope, rope, grad, kv_t, ids, q_out, ca_out, cb_out, kv_scr, ids_scr, sems):
    copies = [pltpu.make_async_copy(kv_t, kv_scr, sems.at[0]), pltpu.make_async_copy(ids, ids_scr, sems.at[1])]
    for n, (source, parts) in enumerate(((nope, 4), (grad, 4), (rope, 2))):
        for i in range(parts):
            at = n * 512 + i * 128
            copies.append(pltpu.make_async_copy(
                source.at[:, i * 128:(i + 1) * 128], q_out.at[at:at + 128, :], sems.at[len(copies)]))
    for copy in copies:
        copy.start()
    copies[0].wait()
    copies[1].wait()
    marks = jnp.broadcast_to(ids_scr[...].astype(F32), (128, 128)).astype(BF)
    q_out[1280:1296, :] = marks[:16]
    rows = jnp.concatenate([kv_scr[...], marks[:64]], axis=0).T
    ca_out[...] = rows[:64]
    cb_out[...] = rows[64:]
    for copy in copies[2:]:
        copy.wait()


def pack(nope, rope, grad, kv_t, ids):
    half = jax.ShapeDtypeStruct((64, 640), BF)
    return call(
        pack_kernel, (jax.ShapeDtypeStruct((1296, 128), BF), half, half), 0, 0, 5,
        scratch=[pltpu.VMEM((576, 128), BF), pltpu.VMEM((1, 128), jnp.int32), pltpu.SemaphoreType.DMA((12,))],
        nbytes=1 << 20, vmem=PACK_VMEM)(nope, rope, grad, kv_t, ids)


def keys_kernel(a0, a1, b0, b1, wk, wv, kc, vs, latents, marks, wk_out=None, wv_out=None):
    lane = lax.broadcasted_iota(jnp.int32, (64, 128), 1)
    for n, c in enumerate((a0, b0, a1, b1)):
        at = slice(n * 64, n * 64 + 64)
        latents[at, :] = c[:, :512]
        tail = c[:, 512:640].astype(F32)
        marks[at, :] = tail
        even = jnp.where(lane < 64, tail, 0.0)
        odd = pltpu.roll(even, 64, 1)
        for h in range(HEADS):
            kc[h, at, 128:256] = (odd if h % 2 else even).astype(BF)
    keys = jnp.dot(latents[...], wk[...], preferred_element_type=F32).astype(BF)
    values = jnp.dot(latents[...], wv[...], preferred_element_type=F32).astype(BF)
    for h in range(HEADS):
        kc[h, :, 0:128] = keys[:, h * 128:(h + 1) * 128]
        vs[h, :, :] = values[:, h * 128:(h + 1) * 128]
    if wk_out is not None:
        wk_out[...] = wk[...]
        wv_out[...] = wv[...]


def run_keys(ca, cb, wk, wv, hand_on):
    sds = jax.ShapeDtypeStruct
    return call(
        keys_kernel,
        (sds((4, HALF, 256), BF), sds((4, HALF, 128), BF), sds((HALF, LATENT), BF), sds((HALF, 128), F32),
         *([sds((512, 512), BF)] * (2 if hand_on else 0))),
        0, 6, flops=500_000_000, nbytes=2 << 20,
    )(*ca, *cb, wk, wv)


def stats_kernel(where, q0, q1, q2a, q2b, q3, kc0, kc1, vs0, vs1, marks0, marks1, qc, gs, es, dps, stats, bias, qid):
    xi, zi = where[0], where[1]
    for s, block in enumerate((q0, q1, (q2a, q2b), q3)):
        at = pl.ds(pl.multiple_of(((xi + s) & 3) * 128, 128), 128)

        def rows(first, count=128):
            if s != 2:
                return block[first:first + count, :]
            part, start = (block[1], first - CUT) if first >= CUT else (block[0], first)
            return part[start:start + count, :]

        for h in range(HEADS):
            qc[h, at, 0:128] = rows(h * 128)
            qc[h, at, 128:256] = rows(1024 + h // 2 * 128)
            gs[h, at, :] = rows(512 + h * 128)
        qid[:, at] = rows(1280, 16)
    q_marks = qid[0:1, :].astype(F32)
    q_pos = zi * QROWS + lax.broadcasted_iota(jnp.int32, (128, QROWS), 1)
    for j in range(REACH):
        at = slice(j * 128, j * 128 + 128)
        first = ((zi - j) & (Z - 1)) * QROWS + xi * 128
        k_pos = first + lax.broadcasted_iota(jnp.int32, (128, QROWS), 0)
        allowed = (k_pos <= q_pos) & ((marks0, marks1)[j // 2][j % 2 * 128:j % 2 * 128 + 128, 64:65] == q_marks)
        bias[at, :] = jnp.where(allowed, 0.0, NEG)
    for h in range(HEADS):
        for b in range(0, QROWS, 256):
            sl = slice(b, b + 256)
            parts = []
            for n, (kc, vs) in enumerate(((kc0, vs0), (kc1, vs1))):
                at = slice(n * HALF, (n + 1) * HALF)
                s = lax.dot_general(kc[h], qc[h, sl, :], NT, preferred_element_type=F32) * SCALE + bias[at, sl]
                dp = lax.dot_general(vs[h], gs[h, sl, :], NT, preferred_element_type=F32)
                dps[h, at, sl] = dp
                parts.append((at, s, dp))
            m = jnp.maximum(*[jnp.max(s, axis=0, keepdims=True) for _, s, _ in parts])
            total = cross = 0.0
            for at, s, dp in parts:
                e = jnp.exp(s - m)
                es[h, at, sl] = e
                total = total + jnp.sum(e, axis=0, keepdims=True)
                cross = cross + jnp.sum(e * dp, axis=0, keepdims=True)
            stats[h:h + 1, sl] = m
            stats[4 + h:5 + h, sl] = total
            stats[8 + h:9 + h, sl] = cross
    stats[12:16, :] = jnp.zeros((4, QROWS), F32)


def run_stats(where, qs, *keys):
    sds = jax.ShapeDtypeStruct
    return call(
        stats_kernel,
        (sds((4, QROWS, 256), BF), sds((4, QROWS, 128), BF),
         sds((4, KROWS, QROWS), F32), sds((4, KROWS, QROWS), F32), sds((16, QROWS), F32)),
        1, 11, scratch=[pltpu.VMEM((KROWS, QROWS), F32), pltpu.VMEM((16, QROWS), BF)],
        flops=1_000_000_000, nbytes=8 << 20,
    )(where, *qs, *keys)


def weight_kernel(where, t0, t1, t2, t3, qc, gs, es, dps, latents0, latents1, wk, wv, w_keep, w_send, ds, dkv, tail, d3, p_scr):
    core = where[2]
    tops = [t[0:4, :] for t in (t0, t1, t2, t3)]
    top = functools.reduce(jnp.maximum, tops)
    total = jnp.zeros((4, QROWS), F32)
    cross = jnp.zeros((4, QROWS), F32)
    for t, m in zip((t0, t1, t2, t3), tops):
        f = jnp.exp(m - top)
        total = total + f * t[4:8, :]
        cross = cross + f * t[8:12, :]
    inv = 1.0 / total
    delta = cross * inv
    scaled = jnp.exp(tops[0] - top) * inv
    rope_grad = [jnp.zeros((KROWS, 128), F32), jnp.zeros((KROWS, 128), F32)]
    for h in range(HEADS):
        for b in range(0, QROWS, 256):
            sl = slice(b, b + 256)
            p = es[h, :, sl] * scaled[h:h + 1, sl]
            p_scr[h % 2, :, sl] = p.astype(BF)
            ds[h, :, sl] = (p * (dps[h, :, sl] - delta[h:h + 1, sl]) * SCALE).astype(BF)
        cols = slice(h * 128, (h + 1) * 128)
        dkv[1, :, cols] = jnp.dot(p_scr[h % 2], gs[h], preferred_element_type=F32).astype(BF)
        dk = jnp.dot(ds[h], qc[h], preferred_element_type=F32)
        dkv[0, :, cols] = dk[:, :128].astype(BF)
        rope_grad[h % 2] = rope_grad[h % 2] + dk[:, 128:]
    for out, which in ((w_send, 1 - core), (w_keep, core)):
        w = (lax.dot_general(dkv[which, :HALF], latents0[...], TN, preferred_element_type=F32)
             + lax.dot_general(dkv[which, HALF:], latents1[...], TN, preferred_element_type=F32)).astype(BF)
        for r in range(32):
            out[r % 4, r // 4 * 16:r // 4 * 16 + 16, :] = w[r * 16:r * 16 + 16, :]
    lane = lax.broadcasted_iota(jnp.int32, (KROWS, 128), 1)
    tail[...] = jnp.where(lane < 64, rope_grad[0] + pltpu.roll(rope_grad[1], 64, 1), 0.0).astype(BF)
    far = slice(3 * ROWS, KROWS)
    d3[:, :512] = (lax.dot_general(dkv[0, far], wk[...], NT, preferred_element_type=F32)
                   + lax.dot_general(dkv[1, far], wv[...], NT, preferred_element_type=F32)).astype(BF)
    d3[:, 512:640] = tail[far, :]


def run_weight(where, ts, *mats):
    sds = jax.ShapeDtypeStruct
    return call(
        weight_kernel,
        (sds((4, 128, 512), BF), sds((4, 128, 512), BF), sds((4, KROWS, QROWS), BF), sds((2, KROWS, 512), BF),
         sds((KROWS, 128), BF), sds((128, 640), BF)),
        1, 12, scratch=[pltpu.VMEM((2, KROWS, QROWS), BF)], flops=1_500_000_000, nbytes=10 << 20,
    )(where, *ts, *mats)


def grads_kernel(where, ds, dkv, tail, kc0, kc1, wk, wv, d0, d1, d2, o0, o1, o2, o3, dq):
    xi = where[0]
    near = slice(0, 3 * ROWS)
    lat = (lax.dot_general(dkv[0, near], wk[...], NT, preferred_element_type=F32)
           + lax.dot_general(dkv[1, near], wv[...], NT, preferred_element_type=F32)).astype(BF)
    for j, d in enumerate((d0, d1, d2)):
        d[:, :512] = lat[j * 128:(j + 1) * 128, :]
        d[:, 512:640] = tail[j * 128:(j + 1) * 128, :]
    for p in range(2):
        pair = 0.0
        for h in (2 * p, 2 * p + 1):
            dqh = (lax.dot_general(ds[h, :HALF], kc0[h], TN, preferred_element_type=F32)
                   + lax.dot_general(ds[h, HALF:], kc1[h], TN, preferred_element_type=F32))
            dq[:, h * 128:(h + 1) * 128] = dqh[:, :128].astype(BF)
            pair = pair + dqh[:, 128:]
        dq[:, 512 + p * 128:640 + p * 128] = pair.astype(BF)
    for s, o in enumerate((o0, o1, o2, o3)):
        o[...] = dq[pl.ds(pl.multiple_of(((xi + s) & 3) * 128, 128), 128), :]


def run_grads(where, ds, dkv, tail, kc0, kc1, wk, wv):
    sds = jax.ShapeDtypeStruct
    return call(
        grads_kernel,
        tuple([sds((128, 640), BF)] * 3 + [sds((128, 768), BF)] * 4),
        1, 7, scratch=[pltpu.VMEM((QROWS, 768), BF)], flops=1_500_000_000, nbytes=10 << 20,
    )(where, ds, dkv, tail, kc0, kc1, wk, wv)


def spread_kernel(where, keep, recv, o0, o1, o2, o3):
    xi = where[0]
    for s, o in enumerate((o0, o1, o2, o3)):
        at = (xi + s) & 3
        o[...] = (keep[at].astype(F32) + recv[at].astype(F32)).astype(BF)


def spread(where, keep, recv):
    return call(spread_kernel, tuple([jax.ShapeDtypeStruct((128, 512), BF)] * 4), 1, 2, nbytes=2 << 20)(where, keep, recv)


def wide(*refs):
    return functools.reduce(jnp.add, [r[...].astype(F32) for r in refs])


def sum_kernel(*refs):
    refs[-1][...] = wide(*refs[:-1]).astype(refs[-1].dtype)


def add_up(*parts, dtype=BF):
    return call(sum_kernel, jax.ShapeDtypeStruct(parts[0].shape, dtype), 0, len(parts), nbytes=1 << 20)(*parts)


def sum_z_kernel(parts, w):
    w[...] = jnp.sum(parts[...].reshape(Z, 16, 512).astype(F32), axis=0).astype(BF)


def query_kernel(q0, q1, q2, q3, nope, rope):
    q = wide(q0, q1, q2, q3).astype(BF)
    nope[...] = q[:, :512]
    rope[...] = q[:, 512:]


def latent_kernel(d1, d0, latent):
    latent[...] = wide(d1, d0).astype(BF)[:, :576].T


def body(kv_latent, q_nope, q_rope, w_key_up, w_value_up, out_grad, segment_ids):
    ctx = lax.axis_index("ctx")
    dp = lax.axis_index("dp")
    core = dp % 2
    where = jnp.stack([ctx % X, ctx // X, core]).astype(jnp.int32)
    q, ca, cb = pack(q_nope[0], q_rope[0], out_grad[0], kv_latent[0].T, segment_ids)
    ca, cb = [ca], [cb]
    for _ in range(REACH - 1):
        ca.append(z_shift(ca[-1], 1))
        cb.append(z_shift(cb[-1], 1))
    right, left = x_shift(q, -1), x_shift(q, 1)
    qs = (q, right, x_shift(left[:CUT], 1), x_shift(right[CUT:], -1), left)
    kc0, vs0, latents0, marks0, wk, wv = run_keys(ca[:2], cb[:2], w_key_up, w_value_up, True)
    kc1, vs1, latents1, marks1 = run_keys(ca[2:], cb[2:], wk, wv, False)
    qc, gs, es, dps, stats = run_stats(where, qs, kc0, kc1, vs0, vs1, marks0, marks1)
    ts = (stats, x_shift(stats, 1), x_shift(stats, 2), x_shift(stats, -1))
    w_keep, w_send, ds, dkv, tail, d3 = run_weight(where, ts, qc, gs, es, dps, latents0, latents1, wk, wv)
    received = core_swap(w_send)
    d0, d1, d2, o0, o1, o2, o3 = run_grads(where, ds, dkv, tail, kc0, kc1, wk, wv)
    pieces = spread(where, w_keep, received)
    sds = jax.ShapeDtypeStruct
    w = add_up(pieces[0], x_shift(pieces[1], 1), x_shift(pieces[2], 2), x_shift(pieces[3], -1))
    w = lax.all_to_all(w, "ctx", 0, 0, tiled=True, axis_index_groups=[[z * X + x for z in range(Z)] for x in range(X)])
    w = call(sum_z_kernel, sds((16, 512), BF), 0, 1, nbytes=1 << 18)(w)
    w = add_up(w, y_pair(w, False))
    w = add_up(w, y_pair(w, True), dtype=F32)
    other = core_swap(w)
    grad_key = jnp.where(core == 0, w, other)
    grad_value = jnp.where(core == 0, other, w)
    d = add_up(z_shift(d3, -1), d2)
    d = add_up(z_shift(d, -1), d1)
    grad_latent = call(latent_kernel, sds((576, 128), BF), 0, 2, nbytes=1 << 20)(z_shift(d, -1), d0)
    grad_nope, grad_rope = call(query_kernel, (sds((128, 512), BF), sds((128, 256), BF)), 0, 4, nbytes=1 << 20)(
        o0, x_shift(o1, 1), x_shift(o2, 2), x_shift(o3, -1))
    return grad_nope[None], grad_rope[None], grad_latent.T[None], grad_key, grad_value


def solution(mesh):
    return jax.shard_map(
        body,
        mesh=mesh,
        in_specs=(
            P("dp", "ctx", None),
            P("dp", "ctx", None),
            P("dp", "ctx", None),
            P(),
            P(),
            P("dp", "ctx", None),
            P("dp", "ctx"),
        ),
        out_specs=(
            P("dp", "ctx", None),
            P("dp", "ctx", None),
            P("dp", "ctx", None),
            P("ctx", None),
            P("ctx", None),
        ),
        check_vma=False,
    )
```

time: 97.7 us -> 85.5 us (0.88)
  waiting for transfers between devices: 38.3 us -> 19.2 us
  starting transfers between devices: 36.8 us -> 46.8 us
  local copies, waits for them, and re-layouts: 7.66 us -> 3.89 us
  Pallas kernels: 12 us -> 13.8 us
  other arithmetic: 1.7 us -> 0.71 us
    ppermute x12 -> x13, waiting for transfers between devices: 16.5 us -> 5.53 us  [x_shift(): lax.ppermute(v, 'ctx', [(i, i // X * X + (i % X + s) % X) for i in range(...]
    all_to_all x1, waiting for transfers between devices: 6.64 us -> 0.64 us  [body(): lax.all_to_all(w, 'ctx', 0, 0, tiled=True, axis_index_groups=[[z * X + x...]
    ppermute x12 -> x13, starting transfers between devices: 11.2 us -> 16.4 us  [x_shift(): lax.ppermute(v, 'ctx', [(i, i // X * X + (i % X + s) % X) for i in range(...]
    ppermute x6 -> x9, starting transfers between devices: 6.27 us -> 10.6 us  [z_shift(): lax.ppermute(v, 'ctx', [(i, (i + s * X) % (Z * X)) for i in range(Z * X)])]
    pallas_call x2 -> x13, Pallas kernels: 7.33 us -> 9.96 us  [the longest x1 2.99 us: run_weight(): call(weight_kernel, (sds((4, 128, 512), BF), sds((4, 128, 512), BF), sds(...]
    unnamed x20 -> x10, local copies, waits for them, and re-layouts: 6.36 us -> 3.86 us
    ppermute x6 -> x9, waiting for transfers between devices: 12.1 us -> 10.3 us  [z_shift(): lax.ppermute(v, 'ctx', [(i, (i + s * X) % (Z * X)) for i in range(Z * X)])]
    broadcast_in_dim x2 -> x0, local copies, waits for them, and re-layouts: 1.3 us -> none  [the longest x1 0.66 us: body(): grad_q[None, :, :512]]
  transfers between devices with their start and end apart: 24 -> 27, of which waited for: 15 -> 12; matrix products, arithmetic and copies ran while one was open for 3% -> 0% of each run, Pallas kernels for 1% -> 7%
where the time goes in v2:
time: 85.5 us; the launch traced here: 85.2 us
  starting transfers between devices  46.8 us (55%)
  waiting for transfers between devices  19.2 us (22%)
  Pallas kernels  13.8 us (16%)
  local copies, waits for them, and re-layouts  3.89 us (5%)
    ppermute x13, starting transfers between devices, x_shift(): lax.ppermute(v, 'ctx', [(i, i // X * X + (i % X + s) % X) for i in range(...  16.4 us
    ppermute x9, starting transfers between devices, z_shift(): lax.ppermute(v, 'ctx', [(i, (i + s * X) % (Z * X)) for i in range(Z * X)])  10.6 us
    ppermute x9, waiting for transfers between devices, z_shift(): lax.ppermute(v, 'ctx', [(i, (i + s * X) % (Z * X)) for i in range(Z * X)])  10.3 us
    ppermute x2, starting transfers between devices, core_swap(): return lax.ppermute(v, 'dp', [(i, i ^ 1) for i in range(2 * Y)])  10.3 us
    ppermute x13, waiting for transfers between devices, x_shift(): lax.ppermute(v, 'ctx', [(i, i // X * X + (i % X + s) % X) for i in range(...  5.53 us
    all_to_all x1, starting transfers between devices, body(): lax.all_to_all(w, 'ctx', 0, 0, tiled=True, axis_index_groups=[[z * X + x...  5.36 us
    ppermute x2, starting transfers between devices, y_pair(): return lax.ppermute(v, 'dp', pairs)  4.12 us
    unnamed x10, local copies, waits for them, and re-layouts  3.86 us
  transfers between devices with their start and end apart: 27, of which 12 were waited for; matrix products, arithmetic and copies ran while one was open for 0% of the time, Pallas kernels for 7%

profile of v2, /device:TPU:1, one launch (start us, length us, event | category | flops | bytes accessed | tf_op | source)
XLA Modules:
  0.0 85.2 jit_solution(6886872671428754376)
XLA Ops:
  0.6 1.9 %shard_map.110 = (bf16[1296,128]{1,0:T(8,128)(2,1)}, bf16[64,640]{1,0:T(8,128)(2,1)}, bf16[64,640]{1,0:T(8,128)(2,1)}) custom-call(bf16[128,512]{1,0:T(8,128)(2,1)} %bitcast.19, bf16[128,256]{1,0:T(8,128)(2,1)} %bitcast.21, bf16[128,512]{1,0:T(8,128)(2,1)} %bitcast.20, bf16[576,128]{1,0:T(8,128)(2,1)} %bitcast.17, s32[1,128]{1,0:T(1,128)} %ids.1), custom_call_target="tpu_custom_call" | custom-call | bytes 1048576 | tf_op jit(solution)/shard_map/pallas_call | solution.py:80
  2.6 2.1 %collective-permute-start.1 = (bf16[1296,128]{1,0:T(8,128)(2,1)}, bf16[1296,128]{1,0:T(8,128)(2,1)S(1)}, u32[]{:S(2)}, u32[]{:S(2)}) collective-permute-start(bf16[1296,128]{1,0:T(8,128)(2,1)} %get-tuple-element.42.q0), channel_id=1, source_target_pairs={{0,1},{1,2},{2,3},{3,0},{4,5},{5,6},{6,7},{7,4},{8,9},{9,10},{10,1... | collective-permute-start | bytes 995336 | tf_op jit(solution)/shard_map/ppermute | solution.py:30
  4.7 1.4 %collective-permute-start = (bf16[1296,128]{1,0:T(8,128)(2,1)}, bf16[1296,128]{1,0:T(8,128)(2,1)S(1)}, u32[]{:S(2)}, u32[]{:S(2)}) collective-permute-start(bf16[1296,128]{1,0:T(8,128)(2,1)} %get-tuple-element.42.q0), channel_id=1, source_target_pairs={{0,3},{1,0},{2,1},{3,2},{4,7},{5,4},{6,5},{7,6},{8,11},{9,8},{10,9... | collective-permute-start | bytes 995336 | tf_op jit(solution)/shard_map/ppermute | solution.py:30
  6.0 1.7 %collective-permute-start.4 = (bf16[64,640]{1,0:T(8,128)(2,1)}, bf16[64,640]{1,0:T(8,128)(2,1)S(1)}, u32[]{:S(2)}, u32[]{:S(2)}) collective-permute-start(bf16[64,640]{1,0:T(8,128)(2,1)} %get-tuple-element.43.a0), channel_id=1, source_target_pairs={{0,4},{1,5},{2,6},{3,7},{4,8},{5,9},{6,10},{7,11},{8,12},{9,13},{1... | collective-permute-start | bytes 245768 | tf_op jit(solution)/shard_map/ppermute | solution.py:34
  7.8 1.6 %collective-permute-start.5 = (bf16[64,640]{1,0:T(8,128)(2,1)}, bf16[64,640]{1,0:T(8,128)(2,1)S(1)}, u32[]{:S(2)}, u32[]{:S(2)}) collective-permute-start(bf16[64,640]{1,0:T(8,128)(2,1)} %get-tuple-element.44.b0), channel_id=1, source_target_pairs={{0,4},{1,5},{2,6},{3,7},{4,8},{5,9},{6,10},{7,11},{8,12},{9,13},{1... | collective-permute-start | bytes 245768 | tf_op jit(solution)/shard_map/ppermute | solution.py:34
  9.4 4.6 %collective-permute-done.4.a1 = bf16[64,640]{1,0:T(8,128)(2,1)S(1)} collective-permute-done((bf16[64,640]{1,0:T(8,128)(2,1)}, bf16[64,640]{1,0:T(8,128)(2,1)S(1)}, u32[]{:S(2)}, u32[]{:S(2)}) %collective-permute-start.4) | collective-permute-done | bytes 81952 | tf_op jit(solution)/shard_map/ppermute | solution.py:34
  14.1 1.2 %collective-permute-done.5.b1 = bf16[64,640]{1,0:T(8,128)(2,1)S(1)} collective-permute-done((bf16[64,640]{1,0:T(8,128)(2,1)}, bf16[64,640]{1,0:T(8,128)(2,1)S(1)}, u32[]{:S(2)}, u32[]{:S(2)}) %collective-permute-start.5) | collective-permute-done | bytes 81952 | tf_op jit(solution)/shard_map/ppermute | solution.py:34
  15.2 3.3 %collective-permute-done.6.a0 = bf16[64,640]{1,0:T(8,128)(2,1)S(1)} collective-permute-done((bf16[64,640]{1,0:T(8,128)(2,1)S(1)}, bf16[64,640]{1,0:T(8,128)(2,1)S(1)}, u32[]{:S(2)}, u32[]{:S(2)}) %collective-permute-start.6) | collective-permute-done | bytes 81952 | tf_op jit(solution)/shard_map/ppermute | solution.py:34
  18.6 1.2 %collective-permute-done.8.b0 = bf16[64,640]{1,0:T(8,128)(2,1)S(1)} collective-permute-done((bf16[64,640]{1,0:T(8,128)(2,1)S(1)}, bf16[64,640]{1,0:T(8,128)(2,1)S(1)}, u32[]{:S(2)}, u32[]{:S(2)}) %collective-permute-start.8) | collective-permute-done | bytes 81952 | tf_op jit(solution)/shard_map/ppermute | solution.py:34
  19.9 2.7 %collective-permute-start.3 = (bf16[656,128]{1,0:T(8,128)(2,1)S(1)}, bf16[656,128]{1,0:T(8,128)(2,1)S(1)}, u32[]{:S(2)}, u32[]{:S(2)}) collective-permute-start(bf16[656,128]{1,0:T(8,128)(2,1)S(1)} %slice.9), channel_id=1, source_target_pairs={{0,3},{1,0},{2,1},{3,2},{4,7},{5,4},{6,5},{7,6},{8,11},{9,8},{10,9... | collective-permute-start | bytes 503816 | tf_op jit(solution)/shard_map/ppermute | solution.py:30
  22.7 1.0 %copy-done = bf16[512,512]{1,0:T(8,128)(2,1)S(1)} copy-done((bf16[512,512]{1,0:T(8,128)(2,1)S(1)}, bf16[512,512]{1,0:T(8,128)(2,1)}, u32[]{:S(2)}) %copy-start) | copy-done | bytes 524312
  23.7 1.0 %copy-done.1 = bf16[512,512]{1,0:T(8,128)(2,1)S(1)} copy-done((bf16[512,512]{1,0:T(8,128)(2,1)S(1)}, bf16[512,512]{1,0:T(8,128)(2,1)}, u32[]{:S(2)}) %copy-start.1) | copy-done | bytes 524312
  24.8 0.9 %copy-done.3 = bf16[64,640]{1,0:T(8,128)(2,1)S(1)} copy-done((bf16[64,640]{1,0:T(8,128)(2,1)S(1)}, bf16[64,640]{1,0:T(8,128)(2,1)}, u32[]{:S(2)}) %copy-start.3) | copy-done | bytes 81944
  25.6 0.9 %copy-done.4 = bf16[64,640]{1,0:T(8,128)(2,1)S(1)} copy-done((bf16[64,640]{1,0:T(8,128)(2,1)S(1)}, bf16[64,640]{1,0:T(8,128)(2,1)}, u32[]{:S(2)}) %copy-start.4) | copy-done | bytes 81944
  26.5 0.4 shard_map.111
  27.0 0.4 shard_map.112
  27.5 3.1 %shard_map.113 = (bf16[4,512,256]{2,1,0:T(8,128)(2,1)S(1)}, bf16[4,512,128]{2,1,0:T(8,128)(2,1)S(1)}, f32[4,512,512]{2,1,0:T(8,128)S(1)}, f32[4,512,512]{2,1,0:T(8,128)S(1)}, f32[16,512]{1,0:T(8,128)S(1)}) custom-call(s32[3]{0:T(128)S(1)} %pad_add_fusion.where, bf16[1296,128]{1,0:T(8,128)(2,1)S(1)} %copy-done.2, ...), custom_call_target="tpu_custom_call" | custom-call | flops 1000000000 | bytes 8388608 | tf_op jit(solution)/shard_map/pallas_call | solution.py:166
  30.6 0.9 %collective-permute-start.12 = (f32[16,512]{1,0:T(8,128)S(1)}, f32[16,512]{1,0:T(8,128)S(1)}, u32[]{:S(2)}, u32[]{:S(2)}) collective-permute-start(f32[16,512]{1,0:T(8,128)S(1)} %get-tuple-element.53.t0), channel_id=1, source_target_pairs={{0,3},{1,0},{2,1},{3,2},{4,7},{5,4},{6,5},{7,6},{8,11},{9,8},{10,9... | collective-permute-start | bytes 98312 | tf_op jit(solution)/shard_map/ppermute | solution.py:30
  31.5 0.9 %collective-permute-start.10 = (f32[16,512]{1,0:T(8,128)S(1)}, f32[16,512]{1,0:T(8,128)S(1)}, u32[]{:S(2)}, u32[]{:S(2)}) collective-permute-start(f32[16,512]{1,0:T(8,128)S(1)} %get-tuple-element.53.t0), channel_id=1, source_target_pairs={{0,1},{1,2},{2,3},{3,0},{4,5},{5,6},{6,7},{7,4},{8,9},{9,10},{10,1... | collective-permute-start | bytes 98312 | tf_op jit(solution)/shard_map/ppermute | solution.py:30
  32.4 1.1 %collective-permute-done.12.t3 = f32[16,512]{1,0:T(8,128)S(1)} collective-permute-done((f32[16,512]{1,0:T(8,128)S(1)}, f32[16,512]{1,0:T(8,128)S(1)}, u32[]{:S(2)}, u32[]{:S(2)}) %collective-permute-start.12) | collective-permute-done | bytes 32800 | tf_op jit(solution)/shard_map/ppermute | solution.py:30
  33.5 2.4 %collective-permute-done.11.t2 = f32[16,512]{1,0:T(8,128)S(1)} collective-permute-done((f32[16,512]{1,0:T(8,128)S(1)}, f32[16,512]{1,0:T(8,128)S(1)}, u32[]{:S(2)}, u32[]{:S(2)}) %collective-permute-start.11) | collective-permute-done | bytes 32800 | tf_op jit(solution)/shard_map/ppermute | solution.py:30
  35.8 0.3 collective-permute-done.10.t1
  36.1 3.0 %shard_map.114 = (bf16[4,128,512]{2,1,0:T(8,128)(2,1)S(1)}, bf16[4,128,512]{2,1,0:T(8,128)(2,1)S(1)}, bf16[4,512,512]{2,1,0:T(8,128)(2,1)S(1)}, bf16[2,512,512]{...) custom-call(s32[3]{0:T(128)S(1)} %pad_add_fusion.where, ...), custom_call_target="tpu_custom_call" | custom-call | flops 1500000000 | bytes 10485760 | tf_op jit(solution)/shard_map/pallas_call | solution.py:215
  39.1 5.4 %collective-permute-start.19 = (bf16[4,128,512]{2,1,0:T(8,128)(2,1)S(1)}, bf16[4,128,512]{2,1,0:T(8,128)(2,1)S(1)}, u32[]{:S(2)}, u32[]{:S(2)}) collective-permute-start(bf16[4,128,512]{2,1,0:T(8,128)(2,1)S(1)} %get-tuple-element.74), channel_id=1, source_target_pairs={{0,32},{32,0},{64,96},{96,64},{128,160},{160,128},{192,224},{224,1... | collective-permute-start | bytes 1572872 | tf_op jit(solution)/shard_map/ppermute | solution.py:43
  44.5 3.0 %collective-permute-start.16 = (bf16[128,640]{1,0:T(8,128)(2,1)S(1)}, bf16[128,640]{1,0:T(8,128)(2,1)S(1)}, u32[]{:S(2)}, u32[]{:S(2)}) collective-permute-start(bf16[128,640]{1,0:T(8,128)(2,1)S(1)} %get-tuple-element.69), channel_id=1, source_target_pairs={{0,28},{1,29},{2,30},{3,31},{4,0},{5,1},{6,2},{7,3},{8,4},{9,5},{1... | collective-permute-start | bytes 491528 | tf_op jit(solution)/shard_map/ppermute | solution.py:34
  47.5 0.7 shard_map.120
  48.1 0.1 collective-permute-start.20
  48.2 2.3 %collective-permute-start.21 = (bf16[128,512]{1,0:T(8,128)(2,1)S(1)}, bf16[128,512]{1,0:T(8,128)(2,1)S(1)}, u32[]{:S(2)}, u32[]{:S(2)}) collective-permute-start(bf16[128,512]{1,0:T(8,128)(2,1)S(1)} %get-tuple-element.77), channel_id=1, source_target_pairs={{0,2},{1,3},{2,0},{3,1},{4,6},{5,7},{6,4},{7,5},{8,10},{9,11},{10,... | collective-permute-start | bytes 393224 | tf_op jit(solution)/shard_map/ppermute | solution.py:30
  50.6 1.4 %collective-permute-start.22 = (bf16[128,512]{1,0:T(8,128)(2,1)S(1)}, bf16[128,512]{1,0:T(8,128)(2,1)S(1)}, u32[]{:S(2)}, u32[]{:S(2)}) collective-permute-start(bf16[128,512]{1,0:T(8,128)(2,1)S(1)} %get-tuple-element.78), channel_id=1, source_target_pairs={{0,3},{1,0},{2,1},{3,2},{4,7},{5,4},{6,5},{7,6},{8,11},{9,8},{10,9... | collective-permute-start | bytes 393224 | tf_op jit(solution)/shard_map/ppermute | solution.py:30
  52.0 1.8 %shard_map.115 = (bf16[128,640]{1,0:T(8,128)(2,1)S(1)}, bf16[128,640]{1,0:T(8,128)(2,1)S(1)}, bf16[128,640]{1,0:T(8,128)(2,1)S(1)}, bf16[128,768]{1,0:T(8,128)(2...) custom-call(s32[3]{0:T(128)S(1)} %pad_add_fusion.where, ...), custom_call_target="tpu_custom_call" | custom-call | flops 1500000000 | bytes 10485760 | tf_op jit(solution)/shard_map/pallas_call | solution.py:245
  53.9 1.6 %collective-permute-start.17 = (bf16[128,640]{1,0:T(8,128)(2,1)S(1)}, bf16[128,640]{1,0:T(8,128)(2,1)S(1)}, u32[]{:S(2)}, u32[]{:S(2)}) collective-permute-start(bf16[128,640]{1,0:T(8,128)(2,1)S(1)} %shard_map.117), channel_id=1, source_target_pairs={{0,28},{1,29},{2,30},{3,31},{4,0},{5,1},{6,2},{7,3},{8,4},{9,5},{1... | collective-permute-start | bytes 491528 | tf_op jit(solution)/shard_map/ppermute | solution.py:34
  55.5 1.2 %collective-permute-done.21.refs_2_ = bf16[128,512]{1,0:T(8,128)(2,1)S(1)} collective-permute-done((bf16[128,512]{1,0:T(8,128)(2,1)S(1)}, bf16[128,512]{1,0:T(8,128)(2,1)S(1)}, u32[]{:S(2)}, u32[]{:S(2)}) %collective-permute-start.21) | collective-permute-done | bytes 131104 | tf_op jit(solution)/shard_map/ppermute | solution.py:30
  56.7 0.5 collective-permute-done.22.refs_3_
  57.2 0.7 shard_map.121
  58.0 5.4 %all-to-all-start = ((bf16[8,16,512]{2,1,0:T(8,128)(2,1)}), bf16[8,16,512]{2,1,0:T(8,128)(2,1)S(1)}, u32[]{:S(2)}, u32[]{:S(2)}) async-start(bf16[8,16,512]{2,1,0:T(8,128)(2,1)} %bitcast.12), calls=%async_computation | async-start | bytes 262144 | tf_op jit(solution)/shard_map/all_to_all | solution.py:311
  63.3 2.1 %collective-permute-start.13 = (bf16[128,768]{1,0:T(8,128)(2,1)S(1)}, bf16[128,768]{1,0:T(8,128)(2,1)S(1)}, u32[]{:S(2)}, u32[]{:S(2)}) collective-permute-start(bf16[128,768]{1,0:T(8,128)(2,1)S(1)} %get-tuple-element.64), channel_id=1, source_target_pairs={{0,1},{1,2},{2,3},{3,0},{4,5},{5,6},{6,7},{7,4},{8,9},{9,10},{10,1... | collective-permute-start | bytes 589832 | tf_op jit(solution)/shard_map/ppermute | solution.py:30
  65.4 2.4 %collective-permute-start.14 = (bf16[128,768]{1,0:T(8,128)(2,1)S(1)}, bf16[128,768]{1,0:T(8,128)(2,1)S(1)}, u32[]{:S(2)}, u32[]{:S(2)}) collective-permute-start(bf16[128,768]{1,0:T(8,128)(2,1)S(1)} %get-tuple-element.65), channel_id=1, source_target_pairs={{0,2},{1,3},{2,0},{3,1},{4,6},{5,7},{6,4},{7,5},{8,10},{9,11},{10,... | collective-permute-start | bytes 589832 | tf_op jit(solution)/shard_map/ppermute | solution.py:30
  67.8 0.1 collective-permute-start.15
  67.9 2.7 %collective-permute-start.18 = (bf16[128,640]{1,0:T(8,128)(2,1)S(1)}, bf16[128,640]{1,0:T(8,128)(2,1)S(1)}, u32[]{:S(2)}, u32[]{:S(2)}) collective-permute-start(bf16[128,640]{1,0:T(8,128)(2,1)S(1)} %shard_map.118), channel_id=1, source_target_pairs={{0,28},{1,29},{2,30},{3,31},{4,0},{5,1},{6,2},{7,3},{8,4},{9,5},{1... | collective-permute-start | bytes 491528 | tf_op jit(solution)/shard_map/ppermute | solution.py:34
  70.6 0.6 all-to-all-done
  71.3 1.4 %collective-permute-start.23 = (bf16[16,512]{1,0:T(8,128)(2,1)S(1)}, bf16[16,512]{1,0:T(8,128)(2,1)S(1)}, u32[]{:S(2)}, u32[]{:S(2)}) collective-permute-start(bf16[16,512]{1,0:T(8,128)(2,1)S(1)} %shard_map.122.refs_0_), channel_id=1, source_target_pairs={{0,64},{32,96},{64,0},{96,32},{128,192},{160,224},{192,128},{224,1... | collective-permute-start | bytes 49160 | tf_op jit(solution)/shard_map/ppermute | solution.py:39
  72.7 1.6 %collective-permute-done.23.refs_1_ = bf16[16,512]{1,0:T(8,128)(2,1)S(1)} collective-permute-done((bf16[16,512]{1,0:T(8,128)(2,1)S(1)}, bf16[16,512]{1,0:T(8,128)(2,1)S(1)}, u32[]{:S(2)}, u32[]{:S(2)}) %collective-permute-start.23) | collective-permute-done | bytes 16416 | tf_op jit(solution)/shard_map/ppermute | solution.py:39
  74.3 2.7 %collective-permute-start.24 = (bf16[16,512]{1,0:T(8,128)(2,1)S(1)}, bf16[16,512]{1,0:T(8,128)(2,1)S(1)}, u32[]{:S(2)}, u32[]{:S(2)}) collective-permute-start(bf16[16,512]{1,0:T(8,128)(2,1)S(1)} %shard_map.123.refs_0_), channel_id=1, source_target_pairs={{0,192},{32,224},{64,128},{96,160},{128,64},{160,96},{192,0},{224,... | collective-permute-start | bytes 49160 | tf_op jit(solution)/shard_map/ppermute | solution.py:39
  77.0 1.1 %collective-permute-done.24.refs_1_ = bf16[16,512]{1,0:T(8,128)(2,1)S(1)} collective-permute-done((bf16[16,512]{1,0:T(8,128)(2,1)S(1)}, bf16[16,512]{1,0:T(8,128)(2,1)S(1)}, u32[]{:S(2)}, u32[]{:S(2)}) %collective-permute-start.24) | collective-permute-done | bytes 16416 | tf_op jit(solution)/shard_map/ppermute | solution.py:39
  78.1 4.9 %collective-permute-start.25 = (f32[16,512]{1,0:T(8,128)S(1)}, f32[16,512]{1,0:T(8,128)S(1)}, u32[]{:S(2)}, u32[]{:S(2)}) collective-permute-start(f32[16,512]{1,0:T(8,128)S(1)} %shard_map.124), channel_id=1, source_target_pairs={{0,32},{32,0},{64,96},{96,64},{128,160},{160,128},{192,224},{224,1... | collective-permute-start | bytes 98312 | tf_op jit(solution)/shard_map/ppermute | solution.py:43
  83.0 0.7 shard_map.116
  83.8 0.8 shard_map.119
  84.5 0.6 broadcast_select_fusion
  (35 shorter events, 0.4 us)
Async XLA Ops:
  2.6 24.9 %copy-start.2 = (bf16[1296,128]{1,0:T(8,128)(2,1)S(1)}, bf16[1296,128]{1,0:T(8,128)(2,1)}, u32[]{:S(2)}) copy-start(bf16[1296,128]{1,0:T(8,128)(2,1)} %get-tuple-element.42.q0) | copy-start | bytes 995332
  2.6 17.2 %collective-permute-start.1 = (bf16[1296,128]{1,0:T(8,128)(2,1)}, bf16[1296,128]{1,0:T(8,128)(2,1)S(1)}, u32[]{:S(2)}, u32[]{:S(2)}) collective-permute-start(bf16[1296,128]{1,0:T(8,128)(2,1)} %get-tuple-element.42.q0), channel_id=1, source_target_pairs={{0,1},{1,2},{2,3},{3,0},{4,5},{5,6},{6,7},{7,4},{8,9},{9,10},{10,1... | collective-permute-start | bytes 995336 | tf_op jit(solution)/shard_map/ppermute | solution.py:30
  4.7 15.2 %collective-permute-start = (bf16[1296,128]{1,0:T(8,128)(2,1)}, bf16[1296,128]{1,0:T(8,128)(2,1)S(1)}, u32[]{:S(2)}, u32[]{:S(2)}) collective-permute-start(bf16[1296,128]{1,0:T(8,128)(2,1)} %get-tuple-element.42.q0), channel_id=1, source_target_pairs={{0,3},{1,0},{2,1},{3,2},{4,7},{5,4},{6,5},{7,6},{8,11},{9,8},{10,9... | collective-permute-start | bytes 995336 | tf_op jit(solution)/shard_map/ppermute | solution.py:30
  6.0 8.0 %collective-permute-start.4 = (bf16[64,640]{1,0:T(8,128)(2,1)}, bf16[64,640]{1,0:T(8,128)(2,1)S(1)}, u32[]{:S(2)}, u32[]{:S(2)}) collective-permute-start(bf16[64,640]{1,0:T(8,128)(2,1)} %get-tuple-element.43.a0), channel_id=1, source_target_pairs={{0,4},{1,5},{2,6},{3,7},{4,8},{5,9},{6,10},{7,11},{8,12},{9,13},{1... | collective-permute-start | bytes 245768 | tf_op jit(solution)/shard_map/ppermute | solution.py:34
  7.8 7.4 %collective-permute-start.5 = (bf16[64,640]{1,0:T(8,128)(2,1)}, bf16[64,640]{1,0:T(8,128)(2,1)S(1)}, u32[]{:S(2)}, u32[]{:S(2)}) collective-permute-start(bf16[64,640]{1,0:T(8,128)(2,1)} %get-tuple-element.44.b0), channel_id=1, source_target_pairs={{0,4},{1,5},{2,6},{3,7},{4,8},{5,9},{6,10},{7,11},{8,12},{9,13},{1... | collective-permute-start | bytes 245768 | tf_op jit(solution)/shard_map/ppermute | solution.py:34
  14.1 4.5 %collective-permute-start.6 = (bf16[64,640]{1,0:T(8,128)(2,1)S(1)}, bf16[64,640]{1,0:T(8,128)(2,1)S(1)}, u32[]{:S(2)}, u32[]{:S(2)}) collective-permute-start(bf16[64,640]{1,0:T(8,128)(2,1)S(1)} %collective-permute-done.4.a1), channel_id=1, source_target_pairs={{0,4},{1,5},{2,6},{3,7},{4,8},{5,9},{6,10},{7,11},{8,12},{9,13},{1... | collective-permute-start | bytes 245768 | tf_op jit(solution)/shard_map/ppermute | solution.py:34
  15.2 4.5 %collective-permute-start.8 = (bf16[64,640]{1,0:T(8,128)(2,1)S(1)}, bf16[64,640]{1,0:T(8,128)(2,1)S(1)}, u32[]{:S(2)}, u32[]{:S(2)}) collective-permute-start(bf16[64,640]{1,0:T(8,128)(2,1)S(1)} %collective-permute-done.5.b1), channel_id=1, source_target_pairs={{0,4},{1,5},{2,6},{3,7},{4,8},{5,9},{6,10},{7,11},{8,12},{9,13},{1... | collective-permute-start | bytes 245768 | tf_op jit(solution)/shard_map/ppermute | solution.py:34
  18.6 8.4 %collective-permute-start.7 = (bf16[64,640]{1,0:T(8,128)(2,1)S(1)}, bf16[64,640]{1,0:T(8,128)(2,1)S(1)}, u32[]{:S(2)}, u32[]{:S(2)}) collective-permute-start(bf16[64,640]{1,0:T(8,128)(2,1)S(1)} %collective-permute-done.6.a0), channel_id=1, source_target_pairs={{0,4},{1,5},{2,6},{3,7},{4,8},{5,9},{6,10},{7,11},{8,12},{9,13},{1... | collective-permute-start | bytes 245768 | tf_op jit(solution)/shard_map/ppermute | solution.py:34
  19.7 7.3 %collective-permute-start.9 = (bf16[64,640]{1,0:T(8,128)(2,1)S(1)}, bf16[64,640]{1,0:T(8,128)(2,1)S(1)}, u32[]{:S(2)}, u32[]{:S(2)}) collective-permute-start(bf16[64,640]{1,0:T(8,128)(2,1)S(1)} %collective-permute-done.8.b0), channel_id=1, source_target_pairs={{0,4},{1,5},{2,6},{3,7},{4,8},{5,9},{6,10},{7,11},{8,12},{9,13},{1... | collective-permute-start | bytes 245768 | tf_op jit(solution)/shard_map/ppermute | solution.py:34
  19.7 7.7 %collective-permute-start.2 = (bf16[640,128]{1,0:T(8,128)(2,1)S(1)}, bf16[640,128]{1,0:T(8,128)(2,1)S(1)}, u32[]{:S(2)}, u32[]{:S(2)}) collective-permute-start(bf16[640,128]{1,0:T(8,128)(2,1)S(1)} %slice.8), channel_id=1, source_target_pairs={{0,1},{1,2},{2,3},{3,0},{4,5},{5,6},{6,7},{7,4},{8,9},{9,10},{10,1... | collective-permute-start | bytes 491528 | tf_op jit(solution)/shard_map/ppermute | solution.py:30
  19.9 7.6 %collective-permute-start.3 = (bf16[656,128]{1,0:T(8,128)(2,1)S(1)}, bf16[656,128]{1,0:T(8,128)(2,1)S(1)}, u32[]{:S(2)}, u32[]{:S(2)}) collective-permute-start(bf16[656,128]{1,0:T(8,128)(2,1)S(1)} %slice.9), channel_id=1, source_target_pairs={{0,3},{1,0},{2,1},{3,2},{4,7},{5,4},{6,5},{7,6},{8,11},{9,8},{10,9... | collective-permute-start | bytes 503816 | tf_op jit(solution)/shard_map/ppermute | solution.py:30
  22.7 1.0 %copy-start = (bf16[512,512]{1,0:T(8,128)(2,1)S(1)}, bf16[512,512]{1,0:T(8,128)(2,1)}, u32[]{:S(2)}) copy-start(bf16[512,512]{1,0:T(8,128)(2,1)} %wk.1) | copy-start | bytes 1572868
  23.7 1.0 %copy-start.1 = (bf16[512,512]{1,0:T(8,128)(2,1)S(1)}, bf16[512,512]{1,0:T(8,128)(2,1)}, u32[]{:S(2)}) copy-start(bf16[512,512]{1,0:T(8,128)(2,1)} %wv.1) | copy-start | bytes 1572868
  24.8 0.9 %copy-start.3 = (bf16[64,640]{1,0:T(8,128)(2,1)S(1)}, bf16[64,640]{1,0:T(8,128)(2,1)}, u32[]{:S(2)}) copy-start(bf16[64,640]{1,0:T(8,128)(2,1)} %get-tuple-element.43.a0) | copy-start | bytes 245764
  25.6 0.9 %copy-start.4 = (bf16[64,640]{1,0:T(8,128)(2,1)S(1)}, bf16[64,640]{1,0:T(8,128)(2,1)}, u32[]{:S(2)}) copy-start(bf16[64,640]{1,0:T(8,128)(2,1)} %get-tuple-element.44.b0) | copy-start | bytes 245764
  30.6 2.8 %collective-permute-start.12 = (f32[16,512]{1,0:T(8,128)S(1)}, f32[16,512]{1,0:T(8,128)S(1)}, u32[]{:S(2)}, u32[]{:S(2)}) collective-permute-start(f32[16,512]{1,0:T(8,128)S(1)} %get-tuple-element.53.t0), channel_id=1, source_target_pairs={{0,3},{1,0},{2,1},{3,2},{4,7},{5,4},{6,5},{7,6},{8,11},{9,8},{10,9... | collective-permute-start | bytes 98312 | tf_op jit(solution)/shard_map/ppermute | solution.py:30
  31.5 4.3 %collective-permute-start.11 = (f32[16,512]{1,0:T(8,128)S(1)}, f32[16,512]{1,0:T(8,128)S(1)}, u32[]{:S(2)}, u32[]{:S(2)}) collective-permute-start(f32[16,512]{1,0:T(8,128)S(1)} %get-tuple-element.53.t0), channel_id=1, source_target_pairs={{0,2},{1,3},{2,0},{3,1},{4,6},{5,7},{6,4},{7,5},{8,10},{9,11},{10,... | collective-permute-start | bytes 98312 | tf_op jit(solution)/shard_map/ppermute | solution.py:30
  31.5 4.6 %collective-permute-start.10 = (f32[16,512]{1,0:T(8,128)S(1)}, f32[16,512]{1,0:T(8,128)S(1)}, u32[]{:S(2)}, u32[]{:S(2)}) collective-permute-start(f32[16,512]{1,0:T(8,128)S(1)} %get-tuple-element.53.t0), channel_id=1, source_target_pairs={{0,1},{1,2},{2,3},{3,0},{4,5},{5,6},{6,7},{7,4},{8,9},{9,10},{10,1... | collective-permute-start | bytes 98312 | tf_op jit(solution)/shard_map/ppermute | solution.py:30
  39.1 8.3 %collective-permute-start.19 = (bf16[4,128,512]{2,1,0:T(8,128)(2,1)S(1)}, bf16[4,128,512]{2,1,0:T(8,128)(2,1)S(1)}, u32[]{:S(2)}, u32[]{:S(2)}) collective-permute-start(bf16[4,128,512]{2,1,0:T(8,128)(2,1)S(1)} %get-tuple-element.74), channel_id=1, source_target_pairs={{0,32},{32,0},{64,96},{96,64},{128,160},{160,128},{192,224},{224,1... | collective-permute-start | bytes 1572872 | tf_op jit(solution)/shard_map/ppermute | solution.py:43
  44.5 9.3 %collective-permute-start.16 = (bf16[128,640]{1,0:T(8,128)(2,1)S(1)}, bf16[128,640]{1,0:T(8,128)(2,1)S(1)}, u32[]{:S(2)}, u32[]{:S(2)}) collective-permute-start(bf16[128,640]{1,0:T(8,128)(2,1)S(1)} %get-tuple-element.69), channel_id=1, source_target_pairs={{0,28},{1,29},{2,30},{3,31},{4,0},{5,1},{6,2},{7,3},{8,4},{9,5},{1... | collective-permute-start | bytes 491528 | tf_op jit(solution)/shard_map/ppermute | solution.py:34
  48.1 7.3 %collective-permute-start.20 = (bf16[128,512]{1,0:T(8,128)(2,1)S(1)}, bf16[128,512]{1,0:T(8,128)(2,1)S(1)}, u32[]{:S(2)}, u32[]{:S(2)}) collective-permute-start(bf16[128,512]{1,0:T(8,128)(2,1)S(1)} %get-tuple-element.76), channel_id=1, source_target_pairs={{0,1},{1,2},{2,3},{3,0},{4,5},{5,6},{6,7},{7,4},{8,9},{9,10},{10,1... | collective-permute-start | bytes 393224 | tf_op jit(solution)/shard_map/ppermute | solution.py:30
  48.2 8.5 %collective-permute-start.21 = (bf16[128,512]{1,0:T(8,128)(2,1)S(1)}, bf16[128,512]{1,0:T(8,128)(2,1)S(1)}, u32[]{:S(2)}, u32[]{:S(2)}) collective-permute-start(bf16[128,512]{1,0:T(8,128)(2,1)S(1)} %get-tuple-element.77), channel_id=1, source_target_pairs={{0,2},{1,3},{2,0},{3,1},{4,6},{5,7},{6,4},{7,5},{8,10},{9,11},{10,... | collective-permute-start | bytes 393224 | tf_op jit(solution)/shard_map/ppermute | solution.py:30
  50.6 6.6 %collective-permute-start.22 = (bf16[128,512]{1,0:T(8,128)(2,1)S(1)}, bf16[128,512]{1,0:T(8,128)(2,1)S(1)}, u32[]{:S(2)}, u32[]{:S(2)}) collective-permute-start(bf16[128,512]{1,0:T(8,128)(2,1)S(1)} %get-tuple-element.78), channel_id=1, source_target_pairs={{0,3},{1,0},{2,1},{3,2},{4,7},{5,4},{6,5},{7,6},{8,11},{9,8},{10,9... | collective-permute-start | bytes 393224 | tf_op jit(solution)/shard_map/ppermute | solution.py:30
  53.9 14.0 %collective-permute-start.17 = (bf16[128,640]{1,0:T(8,128)(2,1)S(1)}, bf16[128,640]{1,0:T(8,128)(2,1)S(1)}, u32[]{:S(2)}, u32[]{:S(2)}) collective-permute-start(bf16[128,640]{1,0:T(8,128)(2,1)S(1)} %shard_map.117), channel_id=1, source_target_pairs={{0,28},{1,29},{2,30},{3,31},{4,0},{5,1},{6,2},{7,3},{8,4},{9,5},{1... | collective-permute-start | bytes 491528 | tf_op jit(solution)/shard_map/ppermute | solution.py:34
  58.0 13.3 %all-to-all-start = ((bf16[8,16,512]{2,1,0:T(8,128)(2,1)}), bf16[8,16,512]{2,1,0:T(8,128)(2,1)S(1)}, u32[]{:S(2)}, u32[]{:S(2)}) async-start(bf16[8,16,512]{2,1,0:T(8,128)(2,1)} %bitcast.12), calls=%async_computation | async-start | bytes 262144 | tf_op jit(solution)/shard_map/all_to_all | solution.py:311
  63.3 19.7 %collective-permute-start.13 = (bf16[128,768]{1,0:T(8,128)(2,1)S(1)}, bf16[128,768]{1,0:T(8,128)(2,1)S(1)}, u32[]{:S(2)}, u32[]{:S(2)}) collective-permute-start(bf16[128,768]{1,0:T(8,128)(2,1)S(1)} %get-tuple-element.64), channel_id=1, source_target_pairs={{0,1},{1,2},{2,3},{3,0},{4,5},{5,6},{6,7},{7,4},{8,9},{9,10},{10,1... | collective-permute-start | bytes 589832 | tf_op jit(solution)/shard_map/ppermute | solution.py:30
  65.4 17.6 %collective-permute-start.14 = (bf16[128,768]{1,0:T(8,128)(2,1)S(1)}, bf16[128,768]{1,0:T(8,128)(2,1)S(1)}, u32[]{:S(2)}, u32[]{:S(2)}) collective-permute-start(bf16[128,768]{1,0:T(8,128)(2,1)S(1)} %get-tuple-element.65), channel_id=1, source_target_pairs={{0,2},{1,3},{2,0},{3,1},{4,6},{5,7},{6,4},{7,5},{8,10},{9,11},{10,... | collective-permute-start | bytes 589832 | tf_op jit(solution)/shard_map/ppermute | solution.py:30
  67.8 15.2 %collective-permute-start.15 = (bf16[128,768]{1,0:T(8,128)(2,1)S(1)}, bf16[128,768]{1,0:T(8,128)(2,1)S(1)}, u32[]{:S(2)}, u32[]{:S(2)}) collective-permute-start(bf16[128,768]{1,0:T(8,128)(2,1)S(1)} %get-tuple-element.66), channel_id=1, source_target_pairs={{0,3},{1,0},{2,1},{3,2},{4,7},{5,4},{6,5},{7,6},{8,11},{9,8},{10,9... | collective-permute-start | bytes 589832 | tf_op jit(solution)/shard_map/ppermute | solution.py:30
  67.9 15.8 %collective-permute-start.18 = (bf16[128,640]{1,0:T(8,128)(2,1)S(1)}, bf16[128,640]{1,0:T(8,128)(2,1)S(1)}, u32[]{:S(2)}, u32[]{:S(2)}) collective-permute-start(bf16[128,640]{1,0:T(8,128)(2,1)S(1)} %shard_map.118), channel_id=1, source_target_pairs={{0,28},{1,29},{2,30},{3,31},{4,0},{5,1},{6,2},{7,3},{8,4},{9,5},{1... | collective-permute-start | bytes 491528 | tf_op jit(solution)/shard_map/ppermute | solution.py:34
  71.3 3.0 %collective-permute-start.23 = (bf16[16,512]{1,0:T(8,128)(2,1)S(1)}, bf16[16,512]{1,0:T(8,128)(2,1)S(1)}, u32[]{:S(2)}, u32[]{:S(2)}) collective-permute-start(bf16[16,512]{1,0:T(8,128)(2,1)S(1)} %shard_map.122.refs_0_), channel_id=1, source_target_pairs={{0,64},{32,96},{64,0},{96,32},{128,192},{160,224},{192,128},{224,1... | collective-permute-start | bytes 49160 | tf_op jit(solution)/shard_map/ppermute | solution.py:39
  74.3 3.9 %collective-permute-start.24 = (bf16[16,512]{1,0:T(8,128)(2,1)S(1)}, bf16[16,512]{1,0:T(8,128)(2,1)S(1)}, u32[]{:S(2)}, u32[]{:S(2)}) collective-permute-start(bf16[16,512]{1,0:T(8,128)(2,1)S(1)} %shard_map.123.refs_0_), channel_id=1, source_target_pairs={{0,192},{32,224},{64,128},{96,160},{128,64},{160,96},{192,0},{224,... | collective-permute-start | bytes 49160 | tf_op jit(solution)/shard_map/ppermute | solution.py:39
  78.1 6.4 %collective-permute-start.25 = (f32[16,512]{1,0:T(8,128)S(1)}, f32[16,512]{1,0:T(8,128)S(1)}, u32[]{:S(2)}, u32[]{:S(2)}) collective-permute-start(f32[16,512]{1,0:T(8,128)S(1)} %shard_map.124), channel_id=1, source_target_pairs={{0,32},{32,0},{64,96},{96,64},{128,160},{160,128},{192,224},{224,1... | collective-permute-start | bytes 98312 | tf_op jit(solution)/shard_map/ppermute | solution.py:43

commit v3 on v2

--- a/solution.py
+++ b/solution.py
@@ -14,9 +14,10 @@
 QROWS = X * ROWS
 KROWS = REACH * ROWS
 HALF = KROWS // 2
+ORDER = (1, 2, 0, 3)
 SCALE = (HEAD + ROPE) ** -0.5
 NEG = -1e30
-CUT = 640
+CUTS = (64, 64)
 PACK_VMEM = 60.5
 BF, F32 = jnp.bfloat16, jnp.float32
 NT = (((1,), (1,)), ((), ()))
@@ -55,7 +56,8 @@
     )
 
 
-def pack_kernel(nope, rope, grad, kv_t, ids, q_out, ca_out, cb_out, kv_scr, ids_scr, sems):
+def pack_kernel(nope, rope, grad, kv_t, ids, q_out, *rest):
+    *c_outs, kv_scr, ids_scr, sems = rest
     copies = [pltpu.make_async_copy(kv_t, kv_scr, sems.at[0]), pltpu.make_async_copy(ids, ids_scr, sems.at[1])]
     for n, (source, parts) in enumerate(((nope, 4), (grad, 4), (rope, 2))):
         for i in range(parts):
@@ -69,61 +71,66 @@
     marks = jnp.broadcast_to(ids_scr[...].astype(F32), (128, 128)).astype(BF)
     q_out[1280:1296, :] = marks[:16]
     rows = jnp.concatenate([kv_scr[...], marks[:64]], axis=0).T
-    ca_out[...] = rows[:64]
-    cb_out[...] = rows[64:]
+    first = 0
+    for c_out in c_outs:
+        c_out[...] = rows[first:first + c_out.shape[0]]
+        first += c_out.shape[0]
     for copy in copies[2:]:
         copy.wait()
 
 
 def pack(nope, rope, grad, kv_t, ids):
-    half = jax.ShapeDtypeStruct((64, 640), BF)
+    pieces = [jax.ShapeDtypeStruct((rows, 640), BF) for rows in CUTS]
     return call(
-        pack_kernel, (jax.ShapeDtypeStruct((1296, 128), BF), half, half), 0, 0, 5,
+        pack_kernel, (jax.ShapeDtypeStruct((1296, 128), BF), *pieces), 0, 0, 5,
         scratch=[pltpu.VMEM((576, 128), BF), pltpu.VMEM((1, 128), jnp.int32), pltpu.SemaphoreType.DMA((12,))],
         nbytes=1 << 20, vmem=PACK_VMEM)(nope, rope, grad, kv_t, ids)
 
 
-def keys_kernel(a0, a1, b0, b1, wk, wv, kc, vs, latents, marks, wk_out=None, wv_out=None):
-    lane = lax.broadcasted_iota(jnp.int32, (64, 128), 1)
-    for n, c in enumerate((a0, b0, a1, b1)):
-        at = slice(n * 64, n * 64 + 64)
+def open_kernel(*refs):
+    pieces, (latents, ropes, marks) = refs[:-3], refs[-3:]
+    first = 0
+    for c in pieces:
+        at = slice(first, first + c.shape[0])
+        first += c.shape[0]
         latents[at, :] = c[:, :512]
         tail = c[:, 512:640].astype(F32)
         marks[at, :] = tail
-        even = jnp.where(lane < 64, tail, 0.0)
-        odd = pltpu.roll(even, 64, 1)
-        for h in range(HEADS):
-            kc[h, at, 128:256] = (odd if h % 2 else even).astype(BF)
+        even = jnp.where(lax.broadcasted_iota(jnp.int32, tail.shape, 1) < 64, tail, 0.0)
+        ropes[0, at, :] = even.astype(BF)
+        ropes[1, at, :] = pltpu.roll(even, 64, 1).astype(BF)
+
+
+def keys_kernel(latents, ropes, wk, wv, kc, vs, *weights):
     keys = jnp.dot(latents[...], wk[...], preferred_element_type=F32).astype(BF)
     values = jnp.dot(latents[...], wv[...], preferred_element_type=F32).astype(BF)
     for h in range(HEADS):
         kc[h, :, 0:128] = keys[:, h * 128:(h + 1) * 128]
+        kc[h, :, 128:256] = ropes[h % 2]
         vs[h, :, :] = values[:, h * 128:(h + 1) * 128]
-    if wk_out is not None:
-        wk_out[...] = wk[...]
-        wv_out[...] = wv[...]
-
-
-def run_keys(ca, cb, wk, wv, hand_on):
-    sds = jax.ShapeDtypeStruct
-    return call(
+    for out, w in zip(weights, (wk, wv)):
+        out[...] = w[...]
+
+
+def run_keys(pieces, wk, wv, hand_on):
+    sds = jax.ShapeDtypeStruct
+    latents, ropes, marks = call(
+        open_kernel, (sds((HALF, LATENT), BF), sds((2, HALF, 128), BF), sds((HALF, 128), F32)),
+        0, len(pieces), flops=1_500_000_000, nbytes=1 << 20)(*pieces)
+    kc, vs, *weights = call(
         keys_kernel,
-        (sds((4, HALF, 256), BF), sds((4, HALF, 128), BF), sds((HALF, LATENT), BF), sds((HALF, 128), F32),
-         *([sds((512, 512), BF)] * (2 if hand_on else 0))),
-        0, 6, flops=500_000_000, nbytes=2 << 20,
-    )(*ca, *cb, wk, wv)
-
-
-def stats_kernel(where, q0, q1, q2a, q2b, q3, kc0, kc1, vs0, vs1, marks0, marks1, qc, gs, es, dps, stats, bias, qid):
+        (sds((4, HALF, 256), BF), sds((4, HALF, 128), BF), *([sds((512, 512), BF)] * (2 if hand_on else 0))),
+        0, 4, flops=500_000_000, nbytes=2 << 20)(latents, ropes, wk, wv)
+    return kc, vs, latents, marks, *weights
+
+
+def stats_kernel(where, q0, q1, q2, q3, kc0, kc1, vs0, vs1, marks0, marks1, qc, gs, es, dps, stats, bias, qid):
     xi, zi = where[0], where[1]
-    for s, block in enumerate((q0, q1, (q2a, q2b), q3)):
+    for s, block in enumerate((q0, q1, q2, q3)):
         at = pl.ds(pl.multiple_of(((xi + s) & 3) * 128, 128), 128)
 
         def rows(first, count=128):
-            if s != 2:
-                return block[first:first + count, :]
-            part, start = (block[1], first - CUT) if first >= CUT else (block[0], first)
-            return part[start:start + count, :]
+            return block[first:first + count, :]
 
         for h in range(HEADS):
             qc[h, at, 0:128] = rows(h * 128)
@@ -134,7 +141,7 @@
     q_pos = zi * QROWS + lax.broadcasted_iota(jnp.int32, (128, QROWS), 1)
     for j in range(REACH):
         at = slice(j * 128, j * 128 + 128)
-        first = ((zi - j) & (Z - 1)) * QROWS + xi * 128
+        first = ((zi - ORDER[j]) & (Z - 1)) * QROWS + xi * 128
         k_pos = first + lax.broadcasted_iota(jnp.int32, (128, QROWS), 0)
         allowed = (k_pos <= q_pos) & ((marks0, marks1)[j // 2][j % 2 * 128:j % 2 * 128 + 128, 64:65] == q_marks)
         bias[at, :] = jnp.where(allowed, 0.0, NEG)
@@ -167,7 +174,7 @@
         stats_kernel,
         (sds((4, QROWS, 256), BF), sds((4, QROWS, 128), BF),
          sds((4, KROWS, QROWS), F32), sds((4, KROWS, QROWS), F32), sds((16, QROWS), F32)),
-        1, 11, scratch=[pltpu.VMEM((KROWS, QROWS), F32), pltpu.VMEM((16, QROWS), BF)],
+        1, 10, scratch=[pltpu.VMEM((KROWS, QROWS), F32), pltpu.VMEM((16, QROWS), BF)],
         flops=1_000_000_000, nbytes=8 << 20,
     )(where, *qs, *keys)
 
@@ -225,7 +232,7 @@
     near = slice(0, 3 * ROWS)
     lat = (lax.dot_general(dkv[0, near], wk[...], NT, preferred_element_type=F32)
            + lax.dot_general(dkv[1, near], wv[...], NT, preferred_element_type=F32)).astype(BF)
-    for j, d in enumerate((d0, d1, d2)):
+    for j, d in enumerate((d1, d2, d0)):
         d[:, :512] = lat[j * 128:(j + 1) * 128, :]
         d[:, 512:640] = tail[j * 128:(j + 1) * 128, :]
     for p in range(2):
@@ -282,8 +289,8 @@
     rope[...] = q[:, 512:]
 
 
-def latent_kernel(d1, d0, latent):
-    latent[...] = wide(d1, d0).astype(BF)[:, :576].T
+def latent_kernel(d2, d1, d0, latent):
+    latent[...] = wide(d2, d1, d0).astype(BF)[:, :576].T
 
 
 def body(kv_latent, q_nope, q_rope, w_key_up, w_value_up, out_grad, segment_ids):
@@ -291,15 +298,14 @@
     dp = lax.axis_index("dp")
     core = dp % 2
     where = jnp.stack([ctx % X, ctx // X, core]).astype(jnp.int32)
-    q, ca, cb = pack(q_nope[0], q_rope[0], out_grad[0], kv_latent[0].T, segment_ids)
-    ca, cb = [ca], [cb]
-    for _ in range(REACH - 1):
-        ca.append(z_shift(ca[-1], 1))
-        cb.append(z_shift(cb[-1], 1))
-    right, left = x_shift(q, -1), x_shift(q, 1)
-    qs = (q, right, x_shift(left[:CUT], 1), x_shift(right[CUT:], -1), left)
-    kc0, vs0, latents0, marks0, wk, wv = run_keys(ca[:2], cb[:2], w_key_up, w_value_up, True)
-    kc1, vs1, latents1, marks1 = run_keys(ca[2:], cb[2:], wk, wv, False)
+    q, *c = pack(q_nope[0], q_rope[0], out_grad[0], kv_latent[0].T, segment_ids)
+    c1 = [z_shift(v, 1) for v in c]
+    c2 = [z_shift(v, 1) for v in c1]
+    kc0, vs0, latents0, marks0, wk, wv = run_keys(c1 + c2, w_key_up, w_value_up, True)
+    c3 = [z_shift(v, 1) for v in c2]
+    later, _ = lax.optimization_barrier((q, c1))
+    qs = (q, x_shift(q, -1), x_shift(q, 2), x_shift(later, 1))
+    kc1, vs1, latents1, marks1 = run_keys(c + c3, wk, wv, False)
     qc, gs, es, dps, stats = run_stats(where, qs, kc0, kc1, vs0, vs1, marks0, marks1)
     ts = (stats, x_shift(stats, 1), x_shift(stats, 2), x_shift(stats, -1))
     w_keep, w_send, ds, dkv, tail, d3 = run_weight(where, ts, qc, gs, es, dps, latents0, latents1, wk, wv)
@@ -309,15 +315,16 @@
     sds = jax.ShapeDtypeStruct
     w = add_up(pieces[0], x_shift(pieces[1], 1), x_shift(pieces[2], 2), x_shift(pieces[3], -1))
     w = lax.all_to_all(w, "ctx", 0, 0, tiled=True, axis_index_groups=[[z * X + x for z in range(Z)] for x in range(X)])
+    d = add_up(z_shift(d3, -1), d2)
+    grad_latent = call(latent_kernel, sds((576, 128), BF), 0, 3, flops=1_000_000_000, nbytes=1 << 20)(
+        z_shift(d, -2), z_shift(d1, -1), d0)
+    w, grad_latent = lax.optimization_barrier((w, grad_latent))
     w = call(sum_z_kernel, sds((16, 512), BF), 0, 1, nbytes=1 << 18)(w)
     w = add_up(w, y_pair(w, False))
     w = add_up(w, y_pair(w, True), dtype=F32)
     other = core_swap(w)
     grad_key = jnp.where(core == 0, w, other)
     grad_value = jnp.where(core == 0, other, w)
-    d = add_up(z_shift(d3, -1), d2)
-    d = add_up(z_shift(d, -1), d1)
-    grad_latent = call(latent_kernel, sds((576, 128), BF), 0, 2, nbytes=1 << 20)(z_shift(d, -1), d0)
     grad_nope, grad_rope = call(query_kernel, (sds((128, 512), BF), sds((128, 256), BF)), 0, 4, nbytes=1 << 20)(
         o0, x_shift(o1, 1), x_shift(o2, 2), x_shift(o3, -1))
     return grad_nope[None], grad_rope[None], grad_latent.T[None], grad_key, grad_value

time: 85.5 us -> 81.1 us (0.949)
  local copies, waits for them, and re-layouts: 3.89 us -> 0.03 us
    unnamed x10, local copies, waits for them, and re-layouts: 3.86 us -> 0.03 us
    ppermute x9, starting transfers between devices: 10.6 us -> 13.2 us  [z_shift(): lax.ppermute(v, 'ctx', [(i, (i + s * X) % (Z * X)) for i in range(Z * X)])]
    ppermute x2, starting transfers between devices: 10.3 us -> 7.92 us  [core_swap(): return lax.ppermute(v, 'dp', [(i, i ^ 1) for i in range(2 * Y)])]
    ppermute x9, waiting for transfers between devices: 10.3 us -> 8.38 us  [z_shift(): lax.ppermute(v, 'ctx', [(i, (i + s * X) % (Z * X)) for i in range(Z * X)])]
    all_to_all x1, waiting for transfers between devices: 0.64 us -> 2.56 us  [body(): lax.all_to_all(w, 'ctx', 0, 0, tiled=True, axis_index_groups=[[z * X + x...]
    ppermute x13 -> x12, waiting for transfers between devices: 5.53 us -> 4.93 us  [x_shift(): lax.ppermute(v, 'ctx', [(i, i // X * X + (i % X + s) % X) for i in range(...]
    pallas_call x4 -> x6, Pallas kernels: 3.56 us -> 3.86 us  [the longest x1 2 us: pack(): call(pack_kernel, (jax.ShapeDtypeStruct((1296, 128), BF), *pieces), 0, 0,...]
    ppermute x13 -> x12, starting transfers between devices: 16.4 us -> 16.2 us  [x_shift(): lax.ppermute(v, 'ctx', [(i, i // X * X + (i % X + s) % X) for i in range(...]
  transfers between devices with their start and end apart: 27 -> 26, of which waited for: 12 -> 14; matrix products, arithmetic and copies ran while one was open for 0% -> 0% of each run, Pallas kernels for 7% -> 7%
where the time goes in v3:
time: 81.1 us; the launch traced here: 80.9 us
  starting transfers between devices  47 us (58%)
  waiting for transfers between devices  18.4 us (23%)
  Pallas kernels  14 us (17%)
    ppermute x12, starting transfers between devices, x_shift(): lax.ppermute(v, 'ctx', [(i, i // X * X + (i % X + s) % X) for i in range(...  16.2 us
    ppermute x9, starting transfers between devices, z_shift(): lax.ppermute(v, 'ctx', [(i, (i + s * X) % (Z * X)) for i in range(Z * X)])  13.2 us
    ppermute x9, waiting for transfers between devices, z_shift(): lax.ppermute(v, 'ctx', [(i, (i + s * X) % (Z * X)) for i in range(Z * X)])  8.38 us
    ppermute x2, starting transfers between devices, core_swap(): return lax.ppermute(v, 'dp', [(i, i ^ 1) for i in range(2 * Y)])  7.92 us
    all_to_all x1, starting transfers between devices, body(): lax.all_to_all(w, 'ctx', 0, 0, tiled=True, axis_index_groups=[[z * X + x...  5.51 us
    ppermute x12, waiting for transfers between devices, x_shift(): lax.ppermute(v, 'ctx', [(i, i // X * X + (i % X + s) % X) for i in range(...  4.93 us
    ppermute x2, starting transfers between devices, y_pair(): return lax.ppermute(v, 'dp', pairs)  4.12 us
    pallas_call x1, Pallas kernels, run_stats(): call(stats_kernel, (sds((4, QROWS, 256), BF), sds((4, QROWS, 128), BF), s...  3.13 us
  transfers between devices with their start and end apart: 26, of which 14 were waited for; matrix products, arithmetic and copies ran while one was open for 0% of the time, Pallas kernels for 7%

profile of v3, /device:TPU:1, one launch (start us, length us, event | category | flops | bytes accessed | tf_op | source)
XLA Modules:
  0.0 80.9 jit_solution(5060635510801419602)
XLA Ops:
  0.7 2.0 %shard_map.110 = (bf16[1296,128]{1,0:T(8,128)(2,1)}, bf16[64,640]{1,0:T(8,128)(2,1)}, bf16[64,640]{1,0:T(8,128)(2,1)}) custom-call(bf16[128,512]{1,0:T(8,128)(2,1)} %bitcast.18, bf16[128,256]{1,0:T(8,128)(2,1)} %bitcast.20, bf16[128,512]{1,0:T(8,128)(2,1)} %bitcast.19, bf16[576,128]{1,0:T(8,128)(2,1)} %bitcast.17, s32[1,128]{1,0:T(1,128)} %ids.1), custom_call_target="tpu_custom_call" | custom-call | bytes 1048576 | tf_op jit(solution)/shard_map/pallas_call | solution.py:84
  2.7 2.5 %collective-permute-start.2 = (bf16[64,640]{1,0:T(8,128)(2,1)}, bf16[64,640]{1,0:T(8,128)(2,1)S(1)}, u32[]{:S(2)}, u32[]{:S(2)}) collective-permute-start(bf16[64,640]{1,0:T(8,128)(2,1)} %get-tuple-element.48.refs_0_), channel_id=1, source_target_pairs={{0,4},{1,5},{2,6},{3,7},{4,8},{5,9},{6,10},{7,11},{8,12},{9,13},{1... | collective-permute-start | bytes 245768 | tf_op jit(solution)/shard_map/ppermute | solution.py:35
  5.2 1.6 %collective-permute-start.3 = (bf16[64,640]{1,0:T(8,128)(2,1)}, bf16[64,640]{1,0:T(8,128)(2,1)S(1)}, u32[]{:S(2)}, u32[]{:S(2)}) collective-permute-start(bf16[64,640]{1,0:T(8,128)(2,1)} %get-tuple-element.49.refs_1_), channel_id=1, source_target_pairs={{0,4},{1,5},{2,6},{3,7},{4,8},{5,9},{6,10},{7,11},{8,12},{9,13},{1... | collective-permute-start | bytes 245768 | tf_op jit(solution)/shard_map/ppermute | solution.py:35
  6.9 2.7 %collective-permute-start.1 = (bf16[1296,128]{1,0:T(8,128)(2,1)}, bf16[1296,128]{1,0:T(8,128)(2,1)S(1)}, u32[]{:S(2)}, u32[]{:S(2)}) collective-permute-start(bf16[1296,128]{1,0:T(8,128)(2,1)} %get-tuple-element.50.q0), channel_id=1, source_target_pairs={{0,2},{1,3},{2,0},{3,1},{4,6},{5,7},{6,4},{7,5},{8,10},{9,11},{10,... | collective-permute-start | bytes 995336 | tf_op jit(solution)/shard_map/ppermute | solution.py:31
  9.6 0.9 %collective-permute-start = (bf16[1296,128]{1,0:T(8,128)(2,1)}, bf16[1296,128]{1,0:T(8,128)(2,1)S(1)}, u32[]{:S(2)}, u32[]{:S(2)}) collective-permute-start(bf16[1296,128]{1,0:T(8,128)(2,1)} %get-tuple-element.50.q0), channel_id=1, source_target_pairs={{0,3},{1,0},{2,1},{3,2},{4,7},{5,4},{6,5},{7,6},{8,11},{9,8},{10,9... | collective-permute-start | bytes 995336 | tf_op jit(solution)/shard_map/ppermute | solution.py:31
  10.5 1.1 %collective-permute-done.2.refs_0_ = bf16[64,640]{1,0:T(8,128)(2,1)S(1)} collective-permute-done((bf16[64,640]{1,0:T(8,128)(2,1)}, bf16[64,640]{1,0:T(8,128)(2,1)S(1)}, u32[]{:S(2)}, u32[]{:S(2)}) %collective-permute-start.2) | collective-permute-done | bytes 81952 | tf_op jit(solution)/shard_map/ppermute | solution.py:35
  11.5 0.6 collective-permute-start.5
  12.1 1.2 %collective-permute-done.3.refs_1_ = bf16[64,640]{1,0:T(8,128)(2,1)S(1)} collective-permute-done((bf16[64,640]{1,0:T(8,128)(2,1)}, bf16[64,640]{1,0:T(8,128)(2,1)S(1)}, u32[]{:S(2)}, u32[]{:S(2)}) %collective-permute-start.3) | collective-permute-done | bytes 81952 | tf_op jit(solution)/shard_map/ppermute | solution.py:35
  13.3 1.7 %collective-permute-start.6 = (bf16[64,640]{1,0:T(8,128)(2,1)S(1)}, bf16[64,640]{1,0:T(8,128)(2,1)S(1)}, u32[]{:S(2)}, u32[]{:S(2)}) collective-permute-start(bf16[64,640]{1,0:T(8,128)(2,1)S(1)} %collective-permute-done.3.refs_1_), channel_id=1, source_target_pairs={{0,4},{1,5},{2,6},{3,7},{4,8},{5,9},{6,10},{7,11},{8,12},{9,13},{1... | collective-permute-start | bytes 245768 | tf_op jit(solution)/shard_map/ppermute | solution.py:35
  15.0 0.6 collective-permute-start.4
  15.7 0.7 collective-permute-done.5.refs_2_
  16.4 1.8 %collective-permute-done.6.refs_3_ = bf16[64,640]{1,0:T(8,128)(2,1)S(1)} collective-permute-done((bf16[64,640]{1,0:T(8,128)(2,1)S(1)}, bf16[64,640]{1,0:T(8,128)(2,1)S(1)}, u32[]{:S(2)}, u32[]{:S(2)}) %collective-permute-start.6) | collective-permute-done | bytes 81952 | tf_op jit(solution)/shard_map/ppermute | solution.py:35
  18.3 0.6 collective-permute-start.8
  19.0 0.5 shard_map.112
  19.4 1.4 %collective-permute-done.7.refs_2_ = bf16[64,640]{1,0:T(8,128)(2,1)S(1)} collective-permute-done((bf16[64,640]{1,0:T(8,128)(2,1)S(1)}, bf16[64,640]{1,0:T(8,128)(2,1)S(1)}, u32[]{:S(2)}, u32[]{:S(2)}) %collective-permute-start.7) | collective-permute-done | bytes 81952 | tf_op jit(solution)/shard_map/ppermute | solution.py:35
  20.8 2.2 %collective-permute-done.8.refs_3_ = bf16[64,640]{1,0:T(8,128)(2,1)S(1)} collective-permute-done((bf16[64,640]{1,0:T(8,128)(2,1)S(1)}, bf16[64,640]{1,0:T(8,128)(2,1)S(1)}, u32[]{:S(2)}, u32[]{:S(2)}) %collective-permute-start.8) | collective-permute-done | bytes 81952 | tf_op jit(solution)/shard_map/ppermute | solution.py:35
  23.2 0.4 shard_map.114
  23.6 1.0 %collective-permute-done.q1 = bf16[1296,128]{1,0:T(8,128)(2,1)S(1)} collective-permute-done((bf16[1296,128]{1,0:T(8,128)(2,1)}, bf16[1296,128]{1,0:T(8,128)(2,1)S(1)}, u32[]{:S(2)}, u32[]{:S(2)}) %collective-permute-start) | collective-permute-done | bytes 331808 | tf_op jit(solution)/shard_map/ppermute | solution.py:31
  24.6 3.1 %shard_map.115 = (bf16[4,512,256]{2,1,0:T(8,128)(2,1)S(1)}, bf16[4,512,128]{2,1,0:T(8,128)(2,1)S(1)}, f32[4,512,512]{2,1,0:T(8,128)S(1)}, f32[4,512,512]{2,1,0:T(8,128)S(1)}, f32[16,512]{1,0:T(8,128)S(1)}) custom-call(s32[3]{0:T(128)S(1)} %pad_add_fusion.where, bf16[1296,128]{1,0:T(8,128)(2,1)S(1)} %copy-done.2, ...), custom_call_target="tpu_custom_call" | custom-call | flops 1000000000 | bytes 8388608 | tf_op jit(solution)/shard_map/pallas_call | solution.py:173
  27.7 3.4 %collective-permute-start.11 = (f32[16,512]{1,0:T(8,128)S(1)}, f32[16,512]{1,0:T(8,128)S(1)}, u32[]{:S(2)}, u32[]{:S(2)}) collective-permute-start(f32[16,512]{1,0:T(8,128)S(1)} %get-tuple-element.63.t0), channel_id=1, source_target_pairs={{0,3},{1,0},{2,1},{3,2},{4,7},{5,4},{6,5},{7,6},{8,11},{9,8},{10,9... | collective-permute-start | bytes 98312 | tf_op jit(solution)/shard_map/ppermute | solution.py:31
  31.1 0.5 collective-permute-start.10
  31.6 0.2 collective-permute-start.9
  31.8 0.3 collective-permute-done.11.t3
  32.1 3.3 %collective-permute-done.10.t2 = f32[16,512]{1,0:T(8,128)S(1)} collective-permute-done((f32[16,512]{1,0:T(8,128)S(1)}, f32[16,512]{1,0:T(8,128)S(1)}, u32[]{:S(2)}, u32[]{:S(2)}) %collective-permute-start.10) | collective-permute-done | bytes 32800 | tf_op jit(solution)/shard_map/ppermute | solution.py:31
  35.4 0.3 collective-permute-done.9.t1
  35.7 3.0 %shard_map.116 = (bf16[4,128,512]{2,1,0:T(8,128)(2,1)S(1)}, bf16[4,128,512]{2,1,0:T(8,128)(2,1)S(1)}, bf16[4,512,512]{2,1,0:T(8,128)(2,1)S(1)}, bf16[2,512,512]{...) custom-call(s32[3]{0:T(128)S(1)} %pad_add_fusion.where, ...), custom_call_target="tpu_custom_call" | custom-call | flops 1500000000 | bytes 10485760 | tf_op jit(solution)/shard_map/pallas_call | solution.py:222
  38.7 2.8 %collective-permute-start.15 = (bf16[4,128,512]{2,1,0:T(8,128)(2,1)S(1)}, bf16[4,128,512]{2,1,0:T(8,128)(2,1)S(1)}, u32[]{:S(2)}, u32[]{:S(2)}) collective-permute-start(bf16[4,128,512]{2,1,0:T(8,128)(2,1)S(1)} %get-tuple-element.78), channel_id=1, source_target_pairs={{0,32},{32,0},{64,96},{96,64},{128,160},{160,128},{192,224},{224,1... | collective-permute-start | bytes 1572872 | tf_op jit(solution)/shard_map/ppermute | solution.py:44
  41.5 1.9 %collective-permute-start.19 = (bf16[128,640]{1,0:T(8,128)(2,1)S(1)}, bf16[128,640]{1,0:T(8,128)(2,1)S(1)}, u32[]{:S(2)}, u32[]{:S(2)}) collective-permute-start(bf16[128,640]{1,0:T(8,128)(2,1)S(1)} %get-tuple-element.83), channel_id=1, source_target_pairs={{0,28},{1,29},{2,30},{3,31},{4,0},{5,1},{6,2},{7,3},{8,4},{9,5},{1... | collective-permute-start | bytes 491528 | tf_op jit(solution)/shard_map/ppermute | solution.py:35
  43.4 0.7 shard_map.119
  44.2 1.3 %collective-permute-start.17 = (bf16[128,512]{1,0:T(8,128)(2,1)S(1)}, bf16[128,512]{1,0:T(8,128)(2,1)S(1)}, u32[]{:S(2)}, u32[]{:S(2)}) collective-permute-start(bf16[128,512]{1,0:T(8,128)(2,1)S(1)} %get-tuple-element.81), channel_id=1, source_target_pairs={{0,2},{1,3},{2,0},{3,1},{4,6},{5,7},{6,4},{7,5},{8,10},{9,11},{10,... | collective-permute-start | bytes 393224 | tf_op jit(solution)/shard_map/ppermute | solution.py:31
  45.5 2.0 %collective-permute-start.18 = (bf16[128,512]{1,0:T(8,128)(2,1)S(1)}, bf16[128,512]{1,0:T(8,128)(2,1)S(1)}, u32[]{:S(2)}, u32[]{:S(2)}) collective-permute-start(bf16[128,512]{1,0:T(8,128)(2,1)S(1)} %get-tuple-element.82), channel_id=1, source_target_pairs={{0,3},{1,0},{2,1},{3,2},{4,7},{5,4},{6,5},{7,6},{8,11},{9,8},{10,9... | collective-permute-start | bytes 393224 | tf_op jit(solution)/shard_map/ppermute | solution.py:31
  47.5 1.8 %shard_map.117 = (bf16[128,640]{1,0:T(8,128)(2,1)S(1)}, bf16[128,640]{1,0:T(8,128)(2,1)S(1)}, bf16[128,640]{1,0:T(8,128)(2,1)S(1)}, bf16[128,768]{1,0:T(8,128)(2...) custom-call(s32[3]{0:T(128)S(1)} %pad_add_fusion.where, ...), custom_call_target="tpu_custom_call" | custom-call | flops 1500000000 | bytes 10485760 | tf_op jit(solution)/shard_map/pallas_call | solution.py:252
  49.3 1.6 %collective-permute-start.21 = (bf16[128,640]{1,0:T(8,128)(2,1)S(1)}, bf16[128,640]{1,0:T(8,128)(2,1)S(1)}, u32[]{:S(2)}, u32[]{:S(2)}) collective-permute-start(bf16[128,640]{1,0:T(8,128)(2,1)S(1)} %get-tuple-element.85), channel_id=1, source_target_pairs={{0,28},{1,29},{2,30},{3,31},{4,0},{5,1},{6,2},{7,3},{8,4},{9,5},{1... | collective-permute-start | bytes 491528 | tf_op jit(solution)/shard_map/ppermute | solution.py:35
  50.9 2.5 %collective-permute-start.20 = (bf16[128,640]{1,0:T(8,128)(2,1)S(1)}, bf16[128,640]{1,0:T(8,128)(2,1)S(1)}, u32[]{:S(2)}, u32[]{:S(2)}) collective-permute-start(bf16[128,640]{1,0:T(8,128)(2,1)S(1)} %shard_map.121), channel_id=1, source_target_pairs={{0,24},{1,25},{2,26},{3,27},{4,28},{5,29},{6,30},{7,31},{8,0},{9,1... | collective-permute-start | bytes 491528 | tf_op jit(solution)/shard_map/ppermute | solution.py:35
  53.5 0.7 shard_map.120
  54.2 5.5 %all-to-all-start = ((bf16[8,16,512]{2,1,0:T(8,128)(2,1)}), bf16[8,16,512]{2,1,0:T(8,128)(2,1)S(1)}, u32[]{:S(2)}, u32[]{:S(2)}) async-start(bf16[8,16,512]{2,1,0:T(8,128)(2,1)} %bitcast.10), calls=%async_computation | async-start | bytes 262144 | tf_op jit(solution)/shard_map/all_to_all | solution.py:317
  59.7 1.5 %collective-permute-start.12 = (bf16[128,768]{1,0:T(8,128)(2,1)S(1)}, bf16[128,768]{1,0:T(8,128)(2,1)S(1)}, u32[]{:S(2)}, u32[]{:S(2)}) collective-permute-start(bf16[128,768]{1,0:T(8,128)(2,1)S(1)} %get-tuple-element.72), channel_id=1, source_target_pairs={{0,1},{1,2},{2,3},{3,0},{4,5},{5,6},{6,7},{7,4},{8,9},{9,10},{10,1... | collective-permute-start | bytes 589832 | tf_op jit(solution)/shard_map/ppermute | solution.py:31
  61.2 3.1 %collective-permute-start.13 = (bf16[128,768]{1,0:T(8,128)(2,1)S(1)}, bf16[128,768]{1,0:T(8,128)(2,1)S(1)}, u32[]{:S(2)}, u32[]{:S(2)}) collective-permute-start(bf16[128,768]{1,0:T(8,128)(2,1)S(1)} %get-tuple-element.73), channel_id=1, source_target_pairs={{0,2},{1,3},{2,0},{3,1},{4,6},{5,7},{6,4},{7,5},{8,10},{9,11},{10,... | collective-permute-start | bytes 589832 | tf_op jit(solution)/shard_map/ppermute | solution.py:31
  64.3 0.8 shard_map.122
  65.1 2.6 %all-to-all-done = bf16[8,16,512]{2,1,0:T(8,128)(2,1)S(1)} async-done(((bf16[8,16,512]{2,1,0:T(8,128)(2,1)}), bf16[8,16,512]{2,1,0:T(8,128)(2,1)S(1)}, u32[]{:S(2)}, u32[]{:S(2)}) %all-to-all-start) | async-done | bytes 131104 | tf_op jit(solution)/shard_map/all_to_all | solution.py:317
  67.7 1.4 %collective-permute-start.22 = (bf16[16,512]{1,0:T(8,128)(2,1)S(1)}, bf16[16,512]{1,0:T(8,128)(2,1)S(1)}, u32[]{:S(2)}, u32[]{:S(2)}) collective-permute-start(bf16[16,512]{1,0:T(8,128)(2,1)S(1)} %shard_map.123.refs_0_), channel_id=1, source_target_pairs={{0,64},{32,96},{64,0},{96,32},{128,192},{160,224},{192,128},{224,1... | collective-permute-start | bytes 49160 | tf_op jit(solution)/shard_map/ppermute | solution.py:40
  69.1 1.3 %collective-permute-done.22.refs_1_ = bf16[16,512]{1,0:T(8,128)(2,1)S(1)} collective-permute-done((bf16[16,512]{1,0:T(8,128)(2,1)S(1)}, bf16[16,512]{1,0:T(8,128)(2,1)S(1)}, u32[]{:S(2)}, u32[]{:S(2)}) %collective-permute-start.22) | collective-permute-done | bytes 16416 | tf_op jit(solution)/shard_map/ppermute | solution.py:40
  70.4 2.7 %collective-permute-start.23 = (bf16[16,512]{1,0:T(8,128)(2,1)S(1)}, bf16[16,512]{1,0:T(8,128)(2,1)S(1)}, u32[]{:S(2)}, u32[]{:S(2)}) collective-permute-start(bf16[16,512]{1,0:T(8,128)(2,1)S(1)} %shard_map.124.refs_0_), channel_id=1, source_target_pairs={{0,192},{32,224},{64,128},{96,160},{128,64},{160,96},{192,0},{224,... | collective-permute-start | bytes 49160 | tf_op jit(solution)/shard_map/ppermute | solution.py:40
  73.1 1.1 %collective-permute-done.23.refs_1_ = bf16[16,512]{1,0:T(8,128)(2,1)S(1)} collective-permute-done((bf16[16,512]{1,0:T(8,128)(2,1)S(1)}, bf16[16,512]{1,0:T(8,128)(2,1)S(1)}, u32[]{:S(2)}, u32[]{:S(2)}) %collective-permute-start.23) | collective-permute-done | bytes 16416 | tf_op jit(solution)/shard_map/ppermute | solution.py:40
  74.2 5.2 %collective-permute-start.24 = (f32[16,512]{1,0:T(8,128)S(1)}, f32[16,512]{1,0:T(8,128)S(1)}, u32[]{:S(2)}, u32[]{:S(2)}) collective-permute-start(f32[16,512]{1,0:T(8,128)S(1)} %shard_map.125), channel_id=1, source_target_pairs={{0,32},{32,0},{64,96},{96,64},{128,160},{160,128},{192,224},{224,1... | collective-permute-start | bytes 98312 | tf_op jit(solution)/shard_map/ppermute | solution.py:44
  79.4 0.7 shard_map.118
  80.2 0.1 collective-permute-done.24
  80.3 0.6 broadcast_select_fusion
  (32 shorter events, 0.6 us)
Async XLA Ops:
  0.6 18.3 %copy-start.1 = (bf16[512,512]{1,0:T(8,128)(2,1)S(1)}, bf16[512,512]{1,0:T(8,128)(2,1)}, u32[]{:S(2)}) copy-start(bf16[512,512]{1,0:T(8,128)(2,1)} %wv.1) | copy-start | bytes 1572868
  0.6 18.3 %copy-start = (bf16[512,512]{1,0:T(8,128)(2,1)S(1)}, bf16[512,512]{1,0:T(8,128)(2,1)}, u32[]{:S(2)}) copy-start(bf16[512,512]{1,0:T(8,128)(2,1)} %wk.1) | copy-start | bytes 1572868
  2.7 20.4 %copy-start.3 = (bf16[64,640]{1,0:T(8,128)(2,1)S(1)}, bf16[64,640]{1,0:T(8,128)(2,1)}, u32[]{:S(2)}) copy-start(bf16[64,640]{1,0:T(8,128)(2,1)} %get-tuple-element.48.refs_0_) | copy-start | bytes 245764
  2.7 20.4 %copy-start.4 = (bf16[64,640]{1,0:T(8,128)(2,1)S(1)}, bf16[64,640]{1,0:T(8,128)(2,1)}, u32[]{:S(2)}) copy-start(bf16[64,640]{1,0:T(8,128)(2,1)} %get-tuple-element.49.refs_1_) | copy-start | bytes 245764
  2.7 8.9 %collective-permute-start.2 = (bf16[64,640]{1,0:T(8,128)(2,1)}, bf16[64,640]{1,0:T(8,128)(2,1)S(1)}, u32[]{:S(2)}, u32[]{:S(2)}) collective-permute-start(bf16[64,640]{1,0:T(8,128)(2,1)} %get-tuple-element.48.refs_0_), channel_id=1, source_target_pairs={{0,4},{1,5},{2,6},{3,7},{4,8},{5,9},{6,10},{7,11},{8,12},{9,13},{1... | collective-permute-start | bytes 245768 | tf_op jit(solution)/shard_map/ppermute | solution.py:35
  5.2 8.1 %collective-permute-start.3 = (bf16[64,640]{1,0:T(8,128)(2,1)}, bf16[64,640]{1,0:T(8,128)(2,1)S(1)}, u32[]{:S(2)}, u32[]{:S(2)}) collective-permute-start(bf16[64,640]{1,0:T(8,128)(2,1)} %get-tuple-element.49.refs_1_), channel_id=1, source_target_pairs={{0,4},{1,5},{2,6},{3,7},{4,8},{5,9},{6,10},{7,11},{8,12},{9,13},{1... | collective-permute-start | bytes 245768 | tf_op jit(solution)/shard_map/ppermute | solution.py:35
  6.9 16.7 %collective-permute-start.1 = (bf16[1296,128]{1,0:T(8,128)(2,1)}, bf16[1296,128]{1,0:T(8,128)(2,1)S(1)}, u32[]{:S(2)}, u32[]{:S(2)}) collective-permute-start(bf16[1296,128]{1,0:T(8,128)(2,1)} %get-tuple-element.50.q0), channel_id=1, source_target_pairs={{0,2},{1,3},{2,0},{3,1},{4,6},{5,7},{6,4},{7,5},{8,10},{9,11},{10,... | collective-permute-start | bytes 995336 | tf_op jit(solution)/shard_map/ppermute | solution.py:31
  9.6 15.0 %collective-permute-start = (bf16[1296,128]{1,0:T(8,128)(2,1)}, bf16[1296,128]{1,0:T(8,128)(2,1)S(1)}, u32[]{:S(2)}, u32[]{:S(2)}) collective-permute-start(bf16[1296,128]{1,0:T(8,128)(2,1)} %get-tuple-element.50.q0), channel_id=1, source_target_pairs={{0,3},{1,0},{2,1},{3,2},{4,7},{5,4},{6,5},{7,6},{8,11},{9,8},{10,9... | collective-permute-start | bytes 995336 | tf_op jit(solution)/shard_map/ppermute | solution.py:31
  11.5 4.8 %collective-permute-start.5 = (bf16[64,640]{1,0:T(8,128)(2,1)S(1)}, bf16[64,640]{1,0:T(8,128)(2,1)S(1)}, u32[]{:S(2)}, u32[]{:S(2)}) collective-permute-start(bf16[64,640]{1,0:T(8,128)(2,1)S(1)} %collective-permute-done.2.refs_0_), channel_id=1, source_target_pairs={{0,4},{1,5},{2,6},{3,7},{4,8},{5,9},{6,10},{7,11},{8,12},{9,13},{1... | collective-permute-start | bytes 245768 | tf_op jit(solution)/shard_map/ppermute | solution.py:35
  13.3 5.0 %collective-permute-start.6 = (bf16[64,640]{1,0:T(8,128)(2,1)S(1)}, bf16[64,640]{1,0:T(8,128)(2,1)S(1)}, u32[]{:S(2)}, u32[]{:S(2)}) collective-permute-start(bf16[64,640]{1,0:T(8,128)(2,1)S(1)} %collective-permute-done.3.refs_1_), channel_id=1, source_target_pairs={{0,4},{1,5},{2,6},{3,7},{4,8},{5,9},{6,10},{7,11},{8,12},{9,13},{1... | collective-permute-start | bytes 245768 | tf_op jit(solution)/shard_map/ppermute | solution.py:35
  15.0 9.5 %collective-permute-start.4 = (bf16[1296,128]{1,0:T(8,128)(2,1)}, bf16[1296,128]{1,0:T(8,128)(2,1)S(1)}, u32[]{:S(2)}, u32[]{:S(2)}) collective-permute-start(bf16[1296,128]{1,0:T(8,128)(2,1)} %get-tuple-element.50.q0), channel_id=1, source_target_pairs={{0,1},{1,2},{2,3},{3,0},{4,5},{5,6},{6,7},{7,4},{8,9},{9,10},{10,1... | collective-permute-start | bytes 995336 | tf_op jit(solution)/shard_map/ppermute | solution.py:31
  16.3 4.5 %collective-permute-start.7 = (bf16[64,640]{1,0:T(8,128)(2,1)S(1)}, bf16[64,640]{1,0:T(8,128)(2,1)S(1)}, u32[]{:S(2)}, u32[]{:S(2)}) collective-permute-start(bf16[64,640]{1,0:T(8,128)(2,1)S(1)} %collective-permute-done.5.refs_2_), channel_id=1, source_target_pairs={{0,4},{1,5},{2,6},{3,7},{4,8},{5,9},{6,10},{7,11},{8,12},{9,13},{1... | collective-permute-start | bytes 245768 | tf_op jit(solution)/shard_map/ppermute | solution.py:35
  18.3 4.8 %collective-permute-start.8 = (bf16[64,640]{1,0:T(8,128)(2,1)S(1)}, bf16[64,640]{1,0:T(8,128)(2,1)S(1)}, u32[]{:S(2)}, u32[]{:S(2)}) collective-permute-start(bf16[64,640]{1,0:T(8,128)(2,1)S(1)} %collective-permute-done.6.refs_3_), channel_id=1, source_target_pairs={{0,4},{1,5},{2,6},{3,7},{4,8},{5,9},{6,10},{7,11},{8,12},{9,13},{1... | collective-permute-start | bytes 245768 | tf_op jit(solution)/shard_map/ppermute | solution.py:35
  19.0 5.6 %copy-start.2 = (bf16[1296,128]{1,0:T(8,128)(2,1)S(1)}, bf16[1296,128]{1,0:T(8,128)(2,1)}, u32[]{:S(2)}) copy-start(bf16[1296,128]{1,0:T(8,128)(2,1)} %get-tuple-element.50.q0) | copy-start | bytes 995332
  27.7 4.4 %collective-permute-start.11 = (f32[16,512]{1,0:T(8,128)S(1)}, f32[16,512]{1,0:T(8,128)S(1)}, u32[]{:S(2)}, u32[]{:S(2)}) collective-permute-start(f32[16,512]{1,0:T(8,128)S(1)} %get-tuple-element.63.t0), channel_id=1, source_target_pairs={{0,3},{1,0},{2,1},{3,2},{4,7},{5,4},{6,5},{7,6},{8,11},{9,8},{10,9... | collective-permute-start | bytes 98312 | tf_op jit(solution)/shard_map/ppermute | solution.py:31
  31.1 4.3 %collective-permute-start.10 = (f32[16,512]{1,0:T(8,128)S(1)}, f32[16,512]{1,0:T(8,128)S(1)}, u32[]{:S(2)}, u32[]{:S(2)}) collective-permute-start(f32[16,512]{1,0:T(8,128)S(1)} %get-tuple-element.63.t0), channel_id=1, source_target_pairs={{0,2},{1,3},{2,0},{3,1},{4,6},{5,7},{6,4},{7,5},{8,10},{9,11},{10,... | collective-permute-start | bytes 98312 | tf_op jit(solution)/shard_map/ppermute | solution.py:31
  31.6 4.1 %collective-permute-start.9 = (f32[16,512]{1,0:T(8,128)S(1)}, f32[16,512]{1,0:T(8,128)S(1)}, u32[]{:S(2)}, u32[]{:S(2)}) collective-permute-start(f32[16,512]{1,0:T(8,128)S(1)} %get-tuple-element.63.t0), channel_id=1, source_target_pairs={{0,1},{1,2},{2,3},{3,0},{4,5},{5,6},{6,7},{7,4},{8,9},{9,10},{10,1... | collective-permute-start | bytes 98312 | tf_op jit(solution)/shard_map/ppermute | solution.py:31
  38.7 4.7 %collective-permute-start.15 = (bf16[4,128,512]{2,1,0:T(8,128)(2,1)S(1)}, bf16[4,128,512]{2,1,0:T(8,128)(2,1)S(1)}, u32[]{:S(2)}, u32[]{:S(2)}) collective-permute-start(bf16[4,128,512]{2,1,0:T(8,128)(2,1)S(1)} %get-tuple-element.78), channel_id=1, source_target_pairs={{0,32},{32,0},{64,96},{96,64},{128,160},{160,128},{192,224},{224,1... | collective-permute-start | bytes 1572872 | tf_op jit(solution)/shard_map/ppermute | solution.py:44
  41.5 9.4 %collective-permute-start.19 = (bf16[128,640]{1,0:T(8,128)(2,1)S(1)}, bf16[128,640]{1,0:T(8,128)(2,1)S(1)}, u32[]{:S(2)}, u32[]{:S(2)}) collective-permute-start(bf16[128,640]{1,0:T(8,128)(2,1)S(1)} %get-tuple-element.83), channel_id=1, source_target_pairs={{0,28},{1,29},{2,30},{3,31},{4,0},{5,1},{6,2},{7,3},{8,4},{9,5},{1... | collective-permute-start | bytes 491528 | tf_op jit(solution)/shard_map/ppermute | solution.py:35
  44.1 9.4 %collective-permute-start.16 = (bf16[128,512]{1,0:T(8,128)(2,1)S(1)}, bf16[128,512]{1,0:T(8,128)(2,1)S(1)}, u32[]{:S(2)}, u32[]{:S(2)}) collective-permute-start(bf16[128,512]{1,0:T(8,128)(2,1)S(1)} %get-tuple-element.80), channel_id=1, source_target_pairs={{0,1},{1,2},{2,3},{3,0},{4,5},{5,6},{6,7},{7,4},{8,9},{9,10},{10,1... | collective-permute-start | bytes 393224 | tf_op jit(solution)/shard_map/ppermute | solution.py:31
  44.2 9.3 %collective-permute-start.17 = (bf16[128,512]{1,0:T(8,128)(2,1)S(1)}, bf16[128,512]{1,0:T(8,128)(2,1)S(1)}, u32[]{:S(2)}, u32[]{:S(2)}) collective-permute-start(bf16[128,512]{1,0:T(8,128)(2,1)S(1)} %get-tuple-element.81), channel_id=1, source_target_pairs={{0,2},{1,3},{2,0},{3,1},{4,6},{5,7},{6,4},{7,5},{8,10},{9,11},{10,... | collective-permute-start | bytes 393224 | tf_op jit(solution)/shard_map/ppermute | solution.py:31
  45.5 8.0 %collective-permute-start.18 = (bf16[128,512]{1,0:T(8,128)(2,1)S(1)}, bf16[128,512]{1,0:T(8,128)(2,1)S(1)}, u32[]{:S(2)}, u32[]{:S(2)}) collective-permute-start(bf16[128,512]{1,0:T(8,128)(2,1)S(1)} %get-tuple-element.82), channel_id=1, source_target_pairs={{0,3},{1,0},{2,1},{3,2},{4,7},{5,4},{6,5},{7,6},{8,11},{9,8},{10,9... | collective-permute-start | bytes 393224 | tf_op jit(solution)/shard_map/ppermute | solution.py:31
  49.3 15.0 %collective-permute-start.21 = (bf16[128,640]{1,0:T(8,128)(2,1)S(1)}, bf16[128,640]{1,0:T(8,128)(2,1)S(1)}, u32[]{:S(2)}, u32[]{:S(2)}) collective-permute-start(bf16[128,640]{1,0:T(8,128)(2,1)S(1)} %get-tuple-element.85), channel_id=1, source_target_pairs={{0,28},{1,29},{2,30},{3,31},{4,0},{5,1},{6,2},{7,3},{8,4},{9,5},{1... | collective-permute-start | bytes 491528 | tf_op jit(solution)/shard_map/ppermute | solution.py:35
  50.9 13.4 %collective-permute-start.20 = (bf16[128,640]{1,0:T(8,128)(2,1)S(1)}, bf16[128,640]{1,0:T(8,128)(2,1)S(1)}, u32[]{:S(2)}, u32[]{:S(2)}) collective-permute-start(bf16[128,640]{1,0:T(8,128)(2,1)S(1)} %shard_map.121), channel_id=1, source_target_pairs={{0,24},{1,25},{2,26},{3,27},{4,28},{5,29},{6,30},{7,31},{8,0},{9,1... | collective-permute-start | bytes 491528 | tf_op jit(solution)/shard_map/ppermute | solution.py:35
  54.2 13.4 %all-to-all-start = ((bf16[8,16,512]{2,1,0:T(8,128)(2,1)}), bf16[8,16,512]{2,1,0:T(8,128)(2,1)S(1)}, u32[]{:S(2)}, u32[]{:S(2)}) async-start(bf16[8,16,512]{2,1,0:T(8,128)(2,1)} %bitcast.10), calls=%async_computation | async-start | bytes 262144 | tf_op jit(solution)/shard_map/all_to_all | solution.py:317
  59.7 19.7 %collective-permute-start.12 = (bf16[128,768]{1,0:T(8,128)(2,1)S(1)}, bf16[128,768]{1,0:T(8,128)(2,1)S(1)}, u32[]{:S(2)}, u32[]{:S(2)}) collective-permute-start(bf16[128,768]{1,0:T(8,128)(2,1)S(1)} %get-tuple-element.72), channel_id=1, source_target_pairs={{0,1},{1,2},{2,3},{3,0},{4,5},{5,6},{6,7},{7,4},{8,9},{9,10},{10,1... | collective-permute-start | bytes 589832 | tf_op jit(solution)/shard_map/ppermute | solution.py:31
  61.2 18.2 %collective-permute-start.13 = (bf16[128,768]{1,0:T(8,128)(2,1)S(1)}, bf16[128,768]{1,0:T(8,128)(2,1)S(1)}, u32[]{:S(2)}, u32[]{:S(2)}) collective-permute-start(bf16[128,768]{1,0:T(8,128)(2,1)S(1)} %get-tuple-element.73), channel_id=1, source_target_pairs={{0,2},{1,3},{2,0},{3,1},{4,6},{5,7},{6,4},{7,5},{8,10},{9,11},{10,... | collective-permute-start | bytes 589832 | tf_op jit(solution)/shard_map/ppermute | solution.py:31
  64.3 15.1 %collective-permute-start.14 = (bf16[128,768]{1,0:T(8,128)(2,1)S(1)}, bf16[128,768]{1,0:T(8,128)(2,1)S(1)}, u32[]{:S(2)}, u32[]{:S(2)}) collective-permute-start(bf16[128,768]{1,0:T(8,128)(2,1)S(1)} %get-tuple-element.74), channel_id=1, source_target_pairs={{0,3},{1,0},{2,1},{3,2},{4,7},{5,4},{6,5},{7,6},{8,11},{9,8},{10,9... | collective-permute-start | bytes 589832 | tf_op jit(solution)/shard_map/ppermute | solution.py:31
  67.7 2.7 %collective-permute-start.22 = (bf16[16,512]{1,0:T(8,128)(2,1)S(1)}, bf16[16,512]{1,0:T(8,128)(2,1)S(1)}, u32[]{:S(2)}, u32[]{:S(2)}) collective-permute-start(bf16[16,512]{1,0:T(8,128)(2,1)S(1)} %shard_map.123.refs_0_), channel_id=1, source_target_pairs={{0,64},{32,96},{64,0},{96,32},{128,192},{160,224},{192,128},{224,1... | collective-permute-start | bytes 49160 | tf_op jit(solution)/shard_map/ppermute | solution.py:40
  70.4 3.9 %collective-permute-start.23 = (bf16[16,512]{1,0:T(8,128)(2,1)S(1)}, bf16[16,512]{1,0:T(8,128)(2,1)S(1)}, u32[]{:S(2)}, u32[]{:S(2)}) collective-permute-start(bf16[16,512]{1,0:T(8,128)(2,1)S(1)} %shard_map.124.refs_0_), channel_id=1, source_target_pairs={{0,192},{32,224},{64,128},{96,160},{128,64},{160,96},{192,0},{224,... | collective-permute-start | bytes 49160 | tf_op jit(solution)/shard_map/ppermute | solution.py:40
  74.2 6.0 %collective-permute-start.24 = (f32[16,512]{1,0:T(8,128)S(1)}, f32[16,512]{1,0:T(8,128)S(1)}, u32[]{:S(2)}, u32[]{:S(2)}) collective-permute-start(f32[16,512]{1,0:T(8,128)S(1)} %shard_map.125), channel_id=1, source_target_pairs={{0,32},{32,0},{64,96},{96,64},{128,160},{160,128},{192,224},{224,1... | collective-permute-start | bytes 98312 | tf_op jit(solution)/shard_map/ppermute | solution.py:44

commit v4 on v3

--- a/solution.py
+++ b/solution.py
@@ -179,8 +179,9 @@
     )(where, *qs, *keys)
 
 
-def weight_kernel(where, t0, t1, t2, t3, qc, gs, es, dps, latents0, latents1, wk, wv, w_keep, w_send, ds, dkv, tail, d3, p_scr):
-    core = where[2]
+def weight_kernel(where, t0, t1, t2, t3, qc, gs, es, dps, latents0, latents1, wk, wv, w_keep, w_far, w_send, ds, dkv, tail, d3,
+                  p_scr, w_scr):
+    xi, core = where[0], where[2]
     tops = [t[0:4, :] for t in (t0, t1, t2, t3)]
     top = functools.reduce(jnp.maximum, tops)
     total = jnp.zeros((4, QROWS), F32)
@@ -204,11 +205,14 @@
         dk = jnp.dot(ds[h], qc[h], preferred_element_type=F32)
         dkv[0, :, cols] = dk[:, :128].astype(BF)
         rope_grad[h % 2] = rope_grad[h % 2] + dk[:, 128:]
-    for out, which in ((w_send, 1 - core), (w_keep, core)):
+    for out, which in ((w_scr, 1 - core), (w_keep, core)):
         w = (lax.dot_general(dkv[which, :HALF], latents0[...], TN, preferred_element_type=F32)
              + lax.dot_general(dkv[which, HALF:], latents1[...], TN, preferred_element_type=F32)).astype(BF)
         for r in range(32):
-            out[r % 4, r // 4 * 16:r // 4 * 16 + 16, :] = w[r * 16:r * 16 + 16, :]
+            out[(r - xi) & 3, r // 4 * 16:r // 4 * 16 + 16, :] = w[r * 16:r * 16 + 16, :]
+    w_far[...] = w_scr[2]
+    for n, s in enumerate((0, 1, 3)):
+        w_send[n] = w_scr[s]
     lane = lax.broadcasted_iota(jnp.int32, (KROWS, 128), 1)
     tail[...] = jnp.where(lane < 64, rope_grad[0] + pltpu.roll(rope_grad[1], 64, 1), 0.0).astype(BF)
     far = slice(3 * ROWS, KROWS)
@@ -221,9 +225,9 @@
     sds = jax.ShapeDtypeStruct
     return call(
         weight_kernel,
-        (sds((4, 128, 512), BF), sds((4, 128, 512), BF), sds((4, KROWS, QROWS), BF), sds((2, KROWS, 512), BF),
+        (sds((4, 128, 512), BF), sds((128, 512), BF), sds((3, 128, 512), BF), sds((4, KROWS, QROWS), BF), sds((2, KROWS, 512), BF),
          sds((KROWS, 128), BF), sds((128, 640), BF)),
-        1, 12, scratch=[pltpu.VMEM((2, KROWS, QROWS), BF)], flops=1_500_000_000, nbytes=10 << 20,
+        1, 12, scratch=[pltpu.VMEM((2, KROWS, QROWS), BF), pltpu.VMEM((4, 128, 512), BF)], flops=1_500_000_000, nbytes=10 << 20,
     )(where, *ts, *mats)
 
 
@@ -256,15 +260,17 @@
     )(where, ds, dkv, tail, kc0, kc1, wk, wv)
 
 
-def spread_kernel(where, keep, recv, o0, o1, o2, o3):
-    xi = where[0]
-    for s, o in enumerate((o0, o1, o2, o3)):
-        at = (xi + s) & 3
-        o[...] = (keep[at].astype(F32) + recv[at].astype(F32)).astype(BF)
-
-
-def spread(where, keep, recv):
-    return call(spread_kernel, tuple([jax.ShapeDtypeStruct((128, 512), BF)] * 4), 1, 2, nbytes=2 << 20)(where, keep, recv)
+def far_sum_kernel(keep, far, out):
+    out[...] = (keep[2].astype(F32) + far[...].astype(F32)).astype(BF)
+
+
+def near_sum_kernel(keep, near, out1, out3):
+    out1[...] = (keep[1].astype(F32) + near[1].astype(F32)).astype(BF)
+    out3[...] = (keep[3].astype(F32) + near[2].astype(F32)).astype(BF)
+
+
+def sum_x_kernel(keep, near, p1, p2, p3, out):
+    out[...] = (keep[0].astype(F32) + near[0].astype(F32) + wide(p1, p2, p3)).astype(BF)
 
 
 def wide(*refs):
@@ -289,8 +295,8 @@
     rope[...] = q[:, 512:]
 
 
-def latent_kernel(d2, d1, d0, latent):
-    latent[...] = wide(d2, d1, d0).astype(BF)[:, :576].T
+def latent_kernel(part, d1, latent):
+    latent[...] = wide(part, d1).astype(BF)[:, :576].T
 
 
 def body(kv_latent, q_nope, q_rope, w_key_up, w_value_up, out_grad, segment_ids):
@@ -308,25 +314,29 @@
     kc1, vs1, latents1, marks1 = run_keys(c + c3, wk, wv, False)
     qc, gs, es, dps, stats = run_stats(where, qs, kc0, kc1, vs0, vs1, marks0, marks1)
     ts = (stats, x_shift(stats, 1), x_shift(stats, 2), x_shift(stats, -1))
-    w_keep, w_send, ds, dkv, tail, d3 = run_weight(where, ts, qc, gs, es, dps, latents0, latents1, wk, wv)
-    received = core_swap(w_send)
+    w_keep, w_far, w_send, ds, dkv, tail, d3 = run_weight(where, ts, qc, gs, es, dps, latents0, latents1, wk, wv)
+    w_far, near = core_swap(w_far), core_swap(w_send)
     d0, d1, d2, o0, o1, o2, o3 = run_grads(where, ds, dkv, tail, kc0, kc1, wk, wv)
-    pieces = spread(where, w_keep, received)
-    sds = jax.ShapeDtypeStruct
-    w = add_up(pieces[0], x_shift(pieces[1], 1), x_shift(pieces[2], 2), x_shift(pieces[3], -1))
+    sds = jax.ShapeDtypeStruct
+    piece = sds((128, 512), BF)
+    p2 = call(far_sum_kernel, piece, 0, 2, nbytes=1 << 18)(w_keep, w_far)
+    p1, p3 = call(near_sum_kernel, (piece, piece), 0, 2, nbytes=1 << 19)(w_keep, near)
+    w = call(sum_x_kernel, piece, 0, 5, nbytes=1 << 20)(w_keep, near, x_shift(p1, 1), x_shift(p2, 2), x_shift(p3, -1))
     w = lax.all_to_all(w, "ctx", 0, 0, tiled=True, axis_index_groups=[[z * X + x for z in range(Z)] for x in range(X)])
     d = add_up(z_shift(d3, -1), d2)
-    grad_latent = call(latent_kernel, sds((576, 128), BF), 0, 3, flops=1_000_000_000, nbytes=1 << 20)(
-        z_shift(d, -2), z_shift(d1, -1), d0)
-    w, grad_latent = lax.optimization_barrier((w, grad_latent))
+    d = call(sum_kernel, sds((128, 640), F32), 0, 2, flops=1_000_000_000, nbytes=1 << 20)(z_shift(d, -2), d0)
+    w, d = lax.optimization_barrier((w, d))
     w = call(sum_z_kernel, sds((16, 512), BF), 0, 1, nbytes=1 << 18)(w)
     w = add_up(w, y_pair(w, False))
-    w = add_up(w, y_pair(w, True), dtype=F32)
+    other = y_pair(w, True)
+    grad_nope, grad_rope = call(query_kernel, (sds((128, 512), BF), sds((128, 256), BF)), 0, 4, nbytes=1 << 20)(
+        o0, x_shift(o1, 1), x_shift(o2, 2), x_shift(o3, -1))
+    grad_latent = call(latent_kernel, sds((576, 128), BF), 0, 2, nbytes=1 << 20)(d, z_shift(d1, -1))
+    w, grad_nope, grad_latent = lax.optimization_barrier((w, grad_nope, grad_latent))
+    w = add_up(w, other, dtype=F32)
     other = core_swap(w)
     grad_key = jnp.where(core == 0, w, other)
     grad_value = jnp.where(core == 0, other, w)
-    grad_nope, grad_rope = call(query_kernel, (sds((128, 512), BF), sds((128, 256), BF)), 0, 4, nbytes=1 << 20)(
-        o0, x_shift(o1, 1), x_shift(o2, 2), x_shift(o3, -1))
     return grad_nope[None], grad_rope[None], grad_latent.T[None], grad_key, grad_value
 
 

time: 81.1 us -> 80.4 us (level)
    ppermute x2 -> x3, starting transfers between devices: 7.92 us -> 6.78 us  [core_swap(): return lax.ppermute(v, 'dp', [(i, i ^ 1) for i in range(2 * Y)])]
    ppermute x9, starting transfers between devices: 13.2 us -> 14.3 us  [z_shift(): lax.ppermute(v, 'ctx', [(i, (i + s * X) % (Z * X)) for i in range(Z * X)])]
    all_to_all x1, waiting for transfers between devices: 2.56 us -> 1.48 us  [body(): lax.all_to_all(w, 'ctx', 0, 0, tiled=True, axis_index_groups=[[z * X + x...]
    ppermute x2, waiting for transfers between devices: 2.42 us -> 1.59 us  [y_pair(): return lax.ppermute(v, 'dp', pairs)]
    pallas_call x3 -> x6, Pallas kernels: 4.42 us -> 4.71 us  [the longest x1 3.08 us: run_weight(): call(weight_kernel, (sds((4, 128, 512), BF), sds((128, 512), BF), sds((3,...]
  transfers between devices with their start and end apart: 26 -> 27, of which waited for: 14 -> 14; matrix products, arithmetic and copies ran while one was open for 0% -> 0% of each run, Pallas kernels for 7% -> 7%
where the time goes in v4:
time: 80.4 us; the launch traced here: 80.2 us
  starting transfers between devices  47 us (58%)
  waiting for transfers between devices  18.1 us (23%)
  Pallas kernels  13.6 us (17%)
  between operations  0.82 us (1%)
    ppermute x12, starting transfers between devices, x_shift(): lax.ppermute(v, 'ctx', [(i, i // X * X + (i % X + s) % X) for i in range(...  16 us
    ppermute x9, starting transfers between devices, z_shift(): lax.ppermute(v, 'ctx', [(i, (i + s * X) % (Z * X)) for i in range(Z * X)])  14.3 us
    ppermute x9, waiting for transfers between devices, z_shift(): lax.ppermute(v, 'ctx', [(i, (i + s * X) % (Z * X)) for i in range(Z * X)])  8.38 us
    ppermute x3, starting transfers between devices, core_swap(): return lax.ppermute(v, 'dp', [(i, i ^ 1) for i in range(2 * Y)])  6.78 us
    all_to_all x1, starting transfers between devices, body(): lax.all_to_all(w, 'ctx', 0, 0, tiled=True, axis_index_groups=[[z * X + x...  5.84 us
    ppermute x12, waiting for transfers between devices, x_shift(): lax.ppermute(v, 'ctx', [(i, i // X * X + (i % X + s) % X) for i in range(...  5.74 us
    ppermute x2, starting transfers between devices, y_pair(): return lax.ppermute(v, 'dp', pairs)  4.11 us
    pallas_call x1, Pallas kernels, run_stats(): call(stats_kernel, (sds((4, QROWS, 256), BF), sds((4, QROWS, 128), BF), s...  3.14 us
  transfers between devices with their start and end apart: 27, of which 14 were waited for; matrix products, arithmetic and copies ran while one was open for 0% of the time, Pallas kernels for 7%

profile of v4, /device:TPU:1, one launch (start us, length us, event | category | flops | bytes accessed | tf_op | source)
XLA Modules:
  0.0 80.2 jit_solution(11940268044953337176)
XLA Ops:
  0.7 2.0 %shard_map.110 = (bf16[1296,128]{1,0:T(8,128)(2,1)}, bf16[64,640]{1,0:T(8,128)(2,1)}, bf16[64,640]{1,0:T(8,128)(2,1)}) custom-call(bf16[128,512]{1,0:T(8,128)(2,1)} %bitcast.19, bf16[128,256]{1,0:T(8,128)(2,1)} %bitcast.21, bf16[128,512]{1,0:T(8,128)(2,1)} %bitcast.20, bf16[576,128]{1,0:T(8,128)(2,1)} %bitcast.18, s32[1,128]{1,0:T(1,128)} %ids.1), custom_call_target="tpu_custom_call" | custom-call | bytes 1048576 | tf_op jit(solution)/shard_map/pallas_call | solution.py:84
  2.7 2.5 %collective-permute-start.2 = (bf16[64,640]{1,0:T(8,128)(2,1)}, bf16[64,640]{1,0:T(8,128)(2,1)S(1)}, u32[]{:S(2)}, u32[]{:S(2)}) collective-permute-start(bf16[64,640]{1,0:T(8,128)(2,1)} %get-tuple-element.50.refs_0_), channel_id=1, source_target_pairs={{0,4},{1,5},{2,6},{3,7},{4,8},{5,9},{6,10},{7,11},{8,12},{9,13},{1... | collective-permute-start | bytes 245768 | tf_op jit(solution)/shard_map/ppermute | solution.py:35
  5.2 1.6 %collective-permute-start.3 = (bf16[64,640]{1,0:T(8,128)(2,1)}, bf16[64,640]{1,0:T(8,128)(2,1)S(1)}, u32[]{:S(2)}, u32[]{:S(2)}) collective-permute-start(bf16[64,640]{1,0:T(8,128)(2,1)} %get-tuple-element.51.refs_1_), channel_id=1, source_target_pairs={{0,4},{1,5},{2,6},{3,7},{4,8},{5,9},{6,10},{7,11},{8,12},{9,13},{1... | collective-permute-start | bytes 245768 | tf_op jit(solution)/shard_map/ppermute | solution.py:35
  6.9 2.7 %collective-permute-start.1 = (bf16[1296,128]{1,0:T(8,128)(2,1)}, bf16[1296,128]{1,0:T(8,128)(2,1)S(1)}, u32[]{:S(2)}, u32[]{:S(2)}) collective-permute-start(bf16[1296,128]{1,0:T(8,128)(2,1)} %get-tuple-element.52.q0), channel_id=1, source_target_pairs={{0,2},{1,3},{2,0},{3,1},{4,6},{5,7},{6,4},{7,5},{8,10},{9,11},{10,... | collective-permute-start | bytes 995336 | tf_op jit(solution)/shard_map/ppermute | solution.py:31
  9.6 0.9 %collective-permute-start = (bf16[1296,128]{1,0:T(8,128)(2,1)}, bf16[1296,128]{1,0:T(8,128)(2,1)S(1)}, u32[]{:S(2)}, u32[]{:S(2)}) collective-permute-start(bf16[1296,128]{1,0:T(8,128)(2,1)} %get-tuple-element.52.q0), channel_id=1, source_target_pairs={{0,3},{1,0},{2,1},{3,2},{4,7},{5,4},{6,5},{7,6},{8,11},{9,8},{10,9... | collective-permute-start | bytes 995336 | tf_op jit(solution)/shard_map/ppermute | solution.py:31
  10.5 1.1 %collective-permute-done.2.refs_0_ = bf16[64,640]{1,0:T(8,128)(2,1)S(1)} collective-permute-done((bf16[64,640]{1,0:T(8,128)(2,1)}, bf16[64,640]{1,0:T(8,128)(2,1)S(1)}, u32[]{:S(2)}, u32[]{:S(2)}) %collective-permute-start.2) | collective-permute-done | bytes 81952 | tf_op jit(solution)/shard_map/ppermute | solution.py:35
  11.5 0.6 collective-permute-start.5
  12.1 1.2 %collective-permute-done.3.refs_1_ = bf16[64,640]{1,0:T(8,128)(2,1)S(1)} collective-permute-done((bf16[64,640]{1,0:T(8,128)(2,1)}, bf16[64,640]{1,0:T(8,128)(2,1)S(1)}, u32[]{:S(2)}, u32[]{:S(2)}) %collective-permute-start.3) | collective-permute-done | bytes 81952 | tf_op jit(solution)/shard_map/ppermute | solution.py:35
  13.3 1.7 %collective-permute-start.6 = (bf16[64,640]{1,0:T(8,128)(2,1)S(1)}, bf16[64,640]{1,0:T(8,128)(2,1)S(1)}, u32[]{:S(2)}, u32[]{:S(2)}) collective-permute-start(bf16[64,640]{1,0:T(8,128)(2,1)S(1)} %collective-permute-done.3.refs_1_), channel_id=1, source_target_pairs={{0,4},{1,5},{2,6},{3,7},{4,8},{5,9},{6,10},{7,11},{8,12},{9,13},{1... | collective-permute-start | bytes 245768 | tf_op jit(solution)/shard_map/ppermute | solution.py:35
  15.0 0.6 collective-permute-start.4
  15.7 0.7 collective-permute-done.5.refs_2_
  16.3 0.1 collective-permute-start.7
  16.4 1.8 %collective-permute-done.6.refs_3_ = bf16[64,640]{1,0:T(8,128)(2,1)S(1)} collective-permute-done((bf16[64,640]{1,0:T(8,128)(2,1)S(1)}, bf16[64,640]{1,0:T(8,128)(2,1)S(1)}, u32[]{:S(2)}, u32[]{:S(2)}) %collective-permute-start.6) | collective-permute-done | bytes 81952 | tf_op jit(solution)/shard_map/ppermute | solution.py:35
  18.3 0.6 collective-permute-start.8
  19.0 0.5 shard_map.112
  19.4 1.4 %collective-permute-done.7.refs_2_ = bf16[64,640]{1,0:T(8,128)(2,1)S(1)} collective-permute-done((bf16[64,640]{1,0:T(8,128)(2,1)S(1)}, bf16[64,640]{1,0:T(8,128)(2,1)S(1)}, u32[]{:S(2)}, u32[]{:S(2)}) %collective-permute-start.7) | collective-permute-done | bytes 81952 | tf_op jit(solution)/shard_map/ppermute | solution.py:35
  20.8 2.2 %collective-permute-done.8.refs_3_ = bf16[64,640]{1,0:T(8,128)(2,1)S(1)} collective-permute-done((bf16[64,640]{1,0:T(8,128)(2,1)S(1)}, bf16[64,640]{1,0:T(8,128)(2,1)S(1)}, u32[]{:S(2)}, u32[]{:S(2)}) %collective-permute-start.8) | collective-permute-done | bytes 81952 | tf_op jit(solution)/shard_map/ppermute | solution.py:35
  23.2 0.4 shard_map.114
  23.6 1.0 %collective-permute-done.q1 = bf16[1296,128]{1,0:T(8,128)(2,1)S(1)} collective-permute-done((bf16[1296,128]{1,0:T(8,128)(2,1)}, bf16[1296,128]{1,0:T(8,128)(2,1)S(1)}, u32[]{:S(2)}, u32[]{:S(2)}) %collective-permute-start) | collective-permute-done | bytes 331808 | tf_op jit(solution)/shard_map/ppermute | solution.py:31
  24.6 3.1 %shard_map.115 = (bf16[4,512,256]{2,1,0:T(8,128)(2,1)S(1)}, bf16[4,512,128]{2,1,0:T(8,128)(2,1)S(1)}, f32[4,512,512]{2,1,0:T(8,128)S(1)}, f32[4,512,512]{2,1,0:T(8,128)S(1)}, f32[16,512]{1,0:T(8,128)S(1)}) custom-call(s32[3]{0:T(128)S(1)} %pad_add_fusion.where, bf16[1296,128]{1,0:T(8,128)(2,1)S(1)} %copy-done.2, ...), custom_call_target="tpu_custom_call" | custom-call | flops 1000000000 | bytes 8388608 | tf_op jit(solution)/shard_map/pallas_call | solution.py:173
  27.7 3.4 %collective-permute-start.11 = (f32[16,512]{1,0:T(8,128)S(1)}, f32[16,512]{1,0:T(8,128)S(1)}, u32[]{:S(2)}, u32[]{:S(2)}) collective-permute-start(f32[16,512]{1,0:T(8,128)S(1)} %get-tuple-element.65.t0), channel_id=1, source_target_pairs={{0,3},{1,0},{2,1},{3,2},{4,7},{5,4},{6,5},{7,6},{8,11},{9,8},{10,9... | collective-permute-start | bytes 98312 | tf_op jit(solution)/shard_map/ppermute | solution.py:31
  31.1 0.5 collective-permute-start.10
  31.6 0.2 collective-permute-start.9
  31.8 0.3 collective-permute-done.11.t3
  32.1 3.3 %collective-permute-done.10.t2 = f32[16,512]{1,0:T(8,128)S(1)} collective-permute-done((f32[16,512]{1,0:T(8,128)S(1)}, f32[16,512]{1,0:T(8,128)S(1)}, u32[]{:S(2)}, u32[]{:S(2)}) %collective-permute-start.10) | collective-permute-done | bytes 32800 | tf_op jit(solution)/shard_map/ppermute | solution.py:31
  35.4 0.3 collective-permute-done.9.t1
  35.7 3.1 %shard_map.116 = (bf16[4,128,512]{2,1,0:T(8,128)(2,1)S(1)}, bf16[128,512]{1,0:T(8,128)(2,1)S(1)}, bf16[3,128,512]{2,1,0:T(8,128)(2,1)S(1)}, bf16[4,512,512]{2,1,...) custom-call(s32[3]{0:T(128)S(1)} %pad_add_fusion.where, ...), custom_call_target="tpu_custom_call" | custom-call | flops 1500000000 | bytes 10485760 | tf_op jit(solution)/shard_map/pallas_call | solution.py:226
  38.8 2.8 %collective-permute-start.12 = (bf16[3,128,512]{2,1,0:T(8,128)(2,1)S(1)}, bf16[3,128,512]{2,1,0:T(8,128)(2,1)S(1)}, u32[]{:S(2)}, u32[]{:S(2)}) collective-permute-start(bf16[3,128,512]{2,1,0:T(8,128)(2,1)S(1)} %get-tuple-element.71), channel_id=1, source_target_pairs={{0,32},{32,0},{64,96},{96,64},{128,160},{160,128},{192,224},{224,1... | collective-permute-start | bytes 1179656 | tf_op jit(solution)/shard_map/ppermute | solution.py:44
  41.7 1.9 %collective-permute-start.17 = (bf16[128,640]{1,0:T(8,128)(2,1)S(1)}, bf16[128,640]{1,0:T(8,128)(2,1)S(1)}, u32[]{:S(2)}, u32[]{:S(2)}) collective-permute-start(bf16[128,640]{1,0:T(8,128)(2,1)S(1)} %get-tuple-element.75), channel_id=1, source_target_pairs={{0,28},{1,29},{2,30},{3,31},{4,0},{5,1},{6,2},{7,3},{8,4},{9,5},{1... | collective-permute-start | bytes 491528 | tf_op jit(solution)/shard_map/ppermute | solution.py:35
  43.6 1.3 %collective-permute-start.15 = (bf16[128,512]{1,0:T(8,128)(2,1)S(1)}, bf16[128,512]{1,0:T(8,128)(2,1)S(1)}, u32[]{:S(2)}, u32[]{:S(2)}) collective-permute-start(bf16[128,512]{1,0:T(8,128)(2,1)S(1)} %shard_map.118), channel_id=1, source_target_pairs={{0,2},{1,3},{2,0},{3,1},{4,6},{5,7},{6,4},{7,5},{8,10},{9,11},{10,... | collective-permute-start | bytes 393224 | tf_op jit(solution)/shard_map/ppermute | solution.py:31
  45.1 2.7 %collective-permute-start.16 = (bf16[128,512]{1,0:T(8,128)(2,1)S(1)}, bf16[128,512]{1,0:T(8,128)(2,1)S(1)}, u32[]{:S(2)}, u32[]{:S(2)}) collective-permute-start(bf16[128,512]{1,0:T(8,128)(2,1)S(1)} %get-tuple-element.74), channel_id=1, source_target_pairs={{0,3},{1,0},{2,1},{3,2},{4,7},{5,4},{6,5},{7,6},{8,11},{9,8},{10,9... | collective-permute-start | bytes 393224 | tf_op jit(solution)/shard_map/ppermute | solution.py:31
  47.8 1.8 %shard_map.120 = (bf16[128,640]{1,0:T(8,128)(2,1)S(1)}, bf16[128,640]{1,0:T(8,128)(2,1)S(1)}, bf16[128,640]{1,0:T(8,128)(2,1)S(1)}, bf16[128,768]{1,0:T(8,128)(2...) custom-call(s32[3]{0:T(128)S(1)} %pad_add_fusion.where, ...), custom_call_target="tpu_custom_call" | custom-call | flops 1500000000 | bytes 10485760 | tf_op jit(solution)/shard_map/pallas_call | solution.py:256
  49.7 2.6 %collective-permute-start.18 = (bf16[128,640]{1,0:T(8,128)(2,1)S(1)}, bf16[128,640]{1,0:T(8,128)(2,1)S(1)}, u32[]{:S(2)}, u32[]{:S(2)}) collective-permute-start(bf16[128,640]{1,0:T(8,128)(2,1)S(1)} %shard_map.121), channel_id=1, source_target_pairs={{0,24},{1,25},{2,26},{3,27},{4,28},{5,29},{6,30},{7,31},{8,0},{9,1... | collective-permute-start | bytes 491528 | tf_op jit(solution)/shard_map/ppermute | solution.py:35
  52.3 0.8 %collective-permute-done.13.p1 = bf16[128,512]{1,0:T(8,128)(2,1)S(1)} collective-permute-done((bf16[128,512]{1,0:T(8,128)(2,1)S(1)}, bf16[128,512]{1,0:T(8,128)(2,1)S(1)}, u32[]{:S(2)}, u32[]{:S(2)}) %collective-permute-start.13) | collective-permute-done | bytes 131104 | tf_op jit(solution)/shard_map/ppermute | solution.py:31
  53.1 0.7 shard_map.119
  53.8 5.8 %all-to-all-start = ((bf16[8,16,512]{2,1,0:T(8,128)(2,1)}), bf16[8,16,512]{2,1,0:T(8,128)(2,1)S(1)}, u32[]{:S(2)}, u32[]{:S(2)}) async-start(bf16[8,16,512]{2,1,0:T(8,128)(2,1)} %bitcast.8), calls=%async_computation | async-start | bytes 262144 | tf_op jit(solution)/shard_map/all_to_all | solution.py:325
  59.7 1.7 %collective-permute-start.21 = (bf16[128,768]{1,0:T(8,128)(2,1)S(1)}, bf16[128,768]{1,0:T(8,128)(2,1)S(1)}, u32[]{:S(2)}, u32[]{:S(2)}) collective-permute-start(bf16[128,768]{1,0:T(8,128)(2,1)S(1)} %get-tuple-element.84), channel_id=1, source_target_pairs={{0,2},{1,3},{2,0},{3,1},{4,6},{5,7},{6,4},{7,5},{8,10},{9,11},{10,... | collective-permute-start | bytes 589832 | tf_op jit(solution)/shard_map/ppermute | solution.py:31
  61.3 2.0 %collective-permute-start.22 = (bf16[128,768]{1,0:T(8,128)(2,1)S(1)}, bf16[128,768]{1,0:T(8,128)(2,1)S(1)}, u32[]{:S(2)}, u32[]{:S(2)}) collective-permute-start(bf16[128,768]{1,0:T(8,128)(2,1)S(1)} %get-tuple-element.85), channel_id=1, source_target_pairs={{0,3},{1,0},{2,1},{3,2},{4,7},{5,4},{6,5},{7,6},{8,11},{9,8},{10,9... | collective-permute-start | bytes 589832 | tf_op jit(solution)/shard_map/ppermute | solution.py:31
  63.3 2.7 %collective-permute-start.23 = (bf16[128,640]{1,0:T(8,128)(2,1)S(1)}, bf16[128,640]{1,0:T(8,128)(2,1)S(1)}, u32[]{:S(2)}, u32[]{:S(2)}) collective-permute-start(bf16[128,640]{1,0:T(8,128)(2,1)S(1)} %get-tuple-element.88), channel_id=1, source_target_pairs={{0,28},{1,29},{2,30},{3,31},{4,0},{5,1},{6,2},{7,3},{8,4},{9,5},{1... | collective-permute-start | bytes 491528 | tf_op jit(solution)/shard_map/ppermute | solution.py:35
  66.0 1.5 %all-to-all-done = bf16[8,16,512]{2,1,0:T(8,128)(2,1)S(1)} async-done(((bf16[8,16,512]{2,1,0:T(8,128)(2,1)}), bf16[8,16,512]{2,1,0:T(8,128)(2,1)S(1)}, u32[]{:S(2)}, u32[]{:S(2)}) %all-to-all-start) | async-done | bytes 131104 | tf_op jit(solution)/shard_map/all_to_all | solution.py:325
  67.5 1.4 %collective-permute-start.19 = (bf16[16,512]{1,0:T(8,128)(2,1)S(1)}, bf16[16,512]{1,0:T(8,128)(2,1)S(1)}, u32[]{:S(2)}, u32[]{:S(2)}) collective-permute-start(bf16[16,512]{1,0:T(8,128)(2,1)S(1)} %shard_map.123.refs_0_), channel_id=1, source_target_pairs={{0,64},{32,96},{64,0},{96,32},{128,192},{160,224},{192,128},{224,1... | collective-permute-start | bytes 49160 | tf_op jit(solution)/shard_map/ppermute | solution.py:40
  68.9 1.6 %collective-permute-done.19.refs_1_ = bf16[16,512]{1,0:T(8,128)(2,1)S(1)} collective-permute-done((bf16[16,512]{1,0:T(8,128)(2,1)S(1)}, bf16[16,512]{1,0:T(8,128)(2,1)S(1)}, u32[]{:S(2)}, u32[]{:S(2)}) %collective-permute-start.19) | collective-permute-done | bytes 16416 | tf_op jit(solution)/shard_map/ppermute | solution.py:40
  70.5 2.7 %collective-permute-start.24 = (bf16[16,512]{1,0:T(8,128)(2,1)S(1)}, bf16[16,512]{1,0:T(8,128)(2,1)S(1)}, u32[]{:S(2)}, u32[]{:S(2)}) collective-permute-start(bf16[16,512]{1,0:T(8,128)(2,1)S(1)} %shard_map.124.refs_0_), channel_id=1, source_target_pairs={{0,192},{32,224},{64,128},{96,160},{128,64},{160,96},{192,0},{224,... | collective-permute-start | bytes 49160 | tf_op jit(solution)/shard_map/ppermute | solution.py:40
  73.3 0.7 shard_map.125
  74.0 0.8 shard_map.126
  74.8 3.9 %collective-permute-start.25 = (f32[16,512]{1,0:T(8,128)S(1)}, f32[16,512]{1,0:T(8,128)S(1)}, u32[]{:S(2)}, u32[]{:S(2)}) collective-permute-start(f32[16,512]{1,0:T(8,128)S(1)} %shard_map.127), channel_id=1, source_target_pairs={{0,32},{32,0},{64,96},{96,64},{128,160},{160,128},{192,224},{224,1... | collective-permute-start | bytes 98312 | tf_op jit(solution)/shard_map/ppermute | solution.py:44
  78.7 0.9 %collective-permute-done.25 = f32[16,512]{1,0:T(8,128)S(1)} collective-permute-done((f32[16,512]{1,0:T(8,128)S(1)}, f32[16,512]{1,0:T(8,128)S(1)}, u32[]{:S(2)}, u32[]{:S(2)}) %collective-permute-start.25) | collective-permute-done | bytes 32800 | tf_op jit(solution)/shard_map/ppermute | solution.py:44
  79.6 0.6 broadcast_select_fusion
  (36 shorter events, 0.7 us)
Async XLA Ops:
  0.6 18.3 %copy-start.1 = (bf16[512,512]{1,0:T(8,128)(2,1)S(1)}, bf16[512,512]{1,0:T(8,128)(2,1)}, u32[]{:S(2)}) copy-start(bf16[512,512]{1,0:T(8,128)(2,1)} %wv.1) | copy-start | bytes 1572868
  0.6 18.3 %copy-start = (bf16[512,512]{1,0:T(8,128)(2,1)S(1)}, bf16[512,512]{1,0:T(8,128)(2,1)}, u32[]{:S(2)}) copy-start(bf16[512,512]{1,0:T(8,128)(2,1)} %wk.1) | copy-start | bytes 1572868
  2.7 20.4 %copy-start.3 = (bf16[64,640]{1,0:T(8,128)(2,1)S(1)}, bf16[64,640]{1,0:T(8,128)(2,1)}, u32[]{:S(2)}) copy-start(bf16[64,640]{1,0:T(8,128)(2,1)} %get-tuple-element.50.refs_0_) | copy-start | bytes 245764
  2.7 20.4 %copy-start.4 = (bf16[64,640]{1,0:T(8,128)(2,1)S(1)}, bf16[64,640]{1,0:T(8,128)(2,1)}, u32[]{:S(2)}) copy-start(bf16[64,640]{1,0:T(8,128)(2,1)} %get-tuple-element.51.refs_1_) | copy-start | bytes 245764
  2.7 8.9 %collective-permute-start.2 = (bf16[64,640]{1,0:T(8,128)(2,1)}, bf16[64,640]{1,0:T(8,128)(2,1)S(1)}, u32[]{:S(2)}, u32[]{:S(2)}) collective-permute-start(bf16[64,640]{1,0:T(8,128)(2,1)} %get-tuple-element.50.refs_0_), channel_id=1, source_target_pairs={{0,4},{1,5},{2,6},{3,7},{4,8},{5,9},{6,10},{7,11},{8,12},{9,13},{1... | collective-permute-start | bytes 245768 | tf_op jit(solution)/shard_map/ppermute | solution.py:35
  5.2 8.1 %collective-permute-start.3 = (bf16[64,640]{1,0:T(8,128)(2,1)}, bf16[64,640]{1,0:T(8,128)(2,1)S(1)}, u32[]{:S(2)}, u32[]{:S(2)}) collective-permute-start(bf16[64,640]{1,0:T(8,128)(2,1)} %get-tuple-element.51.refs_1_), channel_id=1, source_target_pairs={{0,4},{1,5},{2,6},{3,7},{4,8},{5,9},{6,10},{7,11},{8,12},{9,13},{1... | collective-permute-start | bytes 245768 | tf_op jit(solution)/shard_map/ppermute | solution.py:35
  6.9 16.7 %collective-permute-start.1 = (bf16[1296,128]{1,0:T(8,128)(2,1)}, bf16[1296,128]{1,0:T(8,128)(2,1)S(1)}, u32[]{:S(2)}, u32[]{:S(2)}) collective-permute-start(bf16[1296,128]{1,0:T(8,128)(2,1)} %get-tuple-element.52.q0), channel_id=1, source_target_pairs={{0,2},{1,3},{2,0},{3,1},{4,6},{5,7},{6,4},{7,5},{8,10},{9,11},{10,... | collective-permute-start | bytes 995336 | tf_op jit(solution)/shard_map/ppermute | solution.py:31
  9.6 15.0 %collective-permute-start = (bf16[1296,128]{1,0:T(8,128)(2,1)}, bf16[1296,128]{1,0:T(8,128)(2,1)S(1)}, u32[]{:S(2)}, u32[]{:S(2)}) collective-permute-start(bf16[1296,128]{1,0:T(8,128)(2,1)} %get-tuple-element.52.q0), channel_id=1, source_target_pairs={{0,3},{1,0},{2,1},{3,2},{4,7},{5,4},{6,5},{7,6},{8,11},{9,8},{10,9... | collective-permute-start | bytes 995336 | tf_op jit(solution)/shard_map/ppermute | solution.py:31
  11.5 4.8 %collective-permute-start.5 = (bf16[64,640]{1,0:T(8,128)(2,1)S(1)}, bf16[64,640]{1,0:T(8,128)(2,1)S(1)}, u32[]{:S(2)}, u32[]{:S(2)}) collective-permute-start(bf16[64,640]{1,0:T(8,128)(2,1)S(1)} %collective-permute-done.2.refs_0_), channel_id=1, source_target_pairs={{0,4},{1,5},{2,6},{3,7},{4,8},{5,9},{6,10},{7,11},{8,12},{9,13},{1... | collective-permute-start | bytes 245768 | tf_op jit(solution)/shard_map/ppermute | solution.py:35
  13.3 5.0 %collective-permute-start.6 = (bf16[64,640]{1,0:T(8,128)(2,1)S(1)}, bf16[64,640]{1,0:T(8,128)(2,1)S(1)}, u32[]{:S(2)}, u32[]{:S(2)}) collective-permute-start(bf16[64,640]{1,0:T(8,128)(2,1)S(1)} %collective-permute-done.3.refs_1_), channel_id=1, source_target_pairs={{0,4},{1,5},{2,6},{3,7},{4,8},{5,9},{6,10},{7,11},{8,12},{9,13},{1... | collective-permute-start | bytes 245768 | tf_op jit(solution)/shard_map/ppermute | solution.py:35
  15.0 9.5 %collective-permute-start.4 = (bf16[1296,128]{1,0:T(8,128)(2,1)}, bf16[1296,128]{1,0:T(8,128)(2,1)S(1)}, u32[]{:S(2)}, u32[]{:S(2)}) collective-permute-start(bf16[1296,128]{1,0:T(8,128)(2,1)} %get-tuple-element.52.q0), channel_id=1, source_target_pairs={{0,1},{1,2},{2,3},{3,0},{4,5},{5,6},{6,7},{7,4},{8,9},{9,10},{10,1... | collective-permute-start | bytes 995336 | tf_op jit(solution)/shard_map/ppermute | solution.py:31
  16.3 4.5 %collective-permute-start.7 = (bf16[64,640]{1,0:T(8,128)(2,1)S(1)}, bf16[64,640]{1,0:T(8,128)(2,1)S(1)}, u32[]{:S(2)}, u32[]{:S(2)}) collective-permute-start(bf16[64,640]{1,0:T(8,128)(2,1)S(1)} %collective-permute-done.5.refs_2_), channel_id=1, source_target_pairs={{0,4},{1,5},{2,6},{3,7},{4,8},{5,9},{6,10},{7,11},{8,12},{9,13},{1... | collective-permute-start | bytes 245768 | tf_op jit(solution)/shard_map/ppermute | solution.py:35
  18.3 4.8 %collective-permute-start.8 = (bf16[64,640]{1,0:T(8,128)(2,1)S(1)}, bf16[64,640]{1,0:T(8,128)(2,1)S(1)}, u32[]{:S(2)}, u32[]{:S(2)}) collective-permute-start(bf16[64,640]{1,0:T(8,128)(2,1)S(1)} %collective-permute-done.6.refs_3_), channel_id=1, source_target_pairs={{0,4},{1,5},{2,6},{3,7},{4,8},{5,9},{6,10},{7,11},{8,12},{9,13},{1... | collective-permute-start | bytes 245768 | tf_op jit(solution)/shard_map/ppermute | solution.py:35
  19.0 5.6 %copy-start.2 = (bf16[1296,128]{1,0:T(8,128)(2,1)S(1)}, bf16[1296,128]{1,0:T(8,128)(2,1)}, u32[]{:S(2)}) copy-start(bf16[1296,128]{1,0:T(8,128)(2,1)} %get-tuple-element.52.q0) | copy-start | bytes 995332
  27.7 4.4 %collective-permute-start.11 = (f32[16,512]{1,0:T(8,128)S(1)}, f32[16,512]{1,0:T(8,128)S(1)}, u32[]{:S(2)}, u32[]{:S(2)}) collective-permute-start(f32[16,512]{1,0:T(8,128)S(1)} %get-tuple-element.65.t0), channel_id=1, source_target_pairs={{0,3},{1,0},{2,1},{3,2},{4,7},{5,4},{6,5},{7,6},{8,11},{9,8},{10,9... | collective-permute-start | bytes 98312 | tf_op jit(solution)/shard_map/ppermute | solution.py:31
  31.1 4.3 %collective-permute-start.10 = (f32[16,512]{1,0:T(8,128)S(1)}, f32[16,512]{1,0:T(8,128)S(1)}, u32[]{:S(2)}, u32[]{:S(2)}) collective-permute-start(f32[16,512]{1,0:T(8,128)S(1)} %get-tuple-element.65.t0), channel_id=1, source_target_pairs={{0,2},{1,3},{2,0},{3,1},{4,6},{5,7},{6,4},{7,5},{8,10},{9,11},{10,... | collective-permute-start | bytes 98312 | tf_op jit(solution)/shard_map/ppermute | solution.py:31
  31.6 4.1 %collective-permute-start.9 = (f32[16,512]{1,0:T(8,128)S(1)}, f32[16,512]{1,0:T(8,128)S(1)}, u32[]{:S(2)}, u32[]{:S(2)}) collective-permute-start(f32[16,512]{1,0:T(8,128)S(1)} %get-tuple-element.65.t0), channel_id=1, source_target_pairs={{0,1},{1,2},{2,3},{3,0},{4,5},{5,6},{6,7},{7,4},{8,9},{9,10},{10,1... | collective-permute-start | bytes 98312 | tf_op jit(solution)/shard_map/ppermute | solution.py:31
  38.8 6.1 %collective-permute-start.12 = (bf16[3,128,512]{2,1,0:T(8,128)(2,1)S(1)}, bf16[3,128,512]{2,1,0:T(8,128)(2,1)S(1)}, u32[]{:S(2)}, u32[]{:S(2)}) collective-permute-start(bf16[3,128,512]{2,1,0:T(8,128)(2,1)S(1)} %get-tuple-element.71), channel_id=1, source_target_pairs={{0,32},{32,0},{64,96},{96,64},{128,160},{160,128},{192,224},{224,1... | collective-permute-start | bytes 1179656 | tf_op jit(solution)/shard_map/ppermute | solution.py:44
  41.6 2.0 %collective-permute-start.14 = (bf16[128,512]{1,0:T(8,128)(2,1)S(1)}, bf16[128,512]{1,0:T(8,128)(2,1)S(1)}, u32[]{:S(2)}, u32[]{:S(2)}) collective-permute-start(bf16[128,512]{1,0:T(8,128)(2,1)S(1)} %get-tuple-element.73), channel_id=1, source_target_pairs={{0,32},{32,0},{64,96},{96,64},{128,160},{160,128},{192,224},{224,1... | collective-permute-start | bytes 393224 | tf_op jit(solution)/shard_map/ppermute | solution.py:44
  41.7 7.9 %collective-permute-start.17 = (bf16[128,640]{1,0:T(8,128)(2,1)S(1)}, bf16[128,640]{1,0:T(8,128)(2,1)S(1)}, u32[]{:S(2)}, u32[]{:S(2)}) collective-permute-start(bf16[128,640]{1,0:T(8,128)(2,1)S(1)} %get-tuple-element.75), channel_id=1, source_target_pairs={{0,28},{1,29},{2,30},{3,31},{4,0},{5,1},{6,2},{7,3},{8,4},{9,5},{1... | collective-permute-start | bytes 491528 | tf_op jit(solution)/shard_map/ppermute | solution.py:35
  43.6 8.6 %collective-permute-start.15 = (bf16[128,512]{1,0:T(8,128)(2,1)S(1)}, bf16[128,512]{1,0:T(8,128)(2,1)S(1)}, u32[]{:S(2)}, u32[]{:S(2)}) collective-permute-start(bf16[128,512]{1,0:T(8,128)(2,1)S(1)} %shard_map.118), channel_id=1, source_target_pairs={{0,2},{1,3},{2,0},{3,1},{4,6},{5,7},{6,4},{7,5},{8,10},{9,11},{10,... | collective-permute-start | bytes 393224 | tf_op jit(solution)/shard_map/ppermute | solution.py:31
  45.0 8.1 %collective-permute-start.13 = (bf16[128,512]{1,0:T(8,128)(2,1)S(1)}, bf16[128,512]{1,0:T(8,128)(2,1)S(1)}, u32[]{:S(2)}, u32[]{:S(2)}) collective-permute-start(bf16[128,512]{1,0:T(8,128)(2,1)S(1)} %get-tuple-element.72), channel_id=1, source_target_pairs={{0,1},{1,2},{2,3},{3,0},{4,5},{5,6},{6,7},{7,4},{8,9},{9,10},{10,1... | collective-permute-start | bytes 393224 | tf_op jit(solution)/shard_map/ppermute | solution.py:31
  45.1 8.0 %collective-permute-start.16 = (bf16[128,512]{1,0:T(8,128)(2,1)S(1)}, bf16[128,512]{1,0:T(8,128)(2,1)S(1)}, u32[]{:S(2)}, u32[]{:S(2)}) collective-permute-start(bf16[128,512]{1,0:T(8,128)(2,1)S(1)} %get-tuple-element.74), channel_id=1, source_target_pairs={{0,3},{1,0},{2,1},{3,2},{4,7},{5,4},{6,5},{7,6},{8,11},{9,8},{10,9... | collective-permute-start | bytes 393224 | tf_op jit(solution)/shard_map/ppermute | solution.py:31
  49.7 16.3 %collective-permute-start.18 = (bf16[128,640]{1,0:T(8,128)(2,1)S(1)}, bf16[128,640]{1,0:T(8,128)(2,1)S(1)}, u32[]{:S(2)}, u32[]{:S(2)}) collective-permute-start(bf16[128,640]{1,0:T(8,128)(2,1)S(1)} %shard_map.121), channel_id=1, source_target_pairs={{0,24},{1,25},{2,26},{3,27},{4,28},{5,29},{6,30},{7,31},{8,0},{9,1... | collective-permute-start | bytes 491528 | tf_op jit(solution)/shard_map/ppermute | solution.py:35
  53.8 13.7 %all-to-all-start = ((bf16[8,16,512]{2,1,0:T(8,128)(2,1)}), bf16[8,16,512]{2,1,0:T(8,128)(2,1)S(1)}, u32[]{:S(2)}, u32[]{:S(2)}) async-start(bf16[8,16,512]{2,1,0:T(8,128)(2,1)} %bitcast.8), calls=%async_computation | async-start | bytes 262144 | tf_op jit(solution)/shard_map/all_to_all | solution.py:325
  59.6 13.6 %collective-permute-start.20 = (bf16[128,768]{1,0:T(8,128)(2,1)S(1)}, bf16[128,768]{1,0:T(8,128)(2,1)S(1)}, u32[]{:S(2)}, u32[]{:S(2)}) collective-permute-start(bf16[128,768]{1,0:T(8,128)(2,1)S(1)} %get-tuple-element.83), channel_id=1, source_target_pairs={{0,1},{1,2},{2,3},{3,0},{4,5},{5,6},{6,7},{7,4},{8,9},{9,10},{10,1... | collective-permute-start | bytes 589832 | tf_op jit(solution)/shard_map/ppermute | solution.py:31
  59.7 13.6 %collective-permute-start.21 = (bf16[128,768]{1,0:T(8,128)(2,1)S(1)}, bf16[128,768]{1,0:T(8,128)(2,1)S(1)}, u32[]{:S(2)}, u32[]{:S(2)}) collective-permute-start(bf16[128,768]{1,0:T(8,128)(2,1)S(1)} %get-tuple-element.84), channel_id=1, source_target_pairs={{0,2},{1,3},{2,0},{3,1},{4,6},{5,7},{6,4},{7,5},{8,10},{9,11},{10,... | collective-permute-start | bytes 589832 | tf_op jit(solution)/shard_map/ppermute | solution.py:31
  61.3 11.9 %collective-permute-start.22 = (bf16[128,768]{1,0:T(8,128)(2,1)S(1)}, bf16[128,768]{1,0:T(8,128)(2,1)S(1)}, u32[]{:S(2)}, u32[]{:S(2)}) collective-permute-start(bf16[128,768]{1,0:T(8,128)(2,1)S(1)} %get-tuple-element.85), channel_id=1, source_target_pairs={{0,3},{1,0},{2,1},{3,2},{4,7},{5,4},{6,5},{7,6},{8,11},{9,8},{10,9... | collective-permute-start | bytes 589832 | tf_op jit(solution)/shard_map/ppermute | solution.py:31
  63.3 10.7 %collective-permute-start.23 = (bf16[128,640]{1,0:T(8,128)(2,1)S(1)}, bf16[128,640]{1,0:T(8,128)(2,1)S(1)}, u32[]{:S(2)}, u32[]{:S(2)}) collective-permute-start(bf16[128,640]{1,0:T(8,128)(2,1)S(1)} %get-tuple-element.88), channel_id=1, source_target_pairs={{0,28},{1,29},{2,30},{3,31},{4,0},{5,1},{6,2},{7,3},{8,4},{9,5},{1... | collective-permute-start | bytes 491528 | tf_op jit(solution)/shard_map/ppermute | solution.py:35
  67.5 3.0 %collective-permute-start.19 = (bf16[16,512]{1,0:T(8,128)(2,1)S(1)}, bf16[16,512]{1,0:T(8,128)(2,1)S(1)}, u32[]{:S(2)}, u32[]{:S(2)}) collective-permute-start(bf16[16,512]{1,0:T(8,128)(2,1)S(1)} %shard_map.123.refs_0_), channel_id=1, source_target_pairs={{0,64},{32,96},{64,0},{96,32},{128,192},{160,224},{192,128},{224,1... | collective-permute-start | bytes 49160 | tf_op jit(solution)/shard_map/ppermute | solution.py:40
  70.5 4.3 %collective-permute-start.24 = (bf16[16,512]{1,0:T(8,128)(2,1)S(1)}, bf16[16,512]{1,0:T(8,128)(2,1)S(1)}, u32[]{:S(2)}, u32[]{:S(2)}) collective-permute-start(bf16[16,512]{1,0:T(8,128)(2,1)S(1)} %shard_map.124.refs_0_), channel_id=1, source_target_pairs={{0,192},{32,224},{64,128},{96,160},{128,64},{160,96},{192,0},{224,... | collective-permute-start | bytes 49160 | tf_op jit(solution)/shard_map/ppermute | solution.py:40
  74.8 4.8 %collective-permute-start.25 = (f32[16,512]{1,0:T(8,128)S(1)}, f32[16,512]{1,0:T(8,128)S(1)}, u32[]{:S(2)}, u32[]{:S(2)}) collective-permute-start(f32[16,512]{1,0:T(8,128)S(1)} %shard_map.127), channel_id=1, source_target_pairs={{0,32},{32,0},{64,96},{96,64},{128,160},{160,128},{192,224},{224,1... | collective-permute-start | bytes 98312 | tf_op jit(solution)/shard_map/ppermute | solution.py:44

commit v5 on v4

--- a/solution.py
+++ b/solution.py
@@ -124,21 +124,20 @@
     return kc, vs, latents, marks, *weights
 
 
-def stats_kernel(where, q0, q1, q2, q3, kc0, kc1, vs0, vs1, marks0, marks1, qc, gs, es, dps, stats, bias, qid):
+def columns(blocks, first):
+    return jnp.concatenate([q[first:first + 128, :] for q in blocks], axis=0)
+
+
+def queries_of(blocks, h):
+    return jnp.concatenate([columns(blocks, h * 128), columns(blocks, 1024 + h // 2 * 128)], axis=1)
+
+
+def stats_kernel(where, q0, q1, q2, q3, kc0, kc1, vs0, vs1, marks0, marks1, es, dps, stats, bias):
     xi, zi = where[0], where[1]
-    for s, block in enumerate((q0, q1, q2, q3)):
-        at = pl.ds(pl.multiple_of(((xi + s) & 3) * 128, 128), 128)
-
-        def rows(first, count=128):
-            return block[first:first + count, :]
-
-        for h in range(HEADS):
-            qc[h, at, 0:128] = rows(h * 128)
-            qc[h, at, 128:256] = rows(1024 + h // 2 * 128)
-            gs[h, at, :] = rows(512 + h * 128)
-        qid[:, at] = rows(1280, 16)
-    q_marks = qid[0:1, :].astype(F32)
-    q_pos = zi * QROWS + lax.broadcasted_iota(jnp.int32, (128, QROWS), 1)
+    blocks = (q0, q1, q2, q3)
+    q_marks = jnp.concatenate([q[1280:1296, :] for q in blocks], axis=1)[0:1].astype(F32)
+    lane = lax.broadcasted_iota(jnp.int32, (128, QROWS), 1)
+    q_pos = zi * QROWS + ((xi + (lane >> 7)) & 3) * 128 + (lane & 127)
     for j in range(REACH):
         at = slice(j * 128, j * 128 + 128)
         first = ((zi - ORDER[j]) & (Z - 1)) * QROWS + xi * 128
@@ -148,11 +147,13 @@
     for h in range(HEADS):
         for b in range(0, QROWS, 256):
             sl = slice(b, b + 256)
+            pair = blocks[b // 128:b // 128 + 2]
+            qc, gs = queries_of(pair, h), columns(pair, 512 + h * 128)
             parts = []
             for n, (kc, vs) in enumerate(((kc0, vs0), (kc1, vs1))):
                 at = slice(n * HALF, (n + 1) * HALF)
-                s = lax.dot_general(kc[h], qc[h, sl, :], NT, preferred_element_type=F32) * SCALE + bias[at, sl]
-                dp = lax.dot_general(vs[h], gs[h, sl, :], NT, preferred_element_type=F32)
+                s = lax.dot_general(kc[h], qc, NT, preferred_element_type=F32) * SCALE + bias[at, sl]
+                dp = lax.dot_general(vs[h], gs, NT, preferred_element_type=F32)
                 dps[h, at, sl] = dp
                 parts.append((at, s, dp))
             m = jnp.maximum(*[jnp.max(s, axis=0, keepdims=True) for _, s, _ in parts])
@@ -168,28 +169,28 @@
     stats[12:16, :] = jnp.zeros((4, QROWS), F32)
 
 
-def run_stats(where, qs, *keys):
+def run_stats(where, *mats):
     sds = jax.ShapeDtypeStruct
     return call(
-        stats_kernel,
-        (sds((4, QROWS, 256), BF), sds((4, QROWS, 128), BF),
-         sds((4, KROWS, QROWS), F32), sds((4, KROWS, QROWS), F32), sds((16, QROWS), F32)),
-        1, 10, scratch=[pltpu.VMEM((KROWS, QROWS), F32), pltpu.VMEM((16, QROWS), BF)],
-        flops=1_000_000_000, nbytes=8 << 20,
-    )(where, *qs, *keys)
-
-
-def weight_kernel(where, t0, t1, t2, t3, qc, gs, es, dps, latents0, latents1, wk, wv, w_keep, w_far, w_send, ds, dkv, tail, d3,
+        stats_kernel, (sds((4, KROWS, QROWS), F32), sds((4, KROWS, QROWS), F32), sds((16, QROWS), F32)),
+        1, 10, scratch=[pltpu.VMEM((KROWS, QROWS), F32)], flops=1_000_000_000, nbytes=8 << 20,
+    )(where, *mats)
+
+
+def weight_kernel(where, t0, t1, t2, t3, q0, q1, q2, q3, es, dps, latents0, latents1, wk, wv, w_keep, w_far, w_send, ds, dkv, tail, d3,
                   p_scr, w_scr):
     xi, core = where[0], where[2]
-    tops = [t[0:4, :] for t in (t0, t1, t2, t3)]
+    blocks = (q0, q1, q2, q3)
+    ts = [t[...] if s == 0 else jnp.concatenate([t[:, 512 - s * 128:], t[:, :512 - s * 128]], axis=1)
+          for s, t in enumerate((t0, t1, t2, t3))]
+    tops = [t[0:4] for t in ts]
     top = functools.reduce(jnp.maximum, tops)
     total = jnp.zeros((4, QROWS), F32)
     cross = jnp.zeros((4, QROWS), F32)
-    for t, m in zip((t0, t1, t2, t3), tops):
+    for t, m in zip(ts, tops):
         f = jnp.exp(m - top)
-        total = total + f * t[4:8, :]
-        cross = cross + f * t[8:12, :]
+        total = total + f * t[4:8]
+        cross = cross + f * t[8:12]
     inv = 1.0 / total
     delta = cross * inv
     scaled = jnp.exp(tops[0] - top) * inv
@@ -201,8 +202,8 @@
             p_scr[h % 2, :, sl] = p.astype(BF)
             ds[h, :, sl] = (p * (dps[h, :, sl] - delta[h:h + 1, sl]) * SCALE).astype(BF)
         cols = slice(h * 128, (h + 1) * 128)
-        dkv[1, :, cols] = jnp.dot(p_scr[h % 2], gs[h], preferred_element_type=F32).astype(BF)
-        dk = jnp.dot(ds[h], qc[h], preferred_element_type=F32)
+        dkv[1, :, cols] = jnp.dot(p_scr[h % 2], columns(blocks, 512 + h * 128), preferred_element_type=F32).astype(BF)
+        dk = jnp.dot(ds[h], queries_of(blocks, h), preferred_element_type=F32)
         dkv[0, :, cols] = dk[:, :128].astype(BF)
         rope_grad[h % 2] = rope_grad[h % 2] + dk[:, 128:]
     for out, which in ((w_scr, 1 - core), (w_keep, core)):
@@ -227,12 +228,11 @@
         weight_kernel,
         (sds((4, 128, 512), BF), sds((128, 512), BF), sds((3, 128, 512), BF), sds((4, KROWS, QROWS), BF), sds((2, KROWS, 512), BF),
          sds((KROWS, 128), BF), sds((128, 640), BF)),
-        1, 12, scratch=[pltpu.VMEM((2, KROWS, QROWS), BF), pltpu.VMEM((4, 128, 512), BF)], flops=1_500_000_000, nbytes=10 << 20,
+        1, 14, scratch=[pltpu.VMEM((2, KROWS, QROWS), BF), pltpu.VMEM((4, 128, 512), BF)], flops=1_500_000_000, nbytes=10 << 20,
     )(where, *ts, *mats)
 
 
 def grads_kernel(where, ds, dkv, tail, kc0, kc1, wk, wv, d0, d1, d2, o0, o1, o2, o3, dq):
-    xi = where[0]
     near = slice(0, 3 * ROWS)
     lat = (lax.dot_general(dkv[0, near], wk[...], NT, preferred_element_type=F32)
            + lax.dot_general(dkv[1, near], wv[...], NT, preferred_element_type=F32)).astype(BF)
@@ -248,7 +248,7 @@
             pair = pair + dqh[:, 128:]
         dq[:, 512 + p * 128:640 + p * 128] = pair.astype(BF)
     for s, o in enumerate((o0, o1, o2, o3)):
-        o[...] = dq[pl.ds(pl.multiple_of(((xi + s) & 3) * 128, 128), 128), :]
+        o[...] = dq[s * 128:(s + 1) * 128, :]
 
 
 def run_grads(where, ds, dkv, tail, kc0, kc1, wk, wv):
@@ -312,9 +312,9 @@
     later, _ = lax.optimization_barrier((q, c1))
     qs = (q, x_shift(q, -1), x_shift(q, 2), x_shift(later, 1))
     kc1, vs1, latents1, marks1 = run_keys(c + c3, wk, wv, False)
-    qc, gs, es, dps, stats = run_stats(where, qs, kc0, kc1, vs0, vs1, marks0, marks1)
-    ts = (stats, x_shift(stats, 1), x_shift(stats, 2), x_shift(stats, -1))
-    w_keep, w_far, w_send, ds, dkv, tail, d3 = run_weight(where, ts, qc, gs, es, dps, latents0, latents1, wk, wv)
+    es, dps, stats = run_stats(where, *qs, kc0, kc1, vs0, vs1, marks0, marks1)
+    ts = (stats, x_shift(stats, -1), x_shift(stats, 2), x_shift(stats, 1))
+    w_keep, w_far, w_send, ds, dkv, tail, d3 = run_weight(where, ts, *qs, es, dps, latents0, latents1, wk, wv)
     w_far, near = core_swap(w_far), core_swap(w_send)
     d0, d1, d2, o0, o1, o2, o3 = run_grads(where, ds, dkv, tail, kc0, kc1, wk, wv)
     sds = jax.ShapeDtypeStruct
@@ -329,10 +329,10 @@
     w = call(sum_z_kernel, sds((16, 512), BF), 0, 1, nbytes=1 << 18)(w)
     w = add_up(w, y_pair(w, False))
     other = y_pair(w, True)
-    grad_nope, grad_rope = call(query_kernel, (sds((128, 512), BF), sds((128, 256), BF)), 0, 4, nbytes=1 << 20)(
+    grad_nope, grad_rope = call(query_kernel, (sds((128, 512), BF), sds((128, 256), BF)), 0, 4, flops=1_000_000_000, nbytes=1 << 20)(
         o0, x_shift(o1, 1), x_shift(o2, 2), x_shift(o3, -1))
     grad_latent = call(latent_kernel, sds((576, 128), BF), 0, 2, nbytes=1 << 20)(d, z_shift(d1, -1))
-    w, grad_nope, grad_latent = lax.optimization_barrier((w, grad_nope, grad_latent))
+    w, grad_latent = lax.optimization_barrier((w, grad_latent))
     w = add_up(w, other, dtype=F32)
     other = core_swap(w)
     grad_key = jnp.where(core == 0, w, other)

time: 80.4 us -> 79.5 us (0.989)
  waiting for transfers between devices: 18.1 us -> 16.7 us
    ppermute x12, waiting for transfers between devices: 5.74 us -> 4.83 us  [x_shift(): lax.ppermute(v, 'ctx', [(i, i // X * X + (i % X + s) % X) for i in range(...]
where the time goes in v5:
time: 79.5 us; the launch traced here: 79.3 us
  starting transfers between devices  47.8 us (60%)
  waiting for transfers between devices  16.7 us (21%)
  Pallas kernels  13.2 us (17%)
  between operations  0.81 us (1%)
    ppermute x12, starting transfers between devices, x_shift(): lax.ppermute(v, 'ctx', [(i, i // X * X + (i % X + s) % X) for i in range(...  16.8 us
    ppermute x9, starting transfers between devices, z_shift(): lax.ppermute(v, 'ctx', [(i, (i + s * X) % (Z * X)) for i in range(Z * X)])  14.3 us
    ppermute x9, waiting for transfers between devices, z_shift(): lax.ppermute(v, 'ctx', [(i, (i + s * X) % (Z * X)) for i in range(Z * X)])  8.38 us
    ppermute x3, starting transfers between devices, core_swap(): return lax.ppermute(v, 'dp', [(i, i ^ 1) for i in range(2 * Y)])  6.8 us
    all_to_all x1, starting transfers between devices, body(): lax.all_to_all(w, 'ctx', 0, 0, tiled=True, axis_index_groups=[[z * X + x...  5.84 us
    ppermute x12, waiting for transfers between devices, x_shift(): lax.ppermute(v, 'ctx', [(i, i // X * X + (i % X + s) % X) for i in range(...  4.83 us
    ppermute x2, starting transfers between devices, y_pair(): return lax.ppermute(v, 'dp', pairs)  4.11 us
    pallas_call x1, Pallas kernels, run_weight(): call(weight_kernel, (sds((4, 128, 512), BF), sds((128, 512), BF), sds((3,...  3.07 us
  transfers between devices with their start and end apart: 27, of which 14 were waited for; matrix products, arithmetic and copies ran while one was open for 0% of the time, Pallas kernels for 7%

profile of v5, /device:TPU:1, one launch (start us, length us, event | category | flops | bytes accessed | tf_op | source)
XLA Modules:
  0.0 79.3 jit_solution(7819708435370707425)
XLA Ops:
  0.7 2.0 %shard_map.110 = (bf16[1296,128]{1,0:T(8,128)(2,1)}, bf16[64,640]{1,0:T(8,128)(2,1)}, bf16[64,640]{1,0:T(8,128)(2,1)}) custom-call(bf16[128,512]{1,0:T(8,128)(2,1)} %bitcast.19, bf16[128,256]{1,0:T(8,128)(2,1)} %bitcast.21, bf16[128,512]{1,0:T(8,128)(2,1)} %bitcast.20, bf16[576,128]{1,0:T(8,128)(2,1)} %bitcast.18, s32[1,128]{1,0:T(1,128)} %ids.1), custom_call_target="tpu_custom_call" | custom-call | bytes 1048576 | tf_op jit(solution)/shard_map/pallas_call | solution.py:84
  2.7 2.5 %collective-permute-start.2 = (bf16[64,640]{1,0:T(8,128)(2,1)}, bf16[64,640]{1,0:T(8,128)(2,1)S(1)}, u32[]{:S(2)}, u32[]{:S(2)}) collective-permute-start(bf16[64,640]{1,0:T(8,128)(2,1)} %get-tuple-element.47.refs_0_), channel_id=1, source_target_pairs={{0,4},{1,5},{2,6},{3,7},{4,8},{5,9},{6,10},{7,11},{8,12},{9,13},{1... | collective-permute-start | bytes 245768 | tf_op jit(solution)/shard_map/ppermute | solution.py:35
  5.2 1.6 %collective-permute-start.3 = (bf16[64,640]{1,0:T(8,128)(2,1)}, bf16[64,640]{1,0:T(8,128)(2,1)S(1)}, u32[]{:S(2)}, u32[]{:S(2)}) collective-permute-start(bf16[64,640]{1,0:T(8,128)(2,1)} %get-tuple-element.48.refs_1_), channel_id=1, source_target_pairs={{0,4},{1,5},{2,6},{3,7},{4,8},{5,9},{6,10},{7,11},{8,12},{9,13},{1... | collective-permute-start | bytes 245768 | tf_op jit(solution)/shard_map/ppermute | solution.py:35
  6.9 2.7 %collective-permute-start.1 = (bf16[1296,128]{1,0:T(8,128)(2,1)}, bf16[1296,128]{1,0:T(8,128)(2,1)S(1)}, u32[]{:S(2)}, u32[]{:S(2)}) collective-permute-start(bf16[1296,128]{1,0:T(8,128)(2,1)} %get-tuple-element.49.q0), channel_id=1, source_target_pairs={{0,2},{1,3},{2,0},{3,1},{4,6},{5,7},{6,4},{7,5},{8,10},{9,11},{10,... | collective-permute-start | bytes 995336 | tf_op jit(solution)/shard_map/ppermute | solution.py:31
  9.6 0.9 %collective-permute-start = (bf16[1296,128]{1,0:T(8,128)(2,1)}, bf16[1296,128]{1,0:T(8,128)(2,1)S(1)}, u32[]{:S(2)}, u32[]{:S(2)}) collective-permute-start(bf16[1296,128]{1,0:T(8,128)(2,1)} %get-tuple-element.49.q0), channel_id=1, source_target_pairs={{0,3},{1,0},{2,1},{3,2},{4,7},{5,4},{6,5},{7,6},{8,11},{9,8},{10,9... | collective-permute-start | bytes 995336 | tf_op jit(solution)/shard_map/ppermute | solution.py:31
  10.5 1.1 %collective-permute-done.2.refs_0_ = bf16[64,640]{1,0:T(8,128)(2,1)S(1)} collective-permute-done((bf16[64,640]{1,0:T(8,128)(2,1)}, bf16[64,640]{1,0:T(8,128)(2,1)S(1)}, u32[]{:S(2)}, u32[]{:S(2)}) %collective-permute-start.2) | collective-permute-done | bytes 81952 | tf_op jit(solution)/shard_map/ppermute | solution.py:35
  11.5 0.6 collective-permute-start.5
  12.1 1.2 %collective-permute-done.3.refs_1_ = bf16[64,640]{1,0:T(8,128)(2,1)S(1)} collective-permute-done((bf16[64,640]{1,0:T(8,128)(2,1)}, bf16[64,640]{1,0:T(8,128)(2,1)S(1)}, u32[]{:S(2)}, u32[]{:S(2)}) %collective-permute-start.3) | collective-permute-done | bytes 81952 | tf_op jit(solution)/shard_map/ppermute | solution.py:35
  13.3 1.7 %collective-permute-start.6 = (bf16[64,640]{1,0:T(8,128)(2,1)S(1)}, bf16[64,640]{1,0:T(8,128)(2,1)S(1)}, u32[]{:S(2)}, u32[]{:S(2)}) collective-permute-start(bf16[64,640]{1,0:T(8,128)(2,1)S(1)} %collective-permute-done.3.refs_1_), channel_id=1, source_target_pairs={{0,4},{1,5},{2,6},{3,7},{4,8},{5,9},{6,10},{7,11},{8,12},{9,13},{1... | collective-permute-start | bytes 245768 | tf_op jit(solution)/shard_map/ppermute | solution.py:35
  15.0 0.6 collective-permute-start.4
  15.7 0.7 collective-permute-done.5.refs_2_
  16.4 1.8 %collective-permute-done.6.refs_3_ = bf16[64,640]{1,0:T(8,128)(2,1)S(1)} collective-permute-done((bf16[64,640]{1,0:T(8,128)(2,1)S(1)}, bf16[64,640]{1,0:T(8,128)(2,1)S(1)}, u32[]{:S(2)}, u32[]{:S(2)}) %collective-permute-start.6) | collective-permute-done | bytes 81952 | tf_op jit(solution)/shard_map/ppermute | solution.py:35
  18.3 0.6 collective-permute-start.8
  19.0 0.5 shard_map.112
  19.4 1.4 %collective-permute-done.7.refs_2_ = bf16[64,640]{1,0:T(8,128)(2,1)S(1)} collective-permute-done((bf16[64,640]{1,0:T(8,128)(2,1)S(1)}, bf16[64,640]{1,0:T(8,128)(2,1)S(1)}, u32[]{:S(2)}, u32[]{:S(2)}) %collective-permute-start.7) | collective-permute-done | bytes 81952 | tf_op jit(solution)/shard_map/ppermute | solution.py:35
  20.8 2.2 %collective-permute-done.8.refs_3_ = bf16[64,640]{1,0:T(8,128)(2,1)S(1)} collective-permute-done((bf16[64,640]{1,0:T(8,128)(2,1)S(1)}, bf16[64,640]{1,0:T(8,128)(2,1)S(1)}, u32[]{:S(2)}, u32[]{:S(2)}) %collective-permute-start.8) | collective-permute-done | bytes 81952 | tf_op jit(solution)/shard_map/ppermute | solution.py:35
  23.2 0.4 shard_map.114
  23.6 1.0 %collective-permute-done.q1 = bf16[1296,128]{1,0:T(8,128)(2,1)S(1)} collective-permute-done((bf16[1296,128]{1,0:T(8,128)(2,1)}, bf16[1296,128]{1,0:T(8,128)(2,1)S(1)}, u32[]{:S(2)}, u32[]{:S(2)}) %collective-permute-start) | collective-permute-done | bytes 331808 | tf_op jit(solution)/shard_map/ppermute | solution.py:31
  24.6 2.8 %shard_map.115 = (f32[4,512,512]{2,1,0:T(8,128)S(1)}, f32[4,512,512]{2,1,0:T(8,128)S(1)}, f32[16,512]{1,0:T(8,128)S(1)}) custom-call(s32[3]{0:T(128)S(1)} %pad_add_fusion.where, bf16[1296,128]{1,0:T(8,128)(2,1)S(1)} %copy-done, bf16[1296,128]{1,0:T(8,128)(2,1)S(1)} %collective-permute-done.q1, bf16[1296,128]{1,0:T(8,128)(2,1)S(1)} %collective-permute-done.1.q2, ...), custom_call_target="tpu_custom_call" | custom-call | flops 1000000000 | bytes 8388608 | tf_op jit(solution)/shard_map/pallas_call | solution.py:174
  27.4 2.1 %collective-permute-start.11 = (f32[16,512]{1,0:T(8,128)S(1)}, f32[16,512]{1,0:T(8,128)S(1)}, u32[]{:S(2)}, u32[]{:S(2)}) collective-permute-start(f32[16,512]{1,0:T(8,128)S(1)} %get-tuple-element.62.t0), channel_id=1, source_target_pairs={{0,1},{1,2},{2,3},{3,0},{4,5},{5,6},{6,7},{7,4},{8,9},{9,10},{10,1... | collective-permute-start | bytes 98312 | tf_op jit(solution)/shard_map/ppermute | solution.py:31
  29.5 2.5 %collective-permute-start.10 = (f32[16,512]{1,0:T(8,128)S(1)}, f32[16,512]{1,0:T(8,128)S(1)}, u32[]{:S(2)}, u32[]{:S(2)}) collective-permute-start(f32[16,512]{1,0:T(8,128)S(1)} %get-tuple-element.62.t0), channel_id=1, source_target_pairs={{0,2},{1,3},{2,0},{3,1},{4,6},{5,7},{6,4},{7,5},{8,10},{9,11},{10,... | collective-permute-start | bytes 98312 | tf_op jit(solution)/shard_map/ppermute | solution.py:31
  32.0 0.2 collective-permute-start.9
  32.2 1.6 %collective-permute-done.10.t2 = f32[16,512]{1,0:T(8,128)S(1)} collective-permute-done((f32[16,512]{1,0:T(8,128)S(1)}, f32[16,512]{1,0:T(8,128)S(1)}, u32[]{:S(2)}, u32[]{:S(2)}) %collective-permute-start.10) | collective-permute-done | bytes 32800 | tf_op jit(solution)/shard_map/ppermute | solution.py:31
  33.8 1.4 %collective-permute-done.9.t1 = f32[16,512]{1,0:T(8,128)S(1)} collective-permute-done((f32[16,512]{1,0:T(8,128)S(1)}, f32[16,512]{1,0:T(8,128)S(1)}, u32[]{:S(2)}, u32[]{:S(2)}) %collective-permute-start.9) | collective-permute-done | bytes 32800 | tf_op jit(solution)/shard_map/ppermute | solution.py:31
  35.2 3.1 %shard_map.116 = (bf16[4,128,512]{2,1,0:T(8,128)(2,1)S(1)}, bf16[128,512]{1,0:T(8,128)(2,1)S(1)}, bf16[3,128,512]{2,1,0:T(8,128)(2,1)S(1)}, bf16[4,512,512]{2,1,...) custom-call(s32[3]{0:T(128)S(1)} %pad_add_fusion.where, ...), custom_call_target="tpu_custom_call" | custom-call | flops 1500000000 | bytes 10485760 | tf_op jit(solution)/shard_map/pallas_call | solution.py:227
  38.3 2.4 %collective-permute-start.15 = (bf16[3,128,512]{2,1,0:T(8,128)(2,1)S(1)}, bf16[3,128,512]{2,1,0:T(8,128)(2,1)S(1)}, u32[]{:S(2)}, u32[]{:S(2)}) collective-permute-start(bf16[3,128,512]{2,1,0:T(8,128)(2,1)S(1)} %get-tuple-element.75), channel_id=1, source_target_pairs={{0,32},{32,0},{64,96},{96,64},{128,160},{160,128},{192,224},{224,1... | collective-permute-start | bytes 1179656 | tf_op jit(solution)/shard_map/ppermute | solution.py:44
  40.8 1.9 %collective-permute-start.20 = (bf16[128,640]{1,0:T(8,128)(2,1)S(1)}, bf16[128,640]{1,0:T(8,128)(2,1)S(1)}, u32[]{:S(2)}, u32[]{:S(2)}) collective-permute-start(bf16[128,640]{1,0:T(8,128)(2,1)S(1)} %get-tuple-element.79), channel_id=1, source_target_pairs={{0,28},{1,29},{2,30},{3,31},{4,0},{5,1},{6,2},{7,3},{8,4},{9,5},{1... | collective-permute-start | bytes 491528 | tf_op jit(solution)/shard_map/ppermute | solution.py:35
  42.7 1.3 %collective-permute-start.18 = (bf16[128,512]{1,0:T(8,128)(2,1)S(1)}, bf16[128,512]{1,0:T(8,128)(2,1)S(1)}, u32[]{:S(2)}, u32[]{:S(2)}) collective-permute-start(bf16[128,512]{1,0:T(8,128)(2,1)S(1)} %shard_map.120), channel_id=1, source_target_pairs={{0,2},{1,3},{2,0},{3,1},{4,6},{5,7},{6,4},{7,5},{8,10},{9,11},{10,... | collective-permute-start | bytes 393224 | tf_op jit(solution)/shard_map/ppermute | solution.py:31
  44.1 1.8 %collective-permute-start.16 = (bf16[128,512]{1,0:T(8,128)(2,1)S(1)}, bf16[128,512]{1,0:T(8,128)(2,1)S(1)}, u32[]{:S(2)}, u32[]{:S(2)}) collective-permute-start(bf16[128,512]{1,0:T(8,128)(2,1)S(1)} %get-tuple-element.76), channel_id=1, source_target_pairs={{0,1},{1,2},{2,3},{3,0},{4,5},{5,6},{6,7},{7,4},{8,9},{9,10},{10,1... | collective-permute-start | bytes 393224 | tf_op jit(solution)/shard_map/ppermute | solution.py:31
  45.9 1.0 %collective-permute-start.19 = (bf16[128,512]{1,0:T(8,128)(2,1)S(1)}, bf16[128,512]{1,0:T(8,128)(2,1)S(1)}, u32[]{:S(2)}, u32[]{:S(2)}) collective-permute-start(bf16[128,512]{1,0:T(8,128)(2,1)S(1)} %get-tuple-element.78), channel_id=1, source_target_pairs={{0,3},{1,0},{2,1},{3,2},{4,7},{5,4},{6,5},{7,6},{8,11},{9,8},{10,9... | collective-permute-start | bytes 393224 | tf_op jit(solution)/shard_map/ppermute | solution.py:31
  46.9 1.8 %shard_map.117 = (bf16[128,640]{1,0:T(8,128)(2,1)S(1)}, bf16[128,640]{1,0:T(8,128)(2,1)S(1)}, bf16[128,640]{1,0:T(8,128)(2,1)S(1)}, bf16[128,768]{1,0:T(8,128)(2...) custom-call(s32[3]{0:T(128)S(1)} %pad_add_fusion.where, ...), custom_call_target="tpu_custom_call" | custom-call | flops 1500000000 | bytes 10485760 | tf_op jit(solution)/shard_map/pallas_call | solution.py:256
  48.7 2.6 %collective-permute-start.21 = (bf16[128,640]{1,0:T(8,128)(2,1)S(1)}, bf16[128,640]{1,0:T(8,128)(2,1)S(1)}, u32[]{:S(2)}, u32[]{:S(2)}) collective-permute-start(bf16[128,640]{1,0:T(8,128)(2,1)S(1)} %shard_map.122), channel_id=1, source_target_pairs={{0,24},{1,25},{2,26},{3,27},{4,28},{5,29},{6,30},{7,31},{8,0},{9,1... | collective-permute-start | bytes 491528 | tf_op jit(solution)/shard_map/ppermute | solution.py:35
  51.3 0.8 %collective-permute-done.16.p1 = bf16[128,512]{1,0:T(8,128)(2,1)S(1)} collective-permute-done((bf16[128,512]{1,0:T(8,128)(2,1)S(1)}, bf16[128,512]{1,0:T(8,128)(2,1)S(1)}, u32[]{:S(2)}, u32[]{:S(2)}) %collective-permute-start.16) | collective-permute-done | bytes 131104 | tf_op jit(solution)/shard_map/ppermute | solution.py:31
  52.1 0.7 shard_map.121
  52.9 5.8 %all-to-all-start = ((bf16[8,16,512]{2,1,0:T(8,128)(2,1)}), bf16[8,16,512]{2,1,0:T(8,128)(2,1)S(1)}, u32[]{:S(2)}, u32[]{:S(2)}) async-start(bf16[8,16,512]{2,1,0:T(8,128)(2,1)} %bitcast.10), calls=%async_computation | async-start | bytes 262144 | tf_op jit(solution)/shard_map/all_to_all | solution.py:325
  58.7 3.2 %collective-permute-start.13 = (bf16[128,768]{1,0:T(8,128)(2,1)S(1)}, bf16[128,768]{1,0:T(8,128)(2,1)S(1)}, u32[]{:S(2)}, u32[]{:S(2)}) collective-permute-start(bf16[128,768]{1,0:T(8,128)(2,1)S(1)} %get-tuple-element.70), channel_id=1, source_target_pairs={{0,2},{1,3},{2,0},{3,1},{4,6},{5,7},{6,4},{7,5},{8,10},{9,11},{10,... | collective-permute-start | bytes 589832 | tf_op jit(solution)/shard_map/ppermute | solution.py:31
  62.0 0.5 collective-permute-start.14
  62.4 2.7 %collective-permute-start.23 = (bf16[128,640]{1,0:T(8,128)(2,1)S(1)}, bf16[128,640]{1,0:T(8,128)(2,1)S(1)}, u32[]{:S(2)}, u32[]{:S(2)}) collective-permute-start(bf16[128,640]{1,0:T(8,128)(2,1)S(1)} %get-tuple-element.84), channel_id=1, source_target_pairs={{0,28},{1,29},{2,30},{3,31},{4,0},{5,1},{6,2},{7,3},{8,4},{9,5},{1... | collective-permute-start | bytes 491528 | tf_op jit(solution)/shard_map/ppermute | solution.py:35
  65.1 1.5 %all-to-all-done = bf16[8,16,512]{2,1,0:T(8,128)(2,1)S(1)} async-done(((bf16[8,16,512]{2,1,0:T(8,128)(2,1)}), bf16[8,16,512]{2,1,0:T(8,128)(2,1)S(1)}, u32[]{:S(2)}, u32[]{:S(2)}) %all-to-all-start) | async-done | bytes 131104 | tf_op jit(solution)/shard_map/all_to_all | solution.py:325
  66.6 1.4 %collective-permute-start.22 = (bf16[16,512]{1,0:T(8,128)(2,1)S(1)}, bf16[16,512]{1,0:T(8,128)(2,1)S(1)}, u32[]{:S(2)}, u32[]{:S(2)}) collective-permute-start(bf16[16,512]{1,0:T(8,128)(2,1)S(1)} %shard_map.124.refs_0_), channel_id=1, source_target_pairs={{0,64},{32,96},{64,0},{96,32},{128,192},{160,224},{192,128},{224,1... | collective-permute-start | bytes 49160 | tf_op jit(solution)/shard_map/ppermute | solution.py:40
  68.0 1.6 %collective-permute-done.22.refs_1_ = bf16[16,512]{1,0:T(8,128)(2,1)S(1)} collective-permute-done((bf16[16,512]{1,0:T(8,128)(2,1)S(1)}, bf16[16,512]{1,0:T(8,128)(2,1)S(1)}, u32[]{:S(2)}, u32[]{:S(2)}) %collective-permute-start.22) | collective-permute-done | bytes 16416 | tf_op jit(solution)/shard_map/ppermute | solution.py:40
  69.6 2.7 %collective-permute-start.24 = (bf16[16,512]{1,0:T(8,128)(2,1)S(1)}, bf16[16,512]{1,0:T(8,128)(2,1)S(1)}, u32[]{:S(2)}, u32[]{:S(2)}) collective-permute-start(bf16[16,512]{1,0:T(8,128)(2,1)S(1)} %shard_map.125.refs_0_), channel_id=1, source_target_pairs={{0,192},{32,224},{64,128},{96,160},{128,64},{160,96},{192,0},{224,... | collective-permute-start | bytes 49160 | tf_op jit(solution)/shard_map/ppermute | solution.py:40
  72.3 0.8 shard_map.126
  73.1 0.4 collective-permute-done.24.refs_1_
  73.5 4.3 %collective-permute-start.25 = (f32[16,512]{1,0:T(8,128)S(1)}, f32[16,512]{1,0:T(8,128)S(1)}, u32[]{:S(2)}, u32[]{:S(2)}) collective-permute-start(f32[16,512]{1,0:T(8,128)S(1)} %shard_map.127), channel_id=1, source_target_pairs={{0,32},{32,0},{64,96},{96,64},{128,160},{160,128},{192,224},{224,1... | collective-permute-start | bytes 98312 | tf_op jit(solution)/shard_map/ppermute | solution.py:44
  77.8 0.7 shard_map.118
  78.5 0.1 collective-permute-done.25
  78.7 0.6 broadcast_select_fusion
  (36 shorter events, 0.7 us)
Async XLA Ops:
  0.6 18.3 %copy-start.2 = (bf16[512,512]{1,0:T(8,128)(2,1)S(1)}, bf16[512,512]{1,0:T(8,128)(2,1)}, u32[]{:S(2)}) copy-start(bf16[512,512]{1,0:T(8,128)(2,1)} %wv.1) | copy-start | bytes 1572868
  0.6 18.3 %copy-start.1 = (bf16[512,512]{1,0:T(8,128)(2,1)S(1)}, bf16[512,512]{1,0:T(8,128)(2,1)}, u32[]{:S(2)}) copy-start(bf16[512,512]{1,0:T(8,128)(2,1)} %wk.1) | copy-start | bytes 1572868
  2.7 20.4 %copy-start.3 = (bf16[64,640]{1,0:T(8,128)(2,1)S(1)}, bf16[64,640]{1,0:T(8,128)(2,1)}, u32[]{:S(2)}) copy-start(bf16[64,640]{1,0:T(8,128)(2,1)} %get-tuple-element.47.refs_0_) | copy-start | bytes 245764
  2.7 20.4 %copy-start.4 = (bf16[64,640]{1,0:T(8,128)(2,1)S(1)}, bf16[64,640]{1,0:T(8,128)(2,1)}, u32[]{:S(2)}) copy-start(bf16[64,640]{1,0:T(8,128)(2,1)} %get-tuple-element.48.refs_1_) | copy-start | bytes 245764
  2.7 8.9 %collective-permute-start.2 = (bf16[64,640]{1,0:T(8,128)(2,1)}, bf16[64,640]{1,0:T(8,128)(2,1)S(1)}, u32[]{:S(2)}, u32[]{:S(2)}) collective-permute-start(bf16[64,640]{1,0:T(8,128)(2,1)} %get-tuple-element.47.refs_0_), channel_id=1, source_target_pairs={{0,4},{1,5},{2,6},{3,7},{4,8},{5,9},{6,10},{7,11},{8,12},{9,13},{1... | collective-permute-start | bytes 245768 | tf_op jit(solution)/shard_map/ppermute | solution.py:35
  5.2 8.1 %collective-permute-start.3 = (bf16[64,640]{1,0:T(8,128)(2,1)}, bf16[64,640]{1,0:T(8,128)(2,1)S(1)}, u32[]{:S(2)}, u32[]{:S(2)}) collective-permute-start(bf16[64,640]{1,0:T(8,128)(2,1)} %get-tuple-element.48.refs_1_), channel_id=1, source_target_pairs={{0,4},{1,5},{2,6},{3,7},{4,8},{5,9},{6,10},{7,11},{8,12},{9,13},{1... | collective-permute-start | bytes 245768 | tf_op jit(solution)/shard_map/ppermute | solution.py:35
  6.9 16.7 %collective-permute-start.1 = (bf16[1296,128]{1,0:T(8,128)(2,1)}, bf16[1296,128]{1,0:T(8,128)(2,1)S(1)}, u32[]{:S(2)}, u32[]{:S(2)}) collective-permute-start(bf16[1296,128]{1,0:T(8,128)(2,1)} %get-tuple-element.49.q0), channel_id=1, source_target_pairs={{0,2},{1,3},{2,0},{3,1},{4,6},{5,7},{6,4},{7,5},{8,10},{9,11},{10,... | collective-permute-start | bytes 995336 | tf_op jit(solution)/shard_map/ppermute | solution.py:31
  9.6 15.0 %collective-permute-start = (bf16[1296,128]{1,0:T(8,128)(2,1)}, bf16[1296,128]{1,0:T(8,128)(2,1)S(1)}, u32[]{:S(2)}, u32[]{:S(2)}) collective-permute-start(bf16[1296,128]{1,0:T(8,128)(2,1)} %get-tuple-element.49.q0), channel_id=1, source_target_pairs={{0,3},{1,0},{2,1},{3,2},{4,7},{5,4},{6,5},{7,6},{8,11},{9,8},{10,9... | collective-permute-start | bytes 995336 | tf_op jit(solution)/shard_map/ppermute | solution.py:31
  11.5 4.8 %collective-permute-start.5 = (bf16[64,640]{1,0:T(8,128)(2,1)S(1)}, bf16[64,640]{1,0:T(8,128)(2,1)S(1)}, u32[]{:S(2)}, u32[]{:S(2)}) collective-permute-start(bf16[64,640]{1,0:T(8,128)(2,1)S(1)} %collective-permute-done.2.refs_0_), channel_id=1, source_target_pairs={{0,4},{1,5},{2,6},{3,7},{4,8},{5,9},{6,10},{7,11},{8,12},{9,13},{1... | collective-permute-start | bytes 245768 | tf_op jit(solution)/shard_map/ppermute | solution.py:35
  13.3 5.0 %collective-permute-start.6 = (bf16[64,640]{1,0:T(8,128)(2,1)S(1)}, bf16[64,640]{1,0:T(8,128)(2,1)S(1)}, u32[]{:S(2)}, u32[]{:S(2)}) collective-permute-start(bf16[64,640]{1,0:T(8,128)(2,1)S(1)} %collective-permute-done.3.refs_1_), channel_id=1, source_target_pairs={{0,4},{1,5},{2,6},{3,7},{4,8},{5,9},{6,10},{7,11},{8,12},{9,13},{1... | collective-permute-start | bytes 245768 | tf_op jit(solution)/shard_map/ppermute | solution.py:35
  15.0 9.5 %collective-permute-start.4 = (bf16[1296,128]{1,0:T(8,128)(2,1)}, bf16[1296,128]{1,0:T(8,128)(2,1)S(1)}, u32[]{:S(2)}, u32[]{:S(2)}) collective-permute-start(bf16[1296,128]{1,0:T(8,128)(2,1)} %get-tuple-element.49.q0), channel_id=1, source_target_pairs={{0,1},{1,2},{2,3},{3,0},{4,5},{5,6},{6,7},{7,4},{8,9},{9,10},{10,1... | collective-permute-start | bytes 995336 | tf_op jit(solution)/shard_map/ppermute | solution.py:31
  16.3 4.5 %collective-permute-start.7 = (bf16[64,640]{1,0:T(8,128)(2,1)S(1)}, bf16[64,640]{1,0:T(8,128)(2,1)S(1)}, u32[]{:S(2)}, u32[]{:S(2)}) collective-permute-start(bf16[64,640]{1,0:T(8,128)(2,1)S(1)} %collective-permute-done.5.refs_2_), channel_id=1, source_target_pairs={{0,4},{1,5},{2,6},{3,7},{4,8},{5,9},{6,10},{7,11},{8,12},{9,13},{1... | collective-permute-start | bytes 245768 | tf_op jit(solution)/shard_map/ppermute | solution.py:35
  18.3 4.8 %collective-permute-start.8 = (bf16[64,640]{1,0:T(8,128)(2,1)S(1)}, bf16[64,640]{1,0:T(8,128)(2,1)S(1)}, u32[]{:S(2)}, u32[]{:S(2)}) collective-permute-start(bf16[64,640]{1,0:T(8,128)(2,1)S(1)} %collective-permute-done.6.refs_3_), channel_id=1, source_target_pairs={{0,4},{1,5},{2,6},{3,7},{4,8},{5,9},{6,10},{7,11},{8,12},{9,13},{1... | collective-permute-start | bytes 245768 | tf_op jit(solution)/shard_map/ppermute | solution.py:35
  19.0 5.6 %copy-start = (bf16[1296,128]{1,0:T(8,128)(2,1)S(1)}, bf16[1296,128]{1,0:T(8,128)(2,1)}, u32[]{:S(2)}) copy-start(bf16[1296,128]{1,0:T(8,128)(2,1)} %get-tuple-element.49.q0) | copy-start | bytes 995332
  27.4 4.8 %collective-permute-start.11 = (f32[16,512]{1,0:T(8,128)S(1)}, f32[16,512]{1,0:T(8,128)S(1)}, u32[]{:S(2)}, u32[]{:S(2)}) collective-permute-start(f32[16,512]{1,0:T(8,128)S(1)} %get-tuple-element.62.t0), channel_id=1, source_target_pairs={{0,1},{1,2},{2,3},{3,0},{4,5},{5,6},{6,7},{7,4},{8,9},{9,10},{10,1... | collective-permute-start | bytes 98312 | tf_op jit(solution)/shard_map/ppermute | solution.py:31
  29.5 4.3 %collective-permute-start.10 = (f32[16,512]{1,0:T(8,128)S(1)}, f32[16,512]{1,0:T(8,128)S(1)}, u32[]{:S(2)}, u32[]{:S(2)}) collective-permute-start(f32[16,512]{1,0:T(8,128)S(1)} %get-tuple-element.62.t0), channel_id=1, source_target_pairs={{0,2},{1,3},{2,0},{3,1},{4,6},{5,7},{6,4},{7,5},{8,10},{9,11},{10,... | collective-permute-start | bytes 98312 | tf_op jit(solution)/shard_map/ppermute | solution.py:31
  32.0 3.3 %collective-permute-start.9 = (f32[16,512]{1,0:T(8,128)S(1)}, f32[16,512]{1,0:T(8,128)S(1)}, u32[]{:S(2)}, u32[]{:S(2)}) collective-permute-start(f32[16,512]{1,0:T(8,128)S(1)} %get-tuple-element.62.t0), channel_id=1, source_target_pairs={{0,3},{1,0},{2,1},{3,2},{4,7},{5,4},{6,5},{7,6},{8,11},{9,8},{10,9... | collective-permute-start | bytes 98312 | tf_op jit(solution)/shard_map/ppermute | solution.py:31
  38.3 5.7 %collective-permute-start.15 = (bf16[3,128,512]{2,1,0:T(8,128)(2,1)S(1)}, bf16[3,128,512]{2,1,0:T(8,128)(2,1)S(1)}, u32[]{:S(2)}, u32[]{:S(2)}) collective-permute-start(bf16[3,128,512]{2,1,0:T(8,128)(2,1)S(1)} %get-tuple-element.75), channel_id=1, source_target_pairs={{0,32},{32,0},{64,96},{96,64},{128,160},{160,128},{192,224},{224,1... | collective-permute-start | bytes 1179656 | tf_op jit(solution)/shard_map/ppermute | solution.py:44
  40.7 2.0 %collective-permute-start.17 = (bf16[128,512]{1,0:T(8,128)(2,1)S(1)}, bf16[128,512]{1,0:T(8,128)(2,1)S(1)}, u32[]{:S(2)}, u32[]{:S(2)}) collective-permute-start(bf16[128,512]{1,0:T(8,128)(2,1)S(1)} %get-tuple-element.77), channel_id=1, source_target_pairs={{0,32},{32,0},{64,96},{96,64},{128,160},{160,128},{192,224},{224,1... | collective-permute-start | bytes 393224 | tf_op jit(solution)/shard_map/ppermute | solution.py:44
  40.8 7.9 %collective-permute-start.20 = (bf16[128,640]{1,0:T(8,128)(2,1)S(1)}, bf16[128,640]{1,0:T(8,128)(2,1)S(1)}, u32[]{:S(2)}, u32[]{:S(2)}) collective-permute-start(bf16[128,640]{1,0:T(8,128)(2,1)S(1)} %get-tuple-element.79), channel_id=1, source_target_pairs={{0,28},{1,29},{2,30},{3,31},{4,0},{5,1},{6,2},{7,3},{8,4},{9,5},{1... | collective-permute-start | bytes 491528 | tf_op jit(solution)/shard_map/ppermute | solution.py:35
  42.7 8.6 %collective-permute-start.18 = (bf16[128,512]{1,0:T(8,128)(2,1)S(1)}, bf16[128,512]{1,0:T(8,128)(2,1)S(1)}, u32[]{:S(2)}, u32[]{:S(2)}) collective-permute-start(bf16[128,512]{1,0:T(8,128)(2,1)S(1)} %shard_map.120), channel_id=1, source_target_pairs={{0,2},{1,3},{2,0},{3,1},{4,6},{5,7},{6,4},{7,5},{8,10},{9,11},{10,... | collective-permute-start | bytes 393224 | tf_op jit(solution)/shard_map/ppermute | solution.py:31
  44.1 8.0 %collective-permute-start.16 = (bf16[128,512]{1,0:T(8,128)(2,1)S(1)}, bf16[128,512]{1,0:T(8,128)(2,1)S(1)}, u32[]{:S(2)}, u32[]{:S(2)}) collective-permute-start(bf16[128,512]{1,0:T(8,128)(2,1)S(1)} %get-tuple-element.76), channel_id=1, source_target_pairs={{0,1},{1,2},{2,3},{3,0},{4,5},{5,6},{6,7},{7,4},{8,9},{9,10},{10,1... | collective-permute-start | bytes 393224 | tf_op jit(solution)/shard_map/ppermute | solution.py:31
  45.9 6.3 %collective-permute-start.19 = (bf16[128,512]{1,0:T(8,128)(2,1)S(1)}, bf16[128,512]{1,0:T(8,128)(2,1)S(1)}, u32[]{:S(2)}, u32[]{:S(2)}) collective-permute-start(bf16[128,512]{1,0:T(8,128)(2,1)S(1)} %get-tuple-element.78), channel_id=1, source_target_pairs={{0,3},{1,0},{2,1},{3,2},{4,7},{5,4},{6,5},{7,6},{8,11},{9,8},{10,9... | collective-permute-start | bytes 393224 | tf_op jit(solution)/shard_map/ppermute | solution.py:31
  48.7 16.4 %collective-permute-start.21 = (bf16[128,640]{1,0:T(8,128)(2,1)S(1)}, bf16[128,640]{1,0:T(8,128)(2,1)S(1)}, u32[]{:S(2)}, u32[]{:S(2)}) collective-permute-start(bf16[128,640]{1,0:T(8,128)(2,1)S(1)} %shard_map.122), channel_id=1, source_target_pairs={{0,24},{1,25},{2,26},{3,27},{4,28},{5,29},{6,30},{7,31},{8,0},{9,1... | collective-permute-start | bytes 491528 | tf_op jit(solution)/shard_map/ppermute | solution.py:35
  52.9 13.7 %all-to-all-start = ((bf16[8,16,512]{2,1,0:T(8,128)(2,1)}), bf16[8,16,512]{2,1,0:T(8,128)(2,1)S(1)}, u32[]{:S(2)}, u32[]{:S(2)}) async-start(bf16[8,16,512]{2,1,0:T(8,128)(2,1)} %bitcast.10), calls=%async_computation | async-start | bytes 262144 | tf_op jit(solution)/shard_map/all_to_all | solution.py:325
  58.7 19.1 %collective-permute-start.12 = (bf16[128,768]{1,0:T(8,128)(2,1)S(1)}, bf16[128,768]{1,0:T(8,128)(2,1)S(1)}, u32[]{:S(2)}, u32[]{:S(2)}) collective-permute-start(bf16[128,768]{1,0:T(8,128)(2,1)S(1)} %get-tuple-element.69), channel_id=1, source_target_pairs={{0,1},{1,2},{2,3},{3,0},{4,5},{5,6},{6,7},{7,4},{8,9},{9,10},{10,1... | collective-permute-start | bytes 589832 | tf_op jit(solution)/shard_map/ppermute | solution.py:31
  58.7 19.1 %collective-permute-start.13 = (bf16[128,768]{1,0:T(8,128)(2,1)S(1)}, bf16[128,768]{1,0:T(8,128)(2,1)S(1)}, u32[]{:S(2)}, u32[]{:S(2)}) collective-permute-start(bf16[128,768]{1,0:T(8,128)(2,1)S(1)} %get-tuple-element.70), channel_id=1, source_target_pairs={{0,2},{1,3},{2,0},{3,1},{4,6},{5,7},{6,4},{7,5},{8,10},{9,11},{10,... | collective-permute-start | bytes 589832 | tf_op jit(solution)/shard_map/ppermute | solution.py:31
  62.0 15.8 %collective-permute-start.14 = (bf16[128,768]{1,0:T(8,128)(2,1)S(1)}, bf16[128,768]{1,0:T(8,128)(2,1)S(1)}, u32[]{:S(2)}, u32[]{:S(2)}) collective-permute-start(bf16[128,768]{1,0:T(8,128)(2,1)S(1)} %get-tuple-element.71), channel_id=1, source_target_pairs={{0,3},{1,0},{2,1},{3,2},{4,7},{5,4},{6,5},{7,6},{8,11},{9,8},{10,9... | collective-permute-start | bytes 589832 | tf_op jit(solution)/shard_map/ppermute | solution.py:31
  62.4 9.9 %collective-permute-start.23 = (bf16[128,640]{1,0:T(8,128)(2,1)S(1)}, bf16[128,640]{1,0:T(8,128)(2,1)S(1)}, u32[]{:S(2)}, u32[]{:S(2)}) collective-permute-start(bf16[128,640]{1,0:T(8,128)(2,1)S(1)} %get-tuple-element.84), channel_id=1, source_target_pairs={{0,28},{1,29},{2,30},{3,31},{4,0},{5,1},{6,2},{7,3},{8,4},{9,5},{1... | collective-permute-start | bytes 491528 | tf_op jit(solution)/shard_map/ppermute | solution.py:35
  66.6 3.0 %collective-permute-start.22 = (bf16[16,512]{1,0:T(8,128)(2,1)S(1)}, bf16[16,512]{1,0:T(8,128)(2,1)S(1)}, u32[]{:S(2)}, u32[]{:S(2)}) collective-permute-start(bf16[16,512]{1,0:T(8,128)(2,1)S(1)} %shard_map.124.refs_0_), channel_id=1, source_target_pairs={{0,64},{32,96},{64,0},{96,32},{128,192},{160,224},{192,128},{224,1... | collective-permute-start | bytes 49160 | tf_op jit(solution)/shard_map/ppermute | solution.py:40
  69.6 3.9 %collective-permute-start.24 = (bf16[16,512]{1,0:T(8,128)(2,1)S(1)}, bf16[16,512]{1,0:T(8,128)(2,1)S(1)}, u32[]{:S(2)}, u32[]{:S(2)}) collective-permute-start(bf16[16,512]{1,0:T(8,128)(2,1)S(1)} %shard_map.125.refs_0_), channel_id=1, source_target_pairs={{0,192},{32,224},{64,128},{96,160},{128,64},{160,96},{192,0},{224,... | collective-permute-start | bytes 49160 | tf_op jit(solution)/shard_map/ppermute | solution.py:40
  73.5 5.2 %collective-permute-start.25 = (f32[16,512]{1,0:T(8,128)S(1)}, f32[16,512]{1,0:T(8,128)S(1)}, u32[]{:S(2)}, u32[]{:S(2)}) collective-permute-start(f32[16,512]{1,0:T(8,128)S(1)} %shard_map.127), channel_id=1, source_target_pairs={{0,32},{32,0},{64,96},{96,64},{128,160},{160,128},{192,224},{224,1... | collective-permute-start | bytes 98312 | tf_op jit(solution)/shard_map/ppermute | solution.py:44

commit v6 on v5

--- a/solution.py
+++ b/solution.py
@@ -196,11 +196,9 @@
     scaled = jnp.exp(tops[0] - top) * inv
     rope_grad = [jnp.zeros((KROWS, 128), F32), jnp.zeros((KROWS, 128), F32)]
     for h in range(HEADS):
-        for b in range(0, QROWS, 256):
-            sl = slice(b, b + 256)
-            p = es[h, :, sl] * scaled[h:h + 1, sl]
-            p_scr[h % 2, :, sl] = p.astype(BF)
-            ds[h, :, sl] = (p * (dps[h, :, sl] - delta[h:h + 1, sl]) * SCALE).astype(BF)
+        p = es[h] * scaled[h:h + 1]
+        p_scr[h % 2] = p.astype(BF)
+        ds[h] = (p * (dps[h] - delta[h:h + 1]) * SCALE).astype(BF)
         cols = slice(h * 128, (h + 1) * 128)
         dkv[1, :, cols] = jnp.dot(p_scr[h % 2], columns(blocks, 512 + h * 128), preferred_element_type=F32).astype(BF)
         dk = jnp.dot(ds[h], queries_of(blocks, h), preferred_element_type=F32)

time: 79.5 us -> 79.5 us (level)
  no operation moved by 1% of the time
where the time goes in v6:
time: 79.5 us; the launch traced here: 79.3 us
  starting transfers between devices  47.8 us (60%)
  waiting for transfers between devices  16.7 us (21%)
  Pallas kernels  13.2 us (17%)
  between operations  0.81 us (1%)
    ppermute x12, starting transfers between devices, x_shift(): lax.ppermute(v, 'ctx', [(i, i // X * X + (i % X + s) % X) for i in range(...  16.8 us
    ppermute x9, starting transfers between devices, z_shift(): lax.ppermute(v, 'ctx', [(i, (i + s * X) % (Z * X)) for i in range(Z * X)])  14.3 us
    ppermute x9, waiting for transfers between devices, z_shift(): lax.ppermute(v, 'ctx', [(i, (i + s * X) % (Z * X)) for i in range(Z * X)])  8.38 us
    ppermute x3, starting transfers between devices, core_swap(): return lax.ppermute(v, 'dp', [(i, i ^ 1) for i in range(2 * Y)])  6.8 us
    all_to_all x1, starting transfers between devices, body(): lax.all_to_all(w, 'ctx', 0, 0, tiled=True, axis_index_groups=[[z * X + x...  5.84 us
    ppermute x12, waiting for transfers between devices, x_shift(): lax.ppermute(v, 'ctx', [(i, i // X * X + (i % X + s) % X) for i in range(...  4.83 us
    ppermute x2, starting transfers between devices, y_pair(): return lax.ppermute(v, 'dp', pairs)  4.11 us
    pallas_call x1, Pallas kernels, run_weight(): call(weight_kernel, (sds((4, 128, 512), BF), sds((128, 512), BF), sds((3,...  3.07 us
  transfers between devices with their start and end apart: 27, of which 14 were waited for; matrix products, arithmetic and copies ran while one was open for 0% of the time, Pallas kernels for 7%

profile of v6, /device:TPU:1, one launch (start us, length us, event | category | flops | bytes accessed | tf_op | source)
XLA Modules:
  0.0 79.3 jit_solution(7819708435370707425)
XLA Ops:
  0.7 2.0 %shard_map.110 = (bf16[1296,128]{1,0:T(8,128)(2,1)}, bf16[64,640]{1,0:T(8,128)(2,1)}, bf16[64,640]{1,0:T(8,128)(2,1)}) custom-call(bf16[128,512]{1,0:T(8,128)(2,1)} %bitcast.19, bf16[128,256]{1,0:T(8,128)(2,1)} %bitcast.21, bf16[128,512]{1,0:T(8,128)(2,1)} %bitcast.20, bf16[576,128]{1,0:T(8,128)(2,1)} %bitcast.18, s32[1,128]{1,0:T(1,128)} %ids.1), custom_call_target="tpu_custom_call" | custom-call | bytes 1048576 | tf_op jit(solution)/shard_map/pallas_call | solution.py:84
  2.7 2.5 %collective-permute-start.2 = (bf16[64,640]{1,0:T(8,128)(2,1)}, bf16[64,640]{1,0:T(8,128)(2,1)S(1)}, u32[]{:S(2)}, u32[]{:S(2)}) collective-permute-start(bf16[64,640]{1,0:T(8,128)(2,1)} %get-tuple-element.47.refs_0_), channel_id=1, source_target_pairs={{0,4},{1,5},{2,6},{3,7},{4,8},{5,9},{6,10},{7,11},{8,12},{9,13},{1... | collective-permute-start | bytes 245768 | tf_op jit(solution)/shard_map/ppermute | solution.py:35
  5.2 1.6 %collective-permute-start.3 = (bf16[64,640]{1,0:T(8,128)(2,1)}, bf16[64,640]{1,0:T(8,128)(2,1)S(1)}, u32[]{:S(2)}, u32[]{:S(2)}) collective-permute-start(bf16[64,640]{1,0:T(8,128)(2,1)} %get-tuple-element.48.refs_1_), channel_id=1, source_target_pairs={{0,4},{1,5},{2,6},{3,7},{4,8},{5,9},{6,10},{7,11},{8,12},{9,13},{1... | collective-permute-start | bytes 245768 | tf_op jit(solution)/shard_map/ppermute | solution.py:35
  6.9 2.7 %collective-permute-start.1 = (bf16[1296,128]{1,0:T(8,128)(2,1)}, bf16[1296,128]{1,0:T(8,128)(2,1)S(1)}, u32[]{:S(2)}, u32[]{:S(2)}) collective-permute-start(bf16[1296,128]{1,0:T(8,128)(2,1)} %get-tuple-element.49.q0), channel_id=1, source_target_pairs={{0,2},{1,3},{2,0},{3,1},{4,6},{5,7},{6,4},{7,5},{8,10},{9,11},{10,... | collective-permute-start | bytes 995336 | tf_op jit(solution)/shard_map/ppermute | solution.py:31
  9.6 0.9 %collective-permute-start = (bf16[1296,128]{1,0:T(8,128)(2,1)}, bf16[1296,128]{1,0:T(8,128)(2,1)S(1)}, u32[]{:S(2)}, u32[]{:S(2)}) collective-permute-start(bf16[1296,128]{1,0:T(8,128)(2,1)} %get-tuple-element.49.q0), channel_id=1, source_target_pairs={{0,3},{1,0},{2,1},{3,2},{4,7},{5,4},{6,5},{7,6},{8,11},{9,8},{10,9... | collective-permute-start | bytes 995336 | tf_op jit(solution)/shard_map/ppermute | solution.py:31
  10.5 1.1 %collective-permute-done.2.refs_0_ = bf16[64,640]{1,0:T(8,128)(2,1)S(1)} collective-permute-done((bf16[64,640]{1,0:T(8,128)(2,1)}, bf16[64,640]{1,0:T(8,128)(2,1)S(1)}, u32[]{:S(2)}, u32[]{:S(2)}) %collective-permute-start.2) | collective-permute-done | bytes 81952 | tf_op jit(solution)/shard_map/ppermute | solution.py:35
  11.5 0.6 collective-permute-start.5
  12.1 1.2 %collective-permute-done.3.refs_1_ = bf16[64,640]{1,0:T(8,128)(2,1)S(1)} collective-permute-done((bf16[64,640]{1,0:T(8,128)(2,1)}, bf16[64,640]{1,0:T(8,128)(2,1)S(1)}, u32[]{:S(2)}, u32[]{:S(2)}) %collective-permute-start.3) | collective-permute-done | bytes 81952 | tf_op jit(solution)/shard_map/ppermute | solution.py:35
  13.3 1.7 %collective-permute-start.6 = (bf16[64,640]{1,0:T(8,128)(2,1)S(1)}, bf16[64,640]{1,0:T(8,128)(2,1)S(1)}, u32[]{:S(2)}, u32[]{:S(2)}) collective-permute-start(bf16[64,640]{1,0:T(8,128)(2,1)S(1)} %collective-permute-done.3.refs_1_), channel_id=1, source_target_pairs={{0,4},{1,5},{2,6},{3,7},{4,8},{5,9},{6,10},{7,11},{8,12},{9,13},{1... | collective-permute-start | bytes 245768 | tf_op jit(solution)/shard_map/ppermute | solution.py:35
  15.0 0.6 collective-permute-start.4
  15.7 0.7 collective-permute-done.5.refs_2_
  16.4 1.8 %collective-permute-done.6.refs_3_ = bf16[64,640]{1,0:T(8,128)(2,1)S(1)} collective-permute-done((bf16[64,640]{1,0:T(8,128)(2,1)S(1)}, bf16[64,640]{1,0:T(8,128)(2,1)S(1)}, u32[]{:S(2)}, u32[]{:S(2)}) %collective-permute-start.6) | collective-permute-done | bytes 81952 | tf_op jit(solution)/shard_map/ppermute | solution.py:35
  18.3 0.6 collective-permute-start.8
  19.0 0.5 shard_map.112
  19.4 1.4 %collective-permute-done.7.refs_2_ = bf16[64,640]{1,0:T(8,128)(2,1)S(1)} collective-permute-done((bf16[64,640]{1,0:T(8,128)(2,1)S(1)}, bf16[64,640]{1,0:T(8,128)(2,1)S(1)}, u32[]{:S(2)}, u32[]{:S(2)}) %collective-permute-start.7) | collective-permute-done | bytes 81952 | tf_op jit(solution)/shard_map/ppermute | solution.py:35
  20.8 2.2 %collective-permute-done.8.refs_3_ = bf16[64,640]{1,0:T(8,128)(2,1)S(1)} collective-permute-done((bf16[64,640]{1,0:T(8,128)(2,1)S(1)}, bf16[64,640]{1,0:T(8,128)(2,1)S(1)}, u32[]{:S(2)}, u32[]{:S(2)}) %collective-permute-start.8) | collective-permute-done | bytes 81952 | tf_op jit(solution)/shard_map/ppermute | solution.py:35
  23.2 0.4 shard_map.114
  23.6 1.0 %collective-permute-done.q1 = bf16[1296,128]{1,0:T(8,128)(2,1)S(1)} collective-permute-done((bf16[1296,128]{1,0:T(8,128)(2,1)}, bf16[1296,128]{1,0:T(8,128)(2,1)S(1)}, u32[]{:S(2)}, u32[]{:S(2)}) %collective-permute-start) | collective-permute-done | bytes 331808 | tf_op jit(solution)/shard_map/ppermute | solution.py:31
  24.6 2.8 %shard_map.115 = (f32[4,512,512]{2,1,0:T(8,128)S(1)}, f32[4,512,512]{2,1,0:T(8,128)S(1)}, f32[16,512]{1,0:T(8,128)S(1)}) custom-call(s32[3]{0:T(128)S(1)} %pad_add_fusion.where, bf16[1296,128]{1,0:T(8,128)(2,1)S(1)} %copy-done, bf16[1296,128]{1,0:T(8,128)(2,1)S(1)} %collective-permute-done.q1, bf16[1296,128]{1,0:T(8,128)(2,1)S(1)} %collective-permute-done.1.q2, ...), custom_call_target="tpu_custom_call" | custom-call | flops 1000000000 | bytes 8388608 | tf_op jit(solution)/shard_map/pallas_call | solution.py:174
  27.4 2.1 %collective-permute-start.11 = (f32[16,512]{1,0:T(8,128)S(1)}, f32[16,512]{1,0:T(8,128)S(1)}, u32[]{:S(2)}, u32[]{:S(2)}) collective-permute-start(f32[16,512]{1,0:T(8,128)S(1)} %get-tuple-element.62.t0), channel_id=1, source_target_pairs={{0,1},{1,2},{2,3},{3,0},{4,5},{5,6},{6,7},{7,4},{8,9},{9,10},{10,1... | collective-permute-start | bytes 98312 | tf_op jit(solution)/shard_map/ppermute | solution.py:31
  29.5 2.5 %collective-permute-start.10 = (f32[16,512]{1,0:T(8,128)S(1)}, f32[16,512]{1,0:T(8,128)S(1)}, u32[]{:S(2)}, u32[]{:S(2)}) collective-permute-start(f32[16,512]{1,0:T(8,128)S(1)} %get-tuple-element.62.t0), channel_id=1, source_target_pairs={{0,2},{1,3},{2,0},{3,1},{4,6},{5,7},{6,4},{7,5},{8,10},{9,11},{10,... | collective-permute-start | bytes 98312 | tf_op jit(solution)/shard_map/ppermute | solution.py:31
  32.0 0.2 collective-permute-start.9
  32.2 1.6 %collective-permute-done.10.t2 = f32[16,512]{1,0:T(8,128)S(1)} collective-permute-done((f32[16,512]{1,0:T(8,128)S(1)}, f32[16,512]{1,0:T(8,128)S(1)}, u32[]{:S(2)}, u32[]{:S(2)}) %collective-permute-start.10) | collective-permute-done | bytes 32800 | tf_op jit(solution)/shard_map/ppermute | solution.py:31
  33.8 1.4 %collective-permute-done.9.t1 = f32[16,512]{1,0:T(8,128)S(1)} collective-permute-done((f32[16,512]{1,0:T(8,128)S(1)}, f32[16,512]{1,0:T(8,128)S(1)}, u32[]{:S(2)}, u32[]{:S(2)}) %collective-permute-start.9) | collective-permute-done | bytes 32800 | tf_op jit(solution)/shard_map/ppermute | solution.py:31
  35.2 3.1 %shard_map.116 = (bf16[4,128,512]{2,1,0:T(8,128)(2,1)S(1)}, bf16[128,512]{1,0:T(8,128)(2,1)S(1)}, bf16[3,128,512]{2,1,0:T(8,128)(2,1)S(1)}, bf16[4,512,512]{2,1,...) custom-call(s32[3]{0:T(128)S(1)} %pad_add_fusion.where, ...), custom_call_target="tpu_custom_call" | custom-call | flops 1500000000 | bytes 10485760 | tf_op jit(solution)/shard_map/pallas_call | solution.py:225
  38.3 2.4 %collective-permute-start.15 = (bf16[3,128,512]{2,1,0:T(8,128)(2,1)S(1)}, bf16[3,128,512]{2,1,0:T(8,128)(2,1)S(1)}, u32[]{:S(2)}, u32[]{:S(2)}) collective-permute-start(bf16[3,128,512]{2,1,0:T(8,128)(2,1)S(1)} %get-tuple-element.75), channel_id=1, source_target_pairs={{0,32},{32,0},{64,96},{96,64},{128,160},{160,128},{192,224},{224,1... | collective-permute-start | bytes 1179656 | tf_op jit(solution)/shard_map/ppermute | solution.py:44
  40.8 1.9 %collective-permute-start.20 = (bf16[128,640]{1,0:T(8,128)(2,1)S(1)}, bf16[128,640]{1,0:T(8,128)(2,1)S(1)}, u32[]{:S(2)}, u32[]{:S(2)}) collective-permute-start(bf16[128,640]{1,0:T(8,128)(2,1)S(1)} %get-tuple-element.79), channel_id=1, source_target_pairs={{0,28},{1,29},{2,30},{3,31},{4,0},{5,1},{6,2},{7,3},{8,4},{9,5},{1... | collective-permute-start | bytes 491528 | tf_op jit(solution)/shard_map/ppermute | solution.py:35
  42.7 1.3 %collective-permute-start.18 = (bf16[128,512]{1,0:T(8,128)(2,1)S(1)}, bf16[128,512]{1,0:T(8,128)(2,1)S(1)}, u32[]{:S(2)}, u32[]{:S(2)}) collective-permute-start(bf16[128,512]{1,0:T(8,128)(2,1)S(1)} %shard_map.120), channel_id=1, source_target_pairs={{0,2},{1,3},{2,0},{3,1},{4,6},{5,7},{6,4},{7,5},{8,10},{9,11},{10,... | collective-permute-start | bytes 393224 | tf_op jit(solution)/shard_map/ppermute | solution.py:31
  44.1 1.8 %collective-permute-start.16 = (bf16[128,512]{1,0:T(8,128)(2,1)S(1)}, bf16[128,512]{1,0:T(8,128)(2,1)S(1)}, u32[]{:S(2)}, u32[]{:S(2)}) collective-permute-start(bf16[128,512]{1,0:T(8,128)(2,1)S(1)} %get-tuple-element.76), channel_id=1, source_target_pairs={{0,1},{1,2},{2,3},{3,0},{4,5},{5,6},{6,7},{7,4},{8,9},{9,10},{10,1... | collective-permute-start | bytes 393224 | tf_op jit(solution)/shard_map/ppermute | solution.py:31
  45.9 1.0 %collective-permute-start.19 = (bf16[128,512]{1,0:T(8,128)(2,1)S(1)}, bf16[128,512]{1,0:T(8,128)(2,1)S(1)}, u32[]{:S(2)}, u32[]{:S(2)}) collective-permute-start(bf16[128,512]{1,0:T(8,128)(2,1)S(1)} %get-tuple-element.78), channel_id=1, source_target_pairs={{0,3},{1,0},{2,1},{3,2},{4,7},{5,4},{6,5},{7,6},{8,11},{9,8},{10,9... | collective-permute-start | bytes 393224 | tf_op jit(solution)/shard_map/ppermute | solution.py:31
  46.9 1.8 %shard_map.117 = (bf16[128,640]{1,0:T(8,128)(2,1)S(1)}, bf16[128,640]{1,0:T(8,128)(2,1)S(1)}, bf16[128,640]{1,0:T(8,128)(2,1)S(1)}, bf16[128,768]{1,0:T(8,128)(2...) custom-call(s32[3]{0:T(128)S(1)} %pad_add_fusion.where, ...), custom_call_target="tpu_custom_call" | custom-call | flops 1500000000 | bytes 10485760 | tf_op jit(solution)/shard_map/pallas_call | solution.py:254
  48.7 2.6 %collective-permute-start.21 = (bf16[128,640]{1,0:T(8,128)(2,1)S(1)}, bf16[128,640]{1,0:T(8,128)(2,1)S(1)}, u32[]{:S(2)}, u32[]{:S(2)}) collective-permute-start(bf16[128,640]{1,0:T(8,128)(2,1)S(1)} %shard_map.122), channel_id=1, source_target_pairs={{0,24},{1,25},{2,26},{3,27},{4,28},{5,29},{6,30},{7,31},{8,0},{9,1... | collective-permute-start | bytes 491528 | tf_op jit(solution)/shard_map/ppermute | solution.py:35
  51.3 0.8 %collective-permute-done.16.p1 = bf16[128,512]{1,0:T(8,128)(2,1)S(1)} collective-permute-done((bf16[128,512]{1,0:T(8,128)(2,1)S(1)}, bf16[128,512]{1,0:T(8,128)(2,1)S(1)}, u32[]{:S(2)}, u32[]{:S(2)}) %collective-permute-start.16) | collective-permute-done | bytes 131104 | tf_op jit(solution)/shard_map/ppermute | solution.py:31
  52.1 0.7 shard_map.121
  52.9 5.8 %all-to-all-start = ((bf16[8,16,512]{2,1,0:T(8,128)(2,1)}), bf16[8,16,512]{2,1,0:T(8,128)(2,1)S(1)}, u32[]{:S(2)}, u32[]{:S(2)}) async-start(bf16[8,16,512]{2,1,0:T(8,128)(2,1)} %bitcast.10), calls=%async_computation | async-start | bytes 262144 | tf_op jit(solution)/shard_map/all_to_all | solution.py:323
  58.7 3.2 %collective-permute-start.13 = (bf16[128,768]{1,0:T(8,128)(2,1)S(1)}, bf16[128,768]{1,0:T(8,128)(2,1)S(1)}, u32[]{:S(2)}, u32[]{:S(2)}) collective-permute-start(bf16[128,768]{1,0:T(8,128)(2,1)S(1)} %get-tuple-element.70), channel_id=1, source_target_pairs={{0,2},{1,3},{2,0},{3,1},{4,6},{5,7},{6,4},{7,5},{8,10},{9,11},{10,... | collective-permute-start | bytes 589832 | tf_op jit(solution)/shard_map/ppermute | solution.py:31
  62.0 0.5 collective-permute-start.14
  62.4 2.7 %collective-permute-start.23 = (bf16[128,640]{1,0:T(8,128)(2,1)S(1)}, bf16[128,640]{1,0:T(8,128)(2,1)S(1)}, u32[]{:S(2)}, u32[]{:S(2)}) collective-permute-start(bf16[128,640]{1,0:T(8,128)(2,1)S(1)} %get-tuple-element.84), channel_id=1, source_target_pairs={{0,28},{1,29},{2,30},{3,31},{4,0},{5,1},{6,2},{7,3},{8,4},{9,5},{1... | collective-permute-start | bytes 491528 | tf_op jit(solution)/shard_map/ppermute | solution.py:35
  65.1 1.5 %all-to-all-done = bf16[8,16,512]{2,1,0:T(8,128)(2,1)S(1)} async-done(((bf16[8,16,512]{2,1,0:T(8,128)(2,1)}), bf16[8,16,512]{2,1,0:T(8,128)(2,1)S(1)}, u32[]{:S(2)}, u32[]{:S(2)}) %all-to-all-start) | async-done | bytes 131104 | tf_op jit(solution)/shard_map/all_to_all | solution.py:323
  66.6 1.4 %collective-permute-start.22 = (bf16[16,512]{1,0:T(8,128)(2,1)S(1)}, bf16[16,512]{1,0:T(8,128)(2,1)S(1)}, u32[]{:S(2)}, u32[]{:S(2)}) collective-permute-start(bf16[16,512]{1,0:T(8,128)(2,1)S(1)} %shard_map.124.refs_0_), channel_id=1, source_target_pairs={{0,64},{32,96},{64,0},{96,32},{128,192},{160,224},{192,128},{224,1... | collective-permute-start | bytes 49160 | tf_op jit(solution)/shard_map/ppermute | solution.py:40
  68.0 1.6 %collective-permute-done.22.refs_1_ = bf16[16,512]{1,0:T(8,128)(2,1)S(1)} collective-permute-done((bf16[16,512]{1,0:T(8,128)(2,1)S(1)}, bf16[16,512]{1,0:T(8,128)(2,1)S(1)}, u32[]{:S(2)}, u32[]{:S(2)}) %collective-permute-start.22) | collective-permute-done | bytes 16416 | tf_op jit(solution)/shard_map/ppermute | solution.py:40
  69.6 2.7 %collective-permute-start.24 = (bf16[16,512]{1,0:T(8,128)(2,1)S(1)}, bf16[16,512]{1,0:T(8,128)(2,1)S(1)}, u32[]{:S(2)}, u32[]{:S(2)}) collective-permute-start(bf16[16,512]{1,0:T(8,128)(2,1)S(1)} %shard_map.125.refs_0_), channel_id=1, source_target_pairs={{0,192},{32,224},{64,128},{96,160},{128,64},{160,96},{192,0},{224,... | collective-permute-start | bytes 49160 | tf_op jit(solution)/shard_map/ppermute | solution.py:40
  72.3 0.8 shard_map.126
  73.1 0.4 collective-permute-done.24.refs_1_
  73.5 4.3 %collective-permute-start.25 = (f32[16,512]{1,0:T(8,128)S(1)}, f32[16,512]{1,0:T(8,128)S(1)}, u32[]{:S(2)}, u32[]{:S(2)}) collective-permute-start(f32[16,512]{1,0:T(8,128)S(1)} %shard_map.127), channel_id=1, source_target_pairs={{0,32},{32,0},{64,96},{96,64},{128,160},{160,128},{192,224},{224,1... | collective-permute-start | bytes 98312 | tf_op jit(solution)/shard_map/ppermute | solution.py:44
  77.8 0.7 shard_map.118
  78.5 0.1 collective-permute-done.25
  78.7 0.6 broadcast_select_fusion
  (36 shorter events, 0.7 us)
Async XLA Ops:
  0.6 18.3 %copy-start.2 = (bf16[512,512]{1,0:T(8,128)(2,1)S(1)}, bf16[512,512]{1,0:T(8,128)(2,1)}, u32[]{:S(2)}) copy-start(bf16[512,512]{1,0:T(8,128)(2,1)} %wv.1) | copy-start | bytes 1572868
  0.6 18.3 %copy-start.1 = (bf16[512,512]{1,0:T(8,128)(2,1)S(1)}, bf16[512,512]{1,0:T(8,128)(2,1)}, u32[]{:S(2)}) copy-start(bf16[512,512]{1,0:T(8,128)(2,1)} %wk.1) | copy-start | bytes 1572868
  2.7 20.4 %copy-start.3 = (bf16[64,640]{1,0:T(8,128)(2,1)S(1)}, bf16[64,640]{1,0:T(8,128)(2,1)}, u32[]{:S(2)}) copy-start(bf16[64,640]{1,0:T(8,128)(2,1)} %get-tuple-element.47.refs_0_) | copy-start | bytes 245764
  2.7 20.4 %copy-start.4 = (bf16[64,640]{1,0:T(8,128)(2,1)S(1)}, bf16[64,640]{1,0:T(8,128)(2,1)}, u32[]{:S(2)}) copy-start(bf16[64,640]{1,0:T(8,128)(2,1)} %get-tuple-element.48.refs_1_) | copy-start | bytes 245764
  2.7 8.9 %collective-permute-start.2 = (bf16[64,640]{1,0:T(8,128)(2,1)}, bf16[64,640]{1,0:T(8,128)(2,1)S(1)}, u32[]{:S(2)}, u32[]{:S(2)}) collective-permute-start(bf16[64,640]{1,0:T(8,128)(2,1)} %get-tuple-element.47.refs_0_), channel_id=1, source_target_pairs={{0,4},{1,5},{2,6},{3,7},{4,8},{5,9},{6,10},{7,11},{8,12},{9,13},{1... | collective-permute-start | bytes 245768 | tf_op jit(solution)/shard_map/ppermute | solution.py:35
  5.2 8.1 %collective-permute-start.3 = (bf16[64,640]{1,0:T(8,128)(2,1)}, bf16[64,640]{1,0:T(8,128)(2,1)S(1)}, u32[]{:S(2)}, u32[]{:S(2)}) collective-permute-start(bf16[64,640]{1,0:T(8,128)(2,1)} %get-tuple-element.48.refs_1_), channel_id=1, source_target_pairs={{0,4},{1,5},{2,6},{3,7},{4,8},{5,9},{6,10},{7,11},{8,12},{9,13},{1... | collective-permute-start | bytes 245768 | tf_op jit(solution)/shard_map/ppermute | solution.py:35
  6.9 16.7 %collective-permute-start.1 = (bf16[1296,128]{1,0:T(8,128)(2,1)}, bf16[1296,128]{1,0:T(8,128)(2,1)S(1)}, u32[]{:S(2)}, u32[]{:S(2)}) collective-permute-start(bf16[1296,128]{1,0:T(8,128)(2,1)} %get-tuple-element.49.q0), channel_id=1, source_target_pairs={{0,2},{1,3},{2,0},{3,1},{4,6},{5,7},{6,4},{7,5},{8,10},{9,11},{10,... | collective-permute-start | bytes 995336 | tf_op jit(solution)/shard_map/ppermute | solution.py:31
  9.6 15.0 %collective-permute-start = (bf16[1296,128]{1,0:T(8,128)(2,1)}, bf16[1296,128]{1,0:T(8,128)(2,1)S(1)}, u32[]{:S(2)}, u32[]{:S(2)}) collective-permute-start(bf16[1296,128]{1,0:T(8,128)(2,1)} %get-tuple-element.49.q0), channel_id=1, source_target_pairs={{0,3},{1,0},{2,1},{3,2},{4,7},{5,4},{6,5},{7,6},{8,11},{9,8},{10,9... | collective-permute-start | bytes 995336 | tf_op jit(solution)/shard_map/ppermute | solution.py:31
  11.5 4.8 %collective-permute-start.5 = (bf16[64,640]{1,0:T(8,128)(2,1)S(1)}, bf16[64,640]{1,0:T(8,128)(2,1)S(1)}, u32[]{:S(2)}, u32[]{:S(2)}) collective-permute-start(bf16[64,640]{1,0:T(8,128)(2,1)S(1)} %collective-permute-done.2.refs_0_), channel_id=1, source_target_pairs={{0,4},{1,5},{2,6},{3,7},{4,8},{5,9},{6,10},{7,11},{8,12},{9,13},{1... | collective-permute-start | bytes 245768 | tf_op jit(solution)/shard_map/ppermute | solution.py:35
  13.3 5.0 %collective-permute-start.6 = (bf16[64,640]{1,0:T(8,128)(2,1)S(1)}, bf16[64,640]{1,0:T(8,128)(2,1)S(1)}, u32[]{:S(2)}, u32[]{:S(2)}) collective-permute-start(bf16[64,640]{1,0:T(8,128)(2,1)S(1)} %collective-permute-done.3.refs_1_), channel_id=1, source_target_pairs={{0,4},{1,5},{2,6},{3,7},{4,8},{5,9},{6,10},{7,11},{8,12},{9,13},{1... | collective-permute-start | bytes 245768 | tf_op jit(solution)/shard_map/ppermute | solution.py:35
  15.0 9.5 %collective-permute-start.4 = (bf16[1296,128]{1,0:T(8,128)(2,1)}, bf16[1296,128]{1,0:T(8,128)(2,1)S(1)}, u32[]{:S(2)}, u32[]{:S(2)}) collective-permute-start(bf16[1296,128]{1,0:T(8,128)(2,1)} %get-tuple-element.49.q0), channel_id=1, source_target_pairs={{0,1},{1,2},{2,3},{3,0},{4,5},{5,6},{6,7},{7,4},{8,9},{9,10},{10,1... | collective-permute-start | bytes 995336 | tf_op jit(solution)/shard_map/ppermute | solution.py:31
  16.3 4.5 %collective-permute-start.7 = (bf16[64,640]{1,0:T(8,128)(2,1)S(1)}, bf16[64,640]{1,0:T(8,128)(2,1)S(1)}, u32[]{:S(2)}, u32[]{:S(2)}) collective-permute-start(bf16[64,640]{1,0:T(8,128)(2,1)S(1)} %collective-permute-done.5.refs_2_), channel_id=1, source_target_pairs={{0,4},{1,5},{2,6},{3,7},{4,8},{5,9},{6,10},{7,11},{8,12},{9,13},{1... | collective-permute-start | bytes 245768 | tf_op jit(solution)/shard_map/ppermute | solution.py:35
  18.3 4.8 %collective-permute-start.8 = (bf16[64,640]{1,0:T(8,128)(2,1)S(1)}, bf16[64,640]{1,0:T(8,128)(2,1)S(1)}, u32[]{:S(2)}, u32[]{:S(2)}) collective-permute-start(bf16[64,640]{1,0:T(8,128)(2,1)S(1)} %collective-permute-done.6.refs_3_), channel_id=1, source_target_pairs={{0,4},{1,5},{2,6},{3,7},{4,8},{5,9},{6,10},{7,11},{8,12},{9,13},{1... | collective-permute-start | bytes 245768 | tf_op jit(solution)/shard_map/ppermute | solution.py:35
  19.0 5.6 %copy-start = (bf16[1296,128]{1,0:T(8,128)(2,1)S(1)}, bf16[1296,128]{1,0:T(8,128)(2,1)}, u32[]{:S(2)}) copy-start(bf16[1296,128]{1,0:T(8,128)(2,1)} %get-tuple-element.49.q0) | copy-start | bytes 995332
  27.4 4.8 %collective-permute-start.11 = (f32[16,512]{1,0:T(8,128)S(1)}, f32[16,512]{1,0:T(8,128)S(1)}, u32[]{:S(2)}, u32[]{:S(2)}) collective-permute-start(f32[16,512]{1,0:T(8,128)S(1)} %get-tuple-element.62.t0), channel_id=1, source_target_pairs={{0,1},{1,2},{2,3},{3,0},{4,5},{5,6},{6,7},{7,4},{8,9},{9,10},{10,1... | collective-permute-start | bytes 98312 | tf_op jit(solution)/shard_map/ppermute | solution.py:31
  29.5 4.3 %collective-permute-start.10 = (f32[16,512]{1,0:T(8,128)S(1)}, f32[16,512]{1,0:T(8,128)S(1)}, u32[]{:S(2)}, u32[]{:S(2)}) collective-permute-start(f32[16,512]{1,0:T(8,128)S(1)} %get-tuple-element.62.t0), channel_id=1, source_target_pairs={{0,2},{1,3},{2,0},{3,1},{4,6},{5,7},{6,4},{7,5},{8,10},{9,11},{10,... | collective-permute-start | bytes 98312 | tf_op jit(solution)/shard_map/ppermute | solution.py:31
  32.0 3.3 %collective-permute-start.9 = (f32[16,512]{1,0:T(8,128)S(1)}, f32[16,512]{1,0:T(8,128)S(1)}, u32[]{:S(2)}, u32[]{:S(2)}) collective-permute-start(f32[16,512]{1,0:T(8,128)S(1)} %get-tuple-element.62.t0), channel_id=1, source_target_pairs={{0,3},{1,0},{2,1},{3,2},{4,7},{5,4},{6,5},{7,6},{8,11},{9,8},{10,9... | collective-permute-start | bytes 98312 | tf_op jit(solution)/shard_map/ppermute | solution.py:31
  38.3 5.7 %collective-permute-start.15 = (bf16[3,128,512]{2,1,0:T(8,128)(2,1)S(1)}, bf16[3,128,512]{2,1,0:T(8,128)(2,1)S(1)}, u32[]{:S(2)}, u32[]{:S(2)}) collective-permute-start(bf16[3,128,512]{2,1,0:T(8,128)(2,1)S(1)} %get-tuple-element.75), channel_id=1, source_target_pairs={{0,32},{32,0},{64,96},{96,64},{128,160},{160,128},{192,224},{224,1... | collective-permute-start | bytes 1179656 | tf_op jit(solution)/shard_map/ppermute | solution.py:44
  40.7 2.0 %collective-permute-start.17 = (bf16[128,512]{1,0:T(8,128)(2,1)S(1)}, bf16[128,512]{1,0:T(8,128)(2,1)S(1)}, u32[]{:S(2)}, u32[]{:S(2)}) collective-permute-start(bf16[128,512]{1,0:T(8,128)(2,1)S(1)} %get-tuple-element.77), channel_id=1, source_target_pairs={{0,32},{32,0},{64,96},{96,64},{128,160},{160,128},{192,224},{224,1... | collective-permute-start | bytes 393224 | tf_op jit(solution)/shard_map/ppermute | solution.py:44
  40.8 7.9 %collective-permute-start.20 = (bf16[128,640]{1,0:T(8,128)(2,1)S(1)}, bf16[128,640]{1,0:T(8,128)(2,1)S(1)}, u32[]{:S(2)}, u32[]{:S(2)}) collective-permute-start(bf16[128,640]{1,0:T(8,128)(2,1)S(1)} %get-tuple-element.79), channel_id=1, source_target_pairs={{0,28},{1,29},{2,30},{3,31},{4,0},{5,1},{6,2},{7,3},{8,4},{9,5},{1... | collective-permute-start | bytes 491528 | tf_op jit(solution)/shard_map/ppermute | solution.py:35
  42.7 8.6 %collective-permute-start.18 = (bf16[128,512]{1,0:T(8,128)(2,1)S(1)}, bf16[128,512]{1,0:T(8,128)(2,1)S(1)}, u32[]{:S(2)}, u32[]{:S(2)}) collective-permute-start(bf16[128,512]{1,0:T(8,128)(2,1)S(1)} %shard_map.120), channel_id=1, source_target_pairs={{0,2},{1,3},{2,0},{3,1},{4,6},{5,7},{6,4},{7,5},{8,10},{9,11},{10,... | collective-permute-start | bytes 393224 | tf_op jit(solution)/shard_map/ppermute | solution.py:31
  44.1 8.0 %collective-permute-start.16 = (bf16[128,512]{1,0:T(8,128)(2,1)S(1)}, bf16[128,512]{1,0:T(8,128)(2,1)S(1)}, u32[]{:S(2)}, u32[]{:S(2)}) collective-permute-start(bf16[128,512]{1,0:T(8,128)(2,1)S(1)} %get-tuple-element.76), channel_id=1, source_target_pairs={{0,1},{1,2},{2,3},{3,0},{4,5},{5,6},{6,7},{7,4},{8,9},{9,10},{10,1... | collective-permute-start | bytes 393224 | tf_op jit(solution)/shard_map/ppermute | solution.py:31
  45.9 6.3 %collective-permute-start.19 = (bf16[128,512]{1,0:T(8,128)(2,1)S(1)}, bf16[128,512]{1,0:T(8,128)(2,1)S(1)}, u32[]{:S(2)}, u32[]{:S(2)}) collective-permute-start(bf16[128,512]{1,0:T(8,128)(2,1)S(1)} %get-tuple-element.78), channel_id=1, source_target_pairs={{0,3},{1,0},{2,1},{3,2},{4,7},{5,4},{6,5},{7,6},{8,11},{9,8},{10,9... | collective-permute-start | bytes 393224 | tf_op jit(solution)/shard_map/ppermute | solution.py:31
  48.7 16.4 %collective-permute-start.21 = (bf16[128,640]{1,0:T(8,128)(2,1)S(1)}, bf16[128,640]{1,0:T(8,128)(2,1)S(1)}, u32[]{:S(2)}, u32[]{:S(2)}) collective-permute-start(bf16[128,640]{1,0:T(8,128)(2,1)S(1)} %shard_map.122), channel_id=1, source_target_pairs={{0,24},{1,25},{2,26},{3,27},{4,28},{5,29},{6,30},{7,31},{8,0},{9,1... | collective-permute-start | bytes 491528 | tf_op jit(solution)/shard_map/ppermute | solution.py:35
  52.9 13.7 %all-to-all-start = ((bf16[8,16,512]{2,1,0:T(8,128)(2,1)}), bf16[8,16,512]{2,1,0:T(8,128)(2,1)S(1)}, u32[]{:S(2)}, u32[]{:S(2)}) async-start(bf16[8,16,512]{2,1,0:T(8,128)(2,1)} %bitcast.10), calls=%async_computation | async-start | bytes 262144 | tf_op jit(solution)/shard_map/all_to_all | solution.py:323
  58.7 19.1 %collective-permute-start.12 = (bf16[128,768]{1,0:T(8,128)(2,1)S(1)}, bf16[128,768]{1,0:T(8,128)(2,1)S(1)}, u32[]{:S(2)}, u32[]{:S(2)}) collective-permute-start(bf16[128,768]{1,0:T(8,128)(2,1)S(1)} %get-tuple-element.69), channel_id=1, source_target_pairs={{0,1},{1,2},{2,3},{3,0},{4,5},{5,6},{6,7},{7,4},{8,9},{9,10},{10,1... | collective-permute-start | bytes 589832 | tf_op jit(solution)/shard_map/ppermute | solution.py:31
  58.7 19.1 %collective-permute-start.13 = (bf16[128,768]{1,0:T(8,128)(2,1)S(1)}, bf16[128,768]{1,0:T(8,128)(2,1)S(1)}, u32[]{:S(2)}, u32[]{:S(2)}) collective-permute-start(bf16[128,768]{1,0:T(8,128)(2,1)S(1)} %get-tuple-element.70), channel_id=1, source_target_pairs={{0,2},{1,3},{2,0},{3,1},{4,6},{5,7},{6,4},{7,5},{8,10},{9,11},{10,... | collective-permute-start | bytes 589832 | tf_op jit(solution)/shard_map/ppermute | solution.py:31
  62.0 15.8 %collective-permute-start.14 = (bf16[128,768]{1,0:T(8,128)(2,1)S(1)}, bf16[128,768]{1,0:T(8,128)(2,1)S(1)}, u32[]{:S(2)}, u32[]{:S(2)}) collective-permute-start(bf16[128,768]{1,0:T(8,128)(2,1)S(1)} %get-tuple-element.71), channel_id=1, source_target_pairs={{0,3},{1,0},{2,1},{3,2},{4,7},{5,4},{6,5},{7,6},{8,11},{9,8},{10,9... | collective-permute-start | bytes 589832 | tf_op jit(solution)/shard_map/ppermute | solution.py:31
  62.4 9.9 %collective-permute-start.23 = (bf16[128,640]{1,0:T(8,128)(2,1)S(1)}, bf16[128,640]{1,0:T(8,128)(2,1)S(1)}, u32[]{:S(2)}, u32[]{:S(2)}) collective-permute-start(bf16[128,640]{1,0:T(8,128)(2,1)S(1)} %get-tuple-element.84), channel_id=1, source_target_pairs={{0,28},{1,29},{2,30},{3,31},{4,0},{5,1},{6,2},{7,3},{8,4},{9,5},{1... | collective-permute-start | bytes 491528 | tf_op jit(solution)/shard_map/ppermute | solution.py:35
  66.6 3.0 %collective-permute-start.22 = (bf16[16,512]{1,0:T(8,128)(2,1)S(1)}, bf16[16,512]{1,0:T(8,128)(2,1)S(1)}, u32[]{:S(2)}, u32[]{:S(2)}) collective-permute-start(bf16[16,512]{1,0:T(8,128)(2,1)S(1)} %shard_map.124.refs_0_), channel_id=1, source_target_pairs={{0,64},{32,96},{64,0},{96,32},{128,192},{160,224},{192,128},{224,1... | collective-permute-start | bytes 49160 | tf_op jit(solution)/shard_map/ppermute | solution.py:40
  69.6 3.9 %collective-permute-start.24 = (bf16[16,512]{1,0:T(8,128)(2,1)S(1)}, bf16[16,512]{1,0:T(8,128)(2,1)S(1)}, u32[]{:S(2)}, u32[]{:S(2)}) collective-permute-start(bf16[16,512]{1,0:T(8,128)(2,1)S(1)} %shard_map.125.refs_0_), channel_id=1, source_target_pairs={{0,192},{32,224},{64,128},{96,160},{128,64},{160,96},{192,0},{224,... | collective-permute-start | bytes 49160 | tf_op jit(solution)/shard_map/ppermute | solution.py:40
  73.5 5.2 %collective-permute-start.25 = (f32[16,512]{1,0:T(8,128)S(1)}, f32[16,512]{1,0:T(8,128)S(1)}, u32[]{:S(2)}, u32[]{:S(2)}) collective-permute-start(f32[16,512]{1,0:T(8,128)S(1)} %shard_map.127), channel_id=1, source_target_pairs={{0,32},{32,0},{64,96},{96,64},{128,160},{160,128},{192,224},{224,1... | collective-permute-start | bytes 98312 | tf_op jit(solution)/shard_map/ppermute | solution.py:44
